TPU v7x, 1024 devices: a whole 8x8x8 slice. The times are simulated.
1024 devices in a mesh: dp: 64 (over x, y), mp: 16 (over z, core).
Axes of the slice: x: 8, y: 8, z: 8, core: 2. Of those that a mesh axis runs over, the one named last changes fastest.
Arguments:
- query_rows: bfloat16 [32768, 4096], P('dp', 'mp'), may hold values from -6 to 6
- key_rows: bfloat16 [32768, 4096], P('dp', 'mp'), may hold values from -6 to 6
- value_rows: bfloat16 [32768, 4096], P('dp', 'mp'), may hold values from -6 to 6
- out_grad: bfloat16 [32768, 6144], P('dp', 'mp'), may hold values from -6 to 6
- out_weight: bfloat16 [4096, 6144], P('mp'), may hold values from -0.078125 to 0.078125
- destinations: int32 [32768], P('dp'), may hold values from 0 to 63, as said below
- image_ids: int32 [32768], P('dp'), may hold values from 0 to 2, as said below
- patch_counts: int32 [192], P('dp'), may hold values from 2 to 256, as said below
Outputs:
- query_grad: bfloat16 [32768, 4096], P('dp', 'mp')
- key_grad: bfloat16 [32768, 4096], P('dp', 'mp')
- value_grad: bfloat16 [32768, 4096], P('dp', 'mp')
Inputs may be any that keep to these rules, and one draw needn't show every extreme that they name: `destinations`: each device holds its tokens as 64 contiguous runs, each run of one image with one destination. Two runs stay on the device; the others go one to each other device but one. Two devices that exchange tokens send each other equally many. The tokens of one device with one other destination are at least 2 and at most 3, and some pair reaches 3; every device is the destination of exactly 512 tokens. `image_ids`: two images of each device lie whole on it; the third is made of the runs that the other devices send to it. patch_counts[d * 3 + k] is the number of tokens with destination d and image id k; each device has one image of exactly 256 patches.
All inputs are finite; a program needn't handle non-finite values.
Results may differ from a plain program's by a relative error of at most 0.015.
Values may be sent and summed in bfloat16 or wider, within the bound.
No kernel may reach another device: no remote copies, remote signals or barrier semaphores. Data moves between devices by JAX's collectives and lax.ppermute only.
A program may use at most 64 MiB of HBM per device.

v0:
```python
import jax
import jax.numpy as jnp
from jax import lax
from jax.sharding import PartitionSpec as P

HD = 128
CAP = 3


def attend(query_part, key_part, value_part, grad_part, id_part, row_weight):
    score_scale = 1.0 / query_part.shape[-1] ** 0.5
    same_image = id_part[:, None] == id_part[None, :]
    inner = (((1,), (1,)), ((), ()))
    outer = (((0,), (0,)), ((), ()))

    def one_head(parts):
        query_one, key_one, value_one, grad_one = parts
        scores = (
            lax.dot_general(query_one, key_one, inner, preferred_element_type=jnp.float32)
            * score_scale
        )
        scores = jnp.where(same_image, scores, -jnp.inf)
        row_max = jnp.max(scores, axis=-1, keepdims=True)
        raised = jnp.exp(scores - row_max)
        probs = raised / jnp.sum(raised, axis=-1, keepdims=True)
        probs_low = probs.astype(jnp.bfloat16)
        attended = jnp.dot(probs_low, value_one, preferred_element_type=jnp.float32)
        row_dot = jnp.sum(grad_one.astype(jnp.float32) * attended, axis=-1)
        scaled_probs = row_weight[:, None] * probs
        weighted = scaled_probs.astype(jnp.bfloat16)
        value_grad = lax.dot_general(
            weighted, grad_one, outer, preferred_element_type=jnp.float32
        ).astype(jnp.bfloat16)
        prob_grad = lax.dot_general(grad_one, value_one, inner, preferred_element_type=jnp.float32)
        score_grad = (scaled_probs * (prob_grad - row_dot[:, None])).astype(jnp.bfloat16)
        query_grad = (
            jnp.dot(score_grad, key_one, preferred_element_type=jnp.float32) * score_scale
        ).astype(jnp.bfloat16)
        key_grad = (
            lax.dot_general(score_grad, query_one, outer, preferred_element_type=jnp.float32)
            * score_scale
        ).astype(jnp.bfloat16)
        return (query_grad, key_grad, value_grad)

    moved = tuple(
        (jnp.moveaxis(source, 1, 0) for source in (query_part, key_part, value_part, grad_part))
    )
    results = lax.map(one_head, moved)
    return tuple((jnp.moveaxis(part, 0, 1) for part in results))


def local(
    query_rows, key_rows, value_rows, out_grad, out_weight, destinations, image_ids, patch_counts
):
    tok_rows = query_rows.shape[0]
    head_cols = query_rows.shape[1]
    head_dim = HD
    heads_dev = head_cols // head_dim
    dp_size = lax.axis_size("dp")
    slot_rows = dp_size * CAP
    total_rows = slot_rows + tok_rows
    img_dev = patch_counts.shape[0]
    my_index = lax.axis_index("dp")
    remote = destinations != my_index
    dest_hot = (destinations[:, None] == jnp.arange(dp_size, dtype=jnp.int32)[None, :]).astype(
        jnp.int32
    )
    rank_in = jnp.sum((jnp.cumsum(dest_hot, 0) - 1) * dest_hot, 1)
    slot_index = jnp.where(remote, destinations * CAP + rank_in, slot_rows)

    def to_slots(source):
        return (
            jnp.zeros((slot_rows,) + source.shape[1:], source.dtype)
            .at[slot_index]
            .set(source, mode="drop")
        )

    ids_sent = jnp.full((slot_rows,), -1, jnp.int32).at[slot_index].set(image_ids, mode="drop")
    received = (
        lax.all_to_all(to_slots(query_rows), "dp", split_axis=0, concat_axis=0, tiled=True),
        lax.all_to_all(to_slots(key_rows), "dp", split_axis=0, concat_axis=0, tiled=True),
        lax.all_to_all(to_slots(value_rows), "dp", split_axis=0, concat_axis=0, tiled=True),
        lax.all_to_all(to_slots(out_grad), "dp", split_axis=0, concat_axis=0, tiled=True),
        lax.all_to_all(ids_sent, "dp", split_axis=0, concat_axis=0, tiled=True),
    )
    query_in, key_in, value_in, fourth_in, ids_in = received
    stacked_fourth = jnp.concatenate([fourth_in, out_grad], 0)
    grad_all = lax.dot_general(
        lax.all_gather(stacked_fourth, "mp", axis=1, tiled=True),
        out_weight,
        (((1,), (1,)), ((), ())),
        preferred_element_type=jnp.float32,
    ).astype(jnp.bfloat16)
    query_all = jnp.concatenate([query_in, query_rows], 0)
    key_all = jnp.concatenate([key_in, key_rows], 0)
    value_all = jnp.concatenate([value_in, value_rows], 0)
    ids_all = jnp.concatenate([ids_in, jnp.where(remote, -1, image_ids)], 0)
    id_weight = tok_rows / (img_dev * patch_counts.astype(jnp.float32))
    id_hot = ids_all[:, None] == jnp.arange(img_dev, dtype=jnp.int32)[None, :]
    slot_weight = jnp.sum(jnp.where(id_hot, id_weight[None, :], 0.0), 1)

    def split_heads(source):
        return source.reshape(source.shape[0], heads_dev, head_dim)

    sort_key = jnp.where(ids_all < 0, img_dev, ids_all)
    ordering = jnp.argsort(sort_key, stable=True)[:tok_rows]
    results = attend(
        split_heads(query_all[ordering]),
        split_heads(key_all[ordering]),
        split_heads(value_all[ordering]),
        split_heads(grad_all[ordering]),
        ids_all[ordering],
        slot_weight[ordering],
    )
    grads = tuple(
        (
            jnp.zeros((total_rows, head_cols), jnp.bfloat16)
            .at[ordering]
            .set(part.reshape(tok_rows, head_cols))
            for part in results
        )
    )
    returned = (
        lax.all_to_all(grads[0][:slot_rows], "dp", split_axis=0, concat_axis=0, tiled=True),
        lax.all_to_all(grads[1][:slot_rows], "dp", split_axis=0, concat_axis=0, tiled=True),
        lax.all_to_all(grads[2][:slot_rows], "dp", split_axis=0, concat_axis=0, tiled=True),
    )
    safe_index = jnp.minimum(slot_index, slot_rows - 1)
    finals = tuple(
        (
            jnp.where(remote[:, None], returned[k][safe_index], grads[k][slot_rows:])
            for k in range(3)
        )
    )
    return (finals[0], finals[1], finals[2])


def solution(mesh):
    return jax.shard_map(
        local,
        mesh=mesh,
        in_specs=(
            P("dp", "mp"),
            P("dp", "mp"),
            P("dp", "mp"),
            P("dp", "mp"),
            P("mp", None),
            P("dp"),
            P("dp"),
            P("dp"),
        ),
        out_specs=(P("dp", "mp"), P("dp", "mp"), P("dp", "mp")),
        check_vma=False,
    )
```

profile of v0, /device:TPU:2, one launch (start us, length us, event | category | flops | bytes accessed | tf_op | source)
XLA Modules:
  0.0 241.1 jit_solution(17684935010471356944)
XLA Ops:
  7.2 0.8 fusion.56
  8.1 1.2 reduce-window.6
  9.6 0.8 fusion.55
  11.8 2.8 %scatter_custom_fusion.3 = bf16[192,384]{1,0:T(8,128)(2,1)S(1)} fusion(s32[512]{0:T(512)S(1)} %get-tuple-element.114, bf16[512,384]{1,0:T(8,128)(2,1)} %param.13, bf16[]{:T(256)} %constant.26.clone.1), kind=kCustom, calls=%fused_computation.95 | custom fusion | bytes 147968 | tf_op jit(solution)/shard_map/scatter | solution.py:75
  14.6 28.7 %all_to_all.96 = bf16[64,3,384]{2,1,0:T(4,128)(2,1)S(1)} all-to-all(bf16[64,3,384]{2,1,0:T(4,128)(2,1)S(1)} %all_to_all.73), channel_id=1, replica_groups=mesh['dp'=64,'mp'=16] {'dp'}, dimensions={0} | all-to-all | bytes 294912 | tf_op jit(solution)/shard_map/all_to_all | solution.py:83
  43.4 1.9 pad_maximum_fusion
  45.4 2.6 %scatter_custom_fusion = s32[192]{0:T(256)S(1)} fusion(s32[512]{0:T(512)S(1)} %get-tuple-element.114, s32[512]{0:T(512)} %param.16, s32[]{:T(128)} %constant.27.clone.1), kind=kCustom, calls=%fused_computation.116 | custom fusion | bytes 1280 | tf_op jit(solution)/shard_map/scatter | solution.py:78
  48.0 0.7 all_to_all.64
  48.7 5.4 %all-to-all-start = ((s32[64,3,1]{1,2,0:T(1,128)}), s32[64,3,1]{1,2,0:T(1,128)S(1)}, u32[]{:S(2)}, u32[]{:S(2)}) async-start(s32[64,3,1]{1,2,0:T(1,128)} %bitcast.2), calls=%async_computation | async-start | bytes 65536 | tf_op jit(solution)/shard_map/all_to_all | solution.py:84
  54.8 2.7 %scatter_custom_fusion.2 = bf16[192,256]{1,0:T(8,128)(2,1)S(1)} fusion(s32[512]{0:T(512)S(1)} %get-tuple-element.114, bf16[512,256]{1,0:T(8,128)(2,1)} %param.11, bf16[]{:T(256)} %constant.26.clone.1), kind=kCustom, calls=%fused_computation.99 | custom fusion | bytes 98816 | tf_op jit(solution)/shard_map/scatter | solution.py:75
  58.2 2.7 %scatter_custom_fusion.4 = bf16[192,256]{1,0:T(8,128)(2,1)S(1)} fusion(s32[512]{0:T(512)S(1)} %get-tuple-element.114, bf16[512,256]{1,0:T(8,128)(2,1)} %param.12, bf16[]{:T(256)} %constant.26.clone.1), kind=kCustom, calls=%fused_computation.97 | custom fusion | bytes 98816 | tf_op jit(solution)/shard_map/scatter | solution.py:75
  61.6 2.7 %scatter_custom_fusion.1 = bf16[192,256]{1,0:T(8,128)(2,1)S(1)} fusion(s32[512]{0:T(512)S(1)} %get-tuple-element.114, bf16[512,256]{1,0:T(8,128)(2,1)} %param.10, bf16[]{:T(256)} %constant.26.clone.1), kind=kCustom, calls=%fused_computation.101 | custom fusion | bytes 98816 | tf_op jit(solution)/shard_map/scatter | solution.py:75
  65.2 12.7 %all-to-all-start.2 = ((bf16[64,3,256]{2,1,0:T(4,128)(2,1)}), bf16[64,3,256]{2,1,0:T(4,128)(2,1)S(1)}, u32[]{:S(2)}, u32[]{:S(2)}) async-start(bf16[64,3,256]{2,1,0:T(4,128)(2,1)} %all_to_all.70), calls=%async_computation.2 | async-start | bytes 262144 | tf_op jit(solution)/shard_map/all_to_all | solution.py:81
  79.3 4.4 %sort.17 = (s32[704]{0:T(1024)}, s32[704]{0:T(1024)S(1)}) sort(s32[704]{0:T(1024)S(1)} %get-tuple-element.110, s32[704]{0:T(1024)S(1)} %iota.16), dimensions={0}, to_apply=%region_4.5 | sort | flops 7040 | bytes 11264 | tf_op jit(solution)/shard_map/jit(argsort)/sort | solution.py:106
  83.7 5.9 %all-to-all-done.2 = bf16[64,3,256]{2,1,0:T(4,128)(2,1)S(1)} async-done(((bf16[64,3,256]{2,1,0:T(4,128)(2,1)}), bf16[64,3,256]{2,1,0:T(4,128)(2,1)S(1)}, u32[]{:S(2)}, u32[]{:S(2)}) %all-to-all-start.2) | async-done | bytes 98336 | tf_op jit(solution)/shard_map/all_to_all | solution.py:81
  89.6 6.8 %all-to-all-start.4 = ((bf16[64,3,256]{2,1,0:T(4,128)(2,1)}), bf16[64,3,256]{2,1,0:T(4,128)(2,1)S(1)}, u32[]{:S(2)}, u32[]{:S(2)}) async-start(bf16[64,3,256]{2,1,0:T(4,128)(2,1)} %all_to_all.76), calls=%async_computation.4 | async-start | bytes 262144 | tf_op jit(solution)/shard_map/all_to_all | solution.py:82
  96.5 2.3 gather_fusion.3
  98.8 2.3 gather_fusion
  101.9 6.3 %all-to-all-done.4 = bf16[64,3,256]{2,1,0:T(4,128)(2,1)S(1)} async-done(((bf16[64,3,256]{2,1,0:T(4,128)(2,1)}), bf16[64,3,256]{2,1,0:T(4,128)(2,1)S(1)}, u32[]{:S(2)}, u32[]{:S(2)}) %all-to-all-start.4) | async-done | bytes 98336 | tf_op jit(solution)/shard_map/all_to_all | solution.py:82
  108.8 6.6 %all-to-all-start.1 = ((bf16[64,3,256]{2,1,0:T(4,128)(2,1)}), bf16[64,3,256]{2,1,0:T(4,128)(2,1)}, u32[]{:S(2)}, u32[]{:S(2)}) async-start(bf16[64,3,256]{2,1,0:T(4,128)(2,1)} %all_to_all.67), calls=%async_computation.1 | async-start | bytes 262144 | tf_op jit(solution)/shard_map/all_to_all | solution.py:80
  115.4 1.0 pad_maximum_fusion.2
  116.4 2.6 %gather_fusion.2 = bf16[512,256]{1,0:T(8,128)(2,1)} fusion(bf16[704,256]{1,0:T(8,128)(2,1)S(1)} %pad_maximum_fusion.2, s32[1024]{0:T(1024)S(1)} %pad_clamp_fusion.1), kind=kCustom, calls=%fused_computation.2 | custom fusion | bytes 526336 | tf_op jit(solution)/shard_map/gather | solution.py:109
  119.0 1.6 all_to_all.78
  120.6 1.0 pad_maximum_fusion.3
  121.6 2.6 %gather_fusion.5 = bf16[512,256]{1,0:T(8,128)(2,1)} fusion(bf16[704,256]{1,0:T(8,128)(2,1)S(1)} %pad_maximum_fusion.3, s32[1024]{0:T(1024)S(1)} %pad_clamp_fusion.1), kind=kCustom, calls=%fused_computation.5 | custom fusion | bytes 526336 | tf_op jit(solution)/shard_map/gather | solution.py:110
  124.2 2.9 %all-to-all-done.1 = bf16[64,3,256]{2,1,0:T(4,128)(2,1)} async-done(((bf16[64,3,256]{2,1,0:T(4,128)(2,1)}), bf16[64,3,256]{2,1,0:T(4,128)(2,1)}, u32[]{:S(2)}, u32[]{:S(2)}) %all-to-all-start.1) | async-done | bytes 98336 | tf_op jit(solution)/shard_map/all_to_all | solution.py:80
  127.1 1.6 all_to_all.69
  128.7 1.0 pad_maximum_fusion.1
  129.7 2.6 %gather_fusion.1 = bf16[512,256]{1,0:T(8,128)(2,1)} fusion(bf16[704,256]{1,0:T(8,128)(2,1)S(1)} %pad_maximum_fusion.1, s32[1024]{0:T(1024)S(1)} %pad_clamp_fusion.1), kind=kCustom, calls=%fused_computation.1 | custom fusion | bytes 526336 | tf_op jit(solution)/shard_map/gather | solution.py:108
  132.3 1.7 bitcast_bitcast_fusion.2
  134.0 1.9 bitcast_bitcast_fusion
  135.9 5.9 %convolution_convert_fusion.1 = bf16[704,256]{1,0:T(8,128)(2,1)S(1)} fusion(bf16[704,6144]{1,0:T(8,128)(2,1)} %all-gather.2.cloned.1.call-done, bf16[256,6144]{1,0:T(8,128)(2,1)S(1)} %copy-done), kind=kOutput, calls=%fused_computation.64 | convolution fusion | flops 2214772736 | bytes 12156928 | tf_op jit(solution)/shard_map/dot_general | solution.py:88
  141.8 2.6 %gather_fusion.4 = bf16[512,256]{1,0:T(8,128)(2,1)} fusion(bf16[704,256]{1,0:T(8,128)(2,1)S(1)} %convolution_convert_fusion.1, s32[1024]{0:T(1024)S(1)} %pad_clamp_fusion.1), kind=kCustom, calls=%fused_computation.4 | custom fusion | bytes 526336 | tf_op jit(solution)/shard_map/gather | solution.py:111
  144.4 1.8 copy.49
  146.2 16.5 %while.15 = (s32[]{:T(128)}, bf16[2,512,128]{2,1,0:T(8,128)(2,1)}, bf16[2,512,128]{2,1,0:T(8,128)(2,1)}, bf16[2,512,128]{2,1,0:T(8,128)(2,1)}, f32[512]{0:T(512)...) while((s32[]{:T(128)}, bf16[2,512,128]{2,1,0:T(8,128)(2,1)}, ...), condition=%wide.region_14.15_spmd.clone, body=%wide.region_10.14_spmd.clone.sunk | while | flops 408156672 | bytes 15765809 | solution.py:48
  146.2 1.3 fusion.100
  147.7 1.9 fusion.106
  149.6 1.3 fusion.102
  150.9 1.3 fusion.103
  154.4 1.3 fusion.100
  155.9 1.9 fusion.106
  157.8 1.3 fusion.102
  159.1 1.3 fusion.103
  162.7 2.8 %scatter_custom_fusion.5 = bf16[704,256]{1,0:T(8,128)(2,1)S(1)} fusion(s32[512]{0:T(512)S(1)} %compare_select_fusion.2, bf16[2,64,8,128]{3,2,1,0:T(8,128)(2,1)} %bitcast.126, bf16[]{:T(256)} %constant.26.clone.1), kind=kCustom, calls=%fused_computation.75 | custom fusion | bytes 622594 | tf_op jit(solution)/shard_map/scatter | solution.py:119
  166.2 1.6 all_to_all.79
  167.8 10.0 %all-to-all-start.5 = ((bf16[64,3,256]{2,1,0:T(4,128)(2,1)}), bf16[64,3,256]{2,1,0:T(4,128)(2,1)}, u32[]{:S(2)}, u32[]{:S(2)}) async-start(bf16[64,3,256]{2,1,0:T(4,128)(2,1)} %all_to_all.79), calls=%async_computation.5 | async-start | bytes 262144 | tf_op jit(solution)/shard_map/all_to_all | solution.py:124
  177.8 3.4 %scatter_custom_fusion.6 = bf16[704,256]{1,0:T(8,128)(2,1)} fusion(s32[512]{0:T(512)S(1)} %compare_select_fusion.2, bf16[2,64,8,128]{3,2,1,0:T(8,128)(2,1)} %bitcast.127, bf16[]{:T(256)} %constant.26.clone.1), kind=kCustom, calls=%fused_computation.72 | custom fusion | bytes 622594 | tf_op jit(solution)/shard_map/scatter | solution.py:119
  181.3 1.5 slice.57
  182.8 1.6 all_to_all.82
  184.4 5.1 %all-to-all-done.5 = bf16[64,3,256]{2,1,0:T(4,128)(2,1)} async-done(((bf16[64,3,256]{2,1,0:T(4,128)(2,1)}), bf16[64,3,256]{2,1,0:T(4,128)(2,1)}, u32[]{:S(2)}, u32[]{:S(2)}) %all-to-all-start.5) | async-done | bytes 98336 | tf_op jit(solution)/shard_map/all_to_all | solution.py:124
  189.5 7.8 %all-to-all-start.6 = ((bf16[64,3,256]{2,1,0:T(4,128)(2,1)}), bf16[64,3,256]{2,1,0:T(4,128)(2,1)}, u32[]{:S(2)}, u32[]{:S(2)}) async-start(bf16[64,3,256]{2,1,0:T(4,128)(2,1)} %all_to_all.82), calls=%async_computation.6 | async-start | bytes 262144 | tf_op jit(solution)/shard_map/all_to_all | solution.py:125
  197.3 3.4 %scatter_custom_fusion.7 = bf16[704,256]{1,0:T(8,128)(2,1)} fusion(s32[512]{0:T(512)S(1)} %compare_select_fusion.2, bf16[2,64,8,128]{3,2,1,0:T(8,128)(2,1)} %bitcast.128, bf16[]{:T(256)} %constant.26.clone.1), kind=kCustom, calls=%fused_computation.69 | custom fusion | bytes 622594 | tf_op jit(solution)/shard_map/scatter | solution.py:119
  200.7 1.5 slice.59
  202.3 1.6 all_to_all.85
  203.9 5.1 %all-to-all-done.6 = bf16[64,3,256]{2,1,0:T(4,128)(2,1)} async-done(((bf16[64,3,256]{2,1,0:T(4,128)(2,1)}), bf16[64,3,256]{2,1,0:T(4,128)(2,1)}, u32[]{:S(2)}, u32[]{:S(2)}) %all-to-all-start.6) | async-done | bytes 98336 | tf_op jit(solution)/shard_map/all_to_all | solution.py:125
  208.9 7.8 %all-to-all-start.7 = ((bf16[64,3,256]{2,1,0:T(4,128)(2,1)}), bf16[64,3,256]{2,1,0:T(4,128)(2,1)}, u32[]{:S(2)}, u32[]{:S(2)}) async-start(bf16[64,3,256]{2,1,0:T(4,128)(2,1)} %all_to_all.85), calls=%async_computation.7 | async-start | bytes 262144 | tf_op jit(solution)/shard_map/all_to_all | solution.py:126
  216.8 1.0 all_to_all.81
  217.8 2.0 gather_fusion.6
  219.7 1.0 all_to_all.84
  220.7 2.6 %gather_fusion.7 = bf16[512,256]{1,0:T(8,128)(2,1)} fusion(bf16[192,256]{1,0:T(8,128)(2,1)S(1)} %all_to_all.84, s32[1024]{0:T(1024)S(1)} %pad_clamp_fusion), kind=kCustom, calls=%fused_computation.7 | custom fusion | bytes 526336 | tf_op jit(solution)/shard_map/gather | solution.py:131
  223.3 5.1 %all-to-all-done.7 = bf16[64,3,256]{2,1,0:T(4,128)(2,1)} async-done(((bf16[64,3,256]{2,1,0:T(4,128)(2,1)}), bf16[64,3,256]{2,1,0:T(4,128)(2,1)}, u32[]{:S(2)}, u32[]{:S(2)}) %all-to-all-start.7) | async-done | bytes 98336 | tf_op jit(solution)/shard_map/all_to_all | solution.py:126
  228.4 1.0 all_to_all.87
  229.4 2.6 %gather_fusion.8 = bf16[512,256]{1,0:T(8,128)(2,1)} fusion(bf16[192,256]{1,0:T(8,128)(2,1)S(1)} %all_to_all.87, s32[1024]{0:T(1024)S(1)} %pad_clamp_fusion), kind=kCustom, calls=%fused_computation.8 | custom fusion | bytes 526336 | tf_op jit(solution)/shard_map/gather | solution.py:131
  232.0 2.3 slice_select_fusion
  (69 shorter events, 13.2 us)
Async XLA Ops:
  7.2 128.8 %copy-start = (bf16[256,6144]{1,0:T(8,128)(2,1)S(1)}, bf16[256,6144]{1,0:T(8,128)(2,1)}, u32[]{:S(2)}) copy-start(bf16[256,6144]{1,0:T(8,128)(2,1)} %param.14) | copy-start | bytes 9437188
  7.2 128.8 %all-gather.2.cloned.1.call-start = ((), (), s32[]{:S(2)}) async-start(), calls=%async_computation.8 | async-start | bytes 9191424 | tf_op jit(solution)/shard_map/all_gather | solution.py:89
  48.7 16.5 %all-to-all-start = ((s32[64,3,1]{1,2,0:T(1,128)}), s32[64,3,1]{1,2,0:T(1,128)S(1)}, u32[]{:S(2)}, u32[]{:S(2)}) async-start(s32[64,3,1]{1,2,0:T(1,128)} %bitcast.2), calls=%async_computation | async-start | bytes 65536 | tf_op jit(solution)/shard_map/all_to_all | solution.py:84
  65.2 24.4 %all-to-all-start.2 = ((bf16[64,3,256]{2,1,0:T(4,128)(2,1)}), bf16[64,3,256]{2,1,0:T(4,128)(2,1)S(1)}, u32[]{:S(2)}, u32[]{:S(2)}) async-start(bf16[64,3,256]{2,1,0:T(4,128)(2,1)} %all_to_all.70), calls=%async_computation.2 | async-start | bytes 262144 | tf_op jit(solution)/shard_map/all_to_all | solution.py:81
  89.6 18.6 %all-to-all-start.4 = ((bf16[64,3,256]{2,1,0:T(4,128)(2,1)}), bf16[64,3,256]{2,1,0:T(4,128)(2,1)S(1)}, u32[]{:S(2)}, u32[]{:S(2)}) async-start(bf16[64,3,256]{2,1,0:T(4,128)(2,1)} %all_to_all.76), calls=%async_computation.4 | async-start | bytes 262144 | tf_op jit(solution)/shard_map/all_to_all | solution.py:82
  108.2 0.7 copy-start.4
  108.8 18.2 %all-to-all-start.1 = ((bf16[64,3,256]{2,1,0:T(4,128)(2,1)}), bf16[64,3,256]{2,1,0:T(4,128)(2,1)}, u32[]{:S(2)}, u32[]{:S(2)}) async-start(bf16[64,3,256]{2,1,0:T(4,128)(2,1)} %all_to_all.67), calls=%async_computation.1 | async-start | bytes 262144 | tf_op jit(solution)/shard_map/all_to_all | solution.py:80
  147.5 2.1 copy-start.9
  150.9 1.4 copy-start.1
  150.9 1.4 copy-start.7
  150.9 2.4 %copy-start.2 = (bf16[2,512,128]{2,1,0:T(8,128)(2,1)S(1)}, bf16[2,512,128]{2,1,0:T(8,128)(2,1)}, u32[]{:S(2)}) copy-start(bf16[2,512,128]{2,1,0:T(8,128)(2,1)} %get-tuple-element.211) | copy-start | bytes 786436 | tf_op jit(solution)/shard_map/while
  150.9 2.4 %copy-start.5 = (bf16[2,512,128]{2,1,0:T(8,128)(2,1)S(1)}, bf16[2,512,128]{2,1,0:T(8,128)(2,1)}, u32[]{:S(2)}) copy-start(bf16[2,512,128]{2,1,0:T(8,128)(2,1)} %get-tuple-element.195) | copy-start | bytes 786436 | tf_op jit(solution)/shard_map/while
  152.6 0.7 copy-start.8
  153.7 0.7 copy-start.6
  155.7 2.1 copy-start.9
  159.1 1.4 copy-start.1
  159.1 1.4 copy-start.7
  159.1 2.4 %copy-start.2 = (bf16[2,512,128]{2,1,0:T(8,128)(2,1)S(1)}, bf16[2,512,128]{2,1,0:T(8,128)(2,1)}, u32[]{:S(2)}) copy-start(bf16[2,512,128]{2,1,0:T(8,128)(2,1)} %get-tuple-element.211) | copy-start | bytes 786436 | tf_op jit(solution)/shard_map/while
  159.1 2.4 %copy-start.5 = (bf16[2,512,128]{2,1,0:T(8,128)(2,1)S(1)}, bf16[2,512,128]{2,1,0:T(8,128)(2,1)}, u32[]{:S(2)}) copy-start(bf16[2,512,128]{2,1,0:T(8,128)(2,1)} %get-tuple-element.195) | copy-start | bytes 786436 | tf_op jit(solution)/shard_map/while
  160.9 0.7 copy-start.8
  162.0 0.7 copy-start.6
  165.5 51.3 %copy-start.3 = (bf16[704,256]{1,0:T(8,128)(2,1)}, bf16[704,256]{1,0:T(8,128)(2,1)S(1)}, u32[]{:S(2)}) copy-start(bf16[704,256]{1,0:T(8,128)(2,1)S(1)} %scatter_custom_fusion.5) | copy-start | bytes 1081348
  167.8 21.7 %all-to-all-start.5 = ((bf16[64,3,256]{2,1,0:T(4,128)(2,1)}), bf16[64,3,256]{2,1,0:T(4,128)(2,1)}, u32[]{:S(2)}, u32[]{:S(2)}) async-start(bf16[64,3,256]{2,1,0:T(4,128)(2,1)} %all_to_all.79), calls=%async_computation.5 | async-start | bytes 262144 | tf_op jit(solution)/shard_map/all_to_all | solution.py:124
  189.5 19.5 %all-to-all-start.6 = ((bf16[64,3,256]{2,1,0:T(4,128)(2,1)}), bf16[64,3,256]{2,1,0:T(4,128)(2,1)}, u32[]{:S(2)}, u32[]{:S(2)}) async-start(bf16[64,3,256]{2,1,0:T(4,128)(2,1)} %all_to_all.82), calls=%async_computation.6 | async-start | bytes 262144 | tf_op jit(solution)/shard_map/all_to_all | solution.py:125
  208.9 19.5 %all-to-all-start.7 = ((bf16[64,3,256]{2,1,0:T(4,128)(2,1)}), bf16[64,3,256]{2,1,0:T(4,128)(2,1)}, u32[]{:S(2)}, u32[]{:S(2)}) async-start(bf16[64,3,256]{2,1,0:T(4,128)(2,1)} %all_to_all.85), calls=%async_computation.7 | async-start | bytes 262144 | tf_op jit(solution)/shard_map/all_to_all | solution.py:126
Sparse Core Ops, SparseCore 0:
  45.5 64.3 all-gather.1
where the time goes:
time: 243 us; the launch traced here: 241 us
  local copies, waits for them, and re-layouts  73.6 us (30%)
  starting transfers between devices  57.1 us (23%)
  waiting for transfers between devices  30.5 us (13%)
  blocking collectives  28.7 us (12%)
  matrix products  18.9 us (8%)
  other arithmetic  17.8 us (7%)
  between operations  14.3 us (6%)
    all_to_all x1, blocking collectives, local(): lax.all_to_all(to_slots(out_grad), 'dp', split_axis=0, concat_axis=0, til...  28.7 us
    all_to_all x1, starting transfers between devices, local(): lax.all_to_all(to_slots(key_rows), 'dp', split_axis=0, concat_axis=0, til...  12.7 us
    scatter x4, local copies, waits for them, and re-layouts, to_slots(): return jnp.zeros((slot_rows,) + source.shape[1:], source.dtype).at[slot_i...  10.9 us
    all_to_all x1, starting transfers between devices, local(): lax.all_to_all(grads[0][:slot_rows], 'dp', split_axis=0, concat_axis=0, t...  10 us
    scatter x3, local copies, waits for them, and re-layouts, local(): grads = tuple((jnp.zeros((total_rows, head_cols), jnp.bfloat16).at[orderi...  9.69 us
    all_to_all x1, starting transfers between devices, local(): lax.all_to_all(grads[2][:slot_rows], 'dp', split_axis=0, concat_axis=0, t...  7.81 us
    all_to_all x1, starting transfers between devices, local(): lax.all_to_all(grads[1][:slot_rows], 'dp', split_axis=0, concat_axis=0, t...  7.8 us
    gather x3, local copies, waits for them, and re-layouts, local(): returned[k][safe_index]  7.11 us
  transfers between devices with their start and end apart: 8, of which 7 were waited for; matrix products, arithmetic and copies ran while one was open for 21% of the time, Pallas kernels for 0%

commit v1 on v0

v1 whole, which is shorter than its diff:
```python
import functools
import math

import jax
import jax.numpy as jnp
from jax import lax
from jax.experimental import pallas as pl
from jax.experimental.pallas import tpu as pltpu
from jax.sharding import PartitionSpec as P

HD = 128
CAP = 3
BIG = 256
SMALL = 144
KEPT = BIG + SMALL
OCT = 8
LOG2E = 1.4426950408889634
F32 = jnp.float32
BF16 = jnp.bfloat16
MIB = 1024 * 1024
NT = (((1,), (1,)), ((), ()))
TN = (((0,), (0,)), ((), ()))


def iota(shape, dim):
    return lax.broadcasted_iota(jnp.int32, shape, dim)


def one_hot(cond):
    return jnp.where(cond, 1.0, 0.0).astype(BF16)


def pick(hot, rows):
    return jnp.dot(hot, rows, preferred_element_type=F32).astype(BF16)


def slot_row(slot, n_dp):
    return OCT * (slot % n_dp) + 2 * (slot // n_dp)


def plan_kernel(n_dp, dest_ref, ids_ref, counts_ref, og_ref, pos_ref, og_moved_ref):
    tok = dest_ref.shape[1]
    slots = n_dp * CAP
    mine = lax.axis_index("dp")
    dest = dest_ref[...]
    counts = counts_ref[...]
    big_id = jnp.where(
        counts[:, 0:1] == BIG, 0, jnp.where(counts[:, 1:2] == BIG, 1, 2)
    )
    kept_class = jnp.where(ids_ref[...] == big_id, n_dp, n_dp + 1)
    group = jnp.where(dest == mine, kept_class, dest)
    n_rows = n_dp + 16
    row = iota((n_rows, tok), 0)
    member = row == group
    before = one_hot(iota((tok, tok), 0) < iota((tok, tok), 1))
    rank = jnp.dot(one_hot(member), before, preferred_element_type=F32)
    start = jnp.where(row < n_dp, row, jnp.where(row == n_dp, slots, slots + BIG))
    step = jnp.where(row < n_dp, float(n_dp), 1.0)
    place = jnp.where(member, start.astype(F32) + step * rank, 0.0)
    pos = jnp.sum(place, axis=0, keepdims=True).astype(jnp.int32)
    pos_ref[...] = jnp.broadcast_to(pos, pos_ref.shape)
    og_moved_ref[...] = pick(one_hot(iota((slots, tok), 0) == pos), og_ref[...])


def pack_kernel(
    n_dp, pos_ref, og_ref, q_ref, k_ref, v_ref,
    send_ref, og_kept_ref, rows_kept_ref, used_ref, kept_used_ref, pos_col_ref,
):
    tok = og_ref.shape[0]
    slots = n_dp * CAP
    pos = pos_ref[0:1, :]
    q, k, v = q_ref[...], k_ref[...], v_ref[...]
    first = jnp.where(pos < slots, slot_row(pos, n_dp), -OCT)
    row = iota((n_dp * OCT, tok), 0)
    left = jnp.concatenate([q, k[:, :HD]], 1)
    right = jnp.concatenate([k[:, HD:], v], 1)
    send_ref[...] = (
        jnp.dot(one_hot(row == first), left, preferred_element_type=F32)
        + jnp.dot(one_hot(row == first + 1), right, preferred_element_type=F32)
    ).astype(BF16)
    kept_hot = one_hot(iota((KEPT, tok), 0) + slots == pos)
    og_kept_ref[...] = pick(kept_hot, og_ref[...])
    rows_kept_ref[...] = pick(kept_hot, jnp.concatenate([q, k, v], 1))
    ones = jnp.ones((tok, HD), BF16)
    slot_hot = one_hot(iota((slots, tok), 0) == pos)
    used_ref[...] = jnp.dot(slot_hot, ones, preferred_element_type=F32)
    kept_used_ref[...] = jnp.dot(kept_hot[BIG:], ones, preferred_element_type=F32)
    wide = jnp.broadcast_to(pos.astype(F32), (HD, tok))
    pos_col_ref[...] = jnp.transpose(wide).astype(jnp.int32)


def attend(q, k, v, g, valid, weight):
    scale = 1.0 / HD**0.5
    scores = lax.dot_general(k, q, NT, preferred_element_type=F32)
    if valid is not None:
        scores = jnp.where(valid, scores, -1e30)
    top = jnp.max(scores, axis=0, keepdims=True)
    raised = jnp.exp2((scores - top) * (scale * LOG2E))
    total = jnp.sum(raised, axis=0, keepdims=True)
    probs = raised * (1.0 / total)
    prob_grad = lax.dot_general(v, g, NT, preferred_element_type=F32)
    row_dot = jnp.sum(probs * prob_grad, axis=0, keepdims=True)
    scaled = probs * weight
    value_grad = jnp.dot(scaled.astype(BF16), g, preferred_element_type=F32)
    score_grad = (scaled * (prob_grad - row_dot)).astype(BF16)
    key_grad = jnp.dot(score_grad, q, preferred_element_type=F32) * scale
    query_grad = lax.dot_general(score_grad, k, TN, preferred_element_type=F32) * scale
    return query_grad.astype(BF16), key_grad.astype(BF16), value_grad.astype(BF16)


def block_dot(rows, w_ref, start):
    cols = rows.shape[1]
    weight = w_ref[:, pl.ds(pl.multiple_of(start, HD), cols)]
    return lax.dot_general(rows, weight, NT, preferred_element_type=F32)


def partial_kernel(n_mp, own_ref, hop1_ref, hop2_ref, w_ref, w_pair_ref, acc_ref, w_late_ref):
    feat = own_ref.shape[1]
    me = lax.axis_index("mp")
    chips = n_mp // 2
    chip, core = me // 2, me % 2

    def start(away):
        return (jnp.where(core == 0, chip - away, chip + away) + chips) % chips * (2 * feat)

    third = pl.multiple_of(start(3), HD)
    last = pl.multiple_of((me + chips) % n_mp * feat, HD)
    for side, weight_ref in enumerate((w_ref, w_pair_ref)):
        acc = block_dot(own_ref[...], weight_ref, me * feat)
        for away, hop_ref in ((1, hop1_ref), (2, hop2_ref)):
            for half in range(2):
                acc = acc + block_dot(hop_ref[half], weight_ref, start(away) + half * feat)
        acc_ref[side] = acc
        w_late_ref[side, :, : 2 * feat] = weight_ref[:, pl.ds(third, 2 * feat)]
        w_late_ref[side, :, 2 * feat :] = weight_ref[:, pl.ds(last, feat)]


def last_kernel(acc_ref, hop3_ref, hop4_ref, w_late_ref, mine_ref, pair_ref):
    feat = hop4_ref.shape[2]
    for side, out in enumerate((mine_ref, pair_ref)):
        acc = acc_ref[side]
        for part, rows in enumerate((hop3_ref[0], hop3_ref[1], hop4_ref[0])):
            weight = w_late_ref[side, :, part * feat : (part + 1) * feat]
            acc = acc + lax.dot_general(rows, weight, NT, preferred_element_type=F32)
        out[...] = acc


def spread(n_dp, half, slots):
    shape = (n_dp * OCT, slots)
    return one_hot(iota(shape, 0) == slot_row(iota(shape, 1), n_dp) + half)


def moved_kernel(n_dp, mine_ref, pair_ref, send_ref):
    slots = n_dp * CAP
    grad = (mine_ref[...] + pair_ref[...]).astype(BF16)
    send_ref[...] = (
        jnp.dot(spread(n_dp, 0, slots), grad[:, :HD], preferred_element_type=F32)
        + jnp.dot(spread(n_dp, 1, slots), grad[:, HD:], preferred_element_type=F32)
    ).astype(BF16)


def remote_kernel(n_dp, tok, img, rows_ref, grad_ref, valid_ref, send_ref):
    slots = n_dp * CAP
    shape = (slots, n_dp * OCT)
    first = slot_row(iota(shape, 0), n_dp)
    hot0 = one_hot(iota(shape, 1) == first)
    hot1 = one_hot(iota(shape, 1) == first + 1)
    rows, grad = rows_ref[...], grad_ref[...]
    a, b = pick(hot0, rows), pick(hot1, rows)
    g0, g1 = pick(hot0, grad), pick(hot1, grad)
    valid = valid_ref[:, 0:1]
    count = jnp.sum(valid, axis=0, keepdims=True)
    weight = tok / (img * count)
    mask = valid > 0.5
    q0, q1, k0 = a[:, :HD], a[:, HD : 2 * HD], a[:, 2 * HD :]
    k1, v0, v1 = b[:, :HD], b[:, HD : 2 * HD], b[:, 2 * HD :]
    dq0, dk0, dv0 = attend(q0, k0, v0, g0, mask, weight)
    dq1, dk1, dv1 = attend(q1, k1, v1, g1, mask, weight)
    send_ref[...] = (
        jnp.dot(spread(n_dp, 0, slots), jnp.concatenate([dq0, dq1, dk0], 1), preferred_element_type=F32)
        + jnp.dot(spread(n_dp, 1, slots), jnp.concatenate([dk1, dv0, dv1], 1), preferred_element_type=F32)
    ).astype(BF16)


def local_kernel(
    n_dp, tok, img, mine_ref, pair_ref, rows_ref, valid_ref, pos_ref, dq_ref, dk_ref, dv_ref
):
    slots = n_dp * CAP
    grad = (mine_ref[...] + pair_ref[...]).astype(BF16)
    valid = valid_ref[:, 0:1]
    count = jnp.sum(valid, axis=0, keepdims=True)
    images = (
        (slice(0, BIG), None, tok / (img * BIG)),
        (slice(BIG, KEPT), valid > 0.5, tok / (img * count)),
    )
    parts = []
    for head in range(2):
        lanes = slice(head * HD, (head + 1) * HD)
        pieces = []
        for span, mask, weight in images:
            q = rows_ref[span, head * HD : (head + 1) * HD]
            k = rows_ref[span, (2 + head) * HD : (3 + head) * HD]
            v = rows_ref[span, (4 + head) * HD : (5 + head) * HD]
            pieces.append(attend(q, k, v, grad[span, lanes], mask, weight))
        parts.append([jnp.concatenate(p, 0) for p in zip(*pieces)])
    pos = pos_ref[:, 0:1] - slots
    hot = one_hot(iota((tok, KEPT), 1) == pos)
    for name, out in enumerate((dq_ref, dk_ref, dv_ref)):
        out[...] = pick(hot, jnp.concatenate([parts[0][name], parts[1][name]], 1))


def merge_kernel(n_dp, back_ref, pos_ref, q_ref, k_ref, v_ref, dq_ref, dk_ref, dv_ref):
    tok = q_ref.shape[0]
    slots = n_dp * CAP
    pos = pos_ref[:, 0:1]
    first = jnp.where(pos < slots, slot_row(pos, n_dp), -OCT)
    col = iota((tok, n_dp * OCT), 1)
    back = back_ref[...]
    a = pick(one_hot(col == first), back)
    b = pick(one_hot(col == first + 1), back)
    dq_ref[...] = q_ref[...] + a[:, : 2 * HD]
    dk_ref[...] = k_ref[...] + jnp.concatenate([a[:, 2 * HD :], b[:, :HD]], 1)
    dv_ref[...] = v_ref[...] + b[:, HD:]


def sds(shape, dtype):
    return jax.ShapeDtypeStruct(shape, dtype)


def call(kernel, ins, outs, name, vmem=56, flops=0):
    def whole(x):
        zeros = (0,) * len(x.shape)
        return pl.BlockSpec(x.shape, lambda i: zeros)

    many = isinstance(outs, tuple)
    moved = sum(math.prod(x.shape) * x.dtype.itemsize for x in (*ins, *(outs if many else (outs,))))
    return pl.pallas_call(
        kernel,
        out_shape=outs,
        grid=(1,),
        in_specs=[whole(x) for x in ins],
        out_specs=tuple(whole(x) for x in outs) if many else whole(outs),
        compiler_params=pltpu.CompilerParams(vmem_limit_bytes=vmem * MIB),
        cost_estimate=pl.CostEstimate(flops=flops, bytes_accessed=moved, transcendentals=0),
        name=name,
    )(*ins)


def local(
    query_rows, key_rows, value_rows, out_grad, out_weight, destinations, image_ids, patch_counts
):
    tok, cols = query_rows.shape
    feat = out_grad.shape[1]
    n_dp, n_mp = lax.axis_size("dp"), lax.axis_size("mp")
    slots = n_dp * CAP
    img = patch_counts.shape[0]
    exch = n_dp * OCT
    pairs = [[2 * i, 2 * i + 1] for i in range(n_mp // 2)]
    swap = [(i, i ^ 1) for i in range(n_mp)]
    ring = [(i, (i + (2 if i % 2 == 0 else -2)) % n_mp) for i in range(n_mp)]

    def exchange(rows):
        shaped = rows.reshape(n_dp, OCT, rows.shape[1])
        return lax.all_to_all(shaped, "dp", split_axis=0, concat_axis=0, tiled=True).reshape(rows.shape)

    def after(value, earlier):
        return lax.optimization_barrier((value, earlier))[0]

    def hop(block):
        return lax.ppermute(block, "mp", ring)

    def both_cores(rows):
        return lax.all_gather(rows, "mp", axis=0, axis_index_groups=pairs)

    def opposite(block):
        half = lax.dynamic_slice_in_dim(block, lax.axis_index("mp") % 2, 1, 0)
        return hop(half)

    def projected(own, hop1, hop2):
        return call(
            functools.partial(partial_kernel, n_mp),
            (own, hop1, hop2, out_weight, pair_weight),
            (sds((2, own.shape[0], cols), F32), sds((2, cols, 3 * feat), BF16)),
            "partial",
        )

    def finished(acc, w_late, hop3, hop4):
        mine, pair = call(
            last_kernel, (acc, hop3, hop4, w_late), (sds((hop4.shape[1], cols), F32),) * 2, "last"
        )
        return mine, lax.ppermute(pair, "mp", swap)

    pair_weight = lax.ppermute(out_weight, "mp", swap)
    pos, og_moved = call(
        functools.partial(plan_kernel, n_dp),
        (destinations.reshape(1, tok), image_ids.reshape(1, tok), patch_counts.reshape(1, img), out_grad),
        (sds((8, tok), jnp.int32), sds((slots, feat), BF16)),
        "plan",
    )
    hop1 = hop(both_cores(og_moved))
    send, og_kept, rows_kept, used, kept_used, pos_col = call(
        functools.partial(pack_kernel, n_dp),
        (pos, out_grad, query_rows, key_rows, value_rows),
        (
            sds((exch, 3 * HD), BF16),
            sds((KEPT, feat), BF16),
            sds((KEPT, 3 * cols), BF16),
            sds((slots, HD), F32),
            sds((SMALL, HD), F32),
            sds((tok, HD), jnp.int32),
        ),
        "pack",
    )
    kept_block = both_cores(og_kept)
    rows_in = exchange(send)
    hop2 = hop(after(hop1, send))
    hop3 = hop(hop2)
    acc, w_late = projected(og_moved, hop1, hop2)
    hop4 = opposite(after(hop3, acc))
    kept1 = hop(after(kept_block, hop4))
    mine, pair = finished(acc, w_late, hop3, hop4)
    pair = after(pair, rows_in)
    grad_send = call(
        functools.partial(moved_kernel, n_dp), (mine, pair), sds((exch, HD), BF16), "moved", 8
    )
    grad_in = exchange(grad_send)
    kept2 = hop(after(kept1, grad_send))
    kept3 = hop(after(kept2, grad_in))
    back_send = call(
        functools.partial(remote_kernel, n_dp, tok, img),
        (rows_in, grad_in, used),
        sds((exch, 3 * HD), BF16),
        "remote",
        12,
    )
    back = exchange(back_send)
    kept4 = opposite(after(kept3, back_send))
    mine, pair = finished(*projected(og_kept, kept1, kept2), kept3, kept4)
    kept_grads = call(
        functools.partial(local_kernel, n_dp, tok, img),
        (mine, pair, rows_kept, kept_used, pos_col),
        (sds((tok, cols), BF16),) * 3,
        "kept",
        24,
    )
    return call(
        functools.partial(merge_kernel, n_dp),
        (back, pos_col) + kept_grads,
        (sds((tok, cols), BF16),) * 3,
        "merge",
        12,
    )


def solution(mesh):
    rows = P("dp", "mp")
    return jax.shard_map(
        local,
        mesh=mesh,
        in_specs=(rows, rows, rows, rows, P("mp", None), P("dp"), P("dp"), P("dp")),
        out_specs=(rows, rows, rows),
        check_vma=False,
    )
```

time: 243 us -> 151 us (0.62)
  the two profiles are of different devices: /device:TPU:2 before, /device:TPU:1 now
where the time goes in v1:
time: 151 us; the launch traced here: 150 us
  starting transfers between devices  74.3 us (49%)
  Pallas kernels  29.5 us (20%)
  blocking collectives  29.4 us (19%)
  waiting for transfers between devices  10.2 us (7%)
  local copies, waits for them, and re-layouts  6.02 us (4%)
    ppermute x8, starting transfers between devices, hop(): return lax.ppermute(block, 'mp', ring)  30.3 us
    pallas_call x10, Pallas kernels, call(): pl.pallas_call(kernel, out_shape=outs, grid=(1,), in_specs=[whole(x) for...  29.5 us
    all_to_all x1, blocking collectives, exchange(): lax.all_to_all(shaped, 'dp', split_axis=0, concat_axis=0, tiled=True)  23.7 us
    all_to_all x2, starting transfers between devices, exchange(): lax.all_to_all(shaped, 'dp', split_axis=0, concat_axis=0, tiled=True)  17.8 us
    ppermute x1, starting transfers between devices, local(): pair_weight = lax.ppermute(out_weight, 'mp', swap)  16.1 us
    ppermute x2, starting transfers between devices, finished(): return (mine, lax.ppermute(pair, 'mp', swap))  10.1 us
    ppermute x8, waiting for transfers between devices, hop(): return lax.ppermute(block, 'mp', ring)  7.6 us
    all_gather x2, blocking collectives, both_cores(): return lax.all_gather(rows, 'mp', axis=0, axis_index_groups=pairs)  5.66 us
  transfers between devices with their start and end apart: 13, of which 6 were waited for; matrix products, arithmetic and copies ran while one was open for 1% of the time, Pallas kernels for 18%

profile of v1, /device:TPU:1, one launch (start us, length us, event | category | flops | bytes accessed | tf_op | source)
XLA Modules:
  0.0 150.4 jit_solution(13995491260276955962)
XLA Ops:
  0.6 16.1 %collective-permute-start.2 = (bf16[256,6144]{1,0:T(8,128)(2,1)}, bf16[256,6144]{1,0:T(8,128)(2,1)S(1)}, u32[]{:S(2)}, u32[]{:S(2)}) collective-permute-start(bf16[256,6144]{1,0:T(8,128)(2,1)} %w_ref.3), channel_id=1, source_target_pairs={{0,1},{1,0},{2,3},{3,2},{4,5},{5,4},{6,7},{7,6},{8,9},{9,8},{10,11... | collective-permute-start | bytes 9437192 | tf_op jit(solution)/shard_map/ppermute | solution.py:293
  16.7 2.3 %plan.1 = (s32[8,512]{1,0:T(8,128)}, bf16[192,384]{1,0:T(8,128)(2,1)}) custom-call(s32[1,512]{1,0:T(1,128)} %bitcast.18, s32[1,512]{1,0:T(1,128)} %bitcast.19, s32[1,3]{1,0:T(1,128)} %bitcast.20, bf16[512,384]{1,0:T(8,128)(2,1)} %og_ref.3), custom_call_target="tpu_custom_call" | custom-call | bytes 561164 | tf_op jit(solution)/shard_map/plan/pallas_call | solution.py:237
  19.0 3.4 %all-gather = bf16[384,384]{1,0:T(8,128)(2,1)S(1)} all-gather(bf16[192,384]{1,0:T(8,128)(2,1)} %get-tuple-element.31.own_ref), channel_id=2, replica_groups={{0,1},{2,3},{4,5},{6,7},{8,9},{10,11},{12,13},{14,15},{16,17},{18,19},{..., dimensions={0}, use_global_device_ids=true | all-gather | bytes 442368 | tf_op jit(solution)/shard_map/all_gather | solution.py:273
  22.4 4.4 %collective-permute-start = (bf16[2,192,384]{2,1,0:T(8,128)(2,1)S(1)}, bf16[2,192,384]{2,1,0:T(8,128)(2,1)S(1)}, u32[]{:S(2)}, u32[]{:S(2)}) collective-permute-start(bf16[2,192,384]{2,1,0:T(8,128)(2,1)S(1)} %bitcast.17), channel_id=1, source_target_pairs={{0,2},{1,15},{2,4},{3,1},{4,6},{5,3},{6,8},{7,5},{8,10},{9,7},{10,... | collective-permute-start | bytes 884744 | tf_op jit(solution)/shard_map/ppermute | solution.py:270
  26.8 3.5 %pack.1 = (bf16[512,384]{1,0:T(8,128)(2,1)}, bf16[400,384]{1,0:T(8,128)(2,1)}, bf16[400,768]{1,0:T(8,128)(2,1)}, f32[192,128]{1,0:T(8,128)}, f32[144,128]{1,0:T(8,128)}, /*index=5*/s32[512,128]{1,0:T(8,128)}) custom-call(s32[8,512]{1,0:T(8,128)} %get-tuple-element.29.pos_ref, bf16[512,384]{1,0:T(8,128)(2,1)} %og_ref.3, bf16[512,256]{1,0:T(8,128)(2,1)} %q_ref.1, ...), custom_call_target="tpu_custom_call" | custom-call | bytes 2945024 | tf_op jit(solution)/shard_map/pack/pallas_call | solution.py:237
  30.3 0.2 collective-permute-done.hop1_ref
  30.4 0.0 copy-start.12
  30.4 0.7 copy-done.12
  31.1 5.0 %collective-permute-start.1 = (bf16[2,192,384]{2,1,0:T(8,128)(2,1)S(1)}, bf16[2,192,384]{2,1,0:T(8,128)(2,1)}, u32[]{:S(2)}, u32[]{:S(2)}) collective-permute-start(bf16[2,192,384]{2,1,0:T(8,128)(2,1)S(1)} %collective-permute-done.hop1_ref), channel_id=1, source_target_pairs={{0,2},{1,15},{2,4},{3,1},{4,6},{5,3},{6,8},{7,5},{8,10},{9,7},{10,... | collective-permute-start | bytes 884744 | tf_op jit(solution)/shard_map/ppermute | solution.py:270
  36.2 3.6 %collective-permute-done.1.hop2_ref = bf16[2,192,384]{2,1,0:T(8,128)(2,1)} collective-permute-done((bf16[2,192,384]{2,1,0:T(8,128)(2,1)S(1)}, bf16[2,192,384]{2,1,0:T(8,128)(2,1)}, u32[]{:S(2)}, u32[]{:S(2)}) %collective-permute-start.1) | collective-permute-done | bytes 294944 | tf_op jit(solution)/shard_map/ppermute | solution.py:270
  39.8 5.1 %collective-permute-start.3 = (bf16[2,192,384]{2,1,0:T(8,128)(2,1)}, bf16[2,192,384]{2,1,0:T(8,128)(2,1)}, u32[]{:S(2)}, u32[]{:S(2)}) collective-permute-start(bf16[2,192,384]{2,1,0:T(8,128)(2,1)} %collective-permute-done.1.hop2_ref), channel_id=1, source_target_pairs={{0,2},{1,15},{2,4},{3,1},{4,6},{5,3},{6,8},{7,5},{8,10},{9,7},{10,... | collective-permute-start | bytes 884744 | tf_op jit(solution)/shard_map/ppermute | solution.py:270
  44.9 13.2 %all-to-all-start = ((bf16[64,8,384]{2,1,0:T(8,128)(2,1)}), bf16[64,8,384]{2,1,0:T(8,128)(2,1)S(1)}, u32[]{:S(2)}, u32[]{:S(2)}) async-start(bf16[64,8,384]{2,1,0:T(8,128)(2,1)} %bitcast.16), calls=%async_computation | async-start | bytes 786432 | tf_op jit(solution)/shard_map/all_to_all | solution.py:264
  58.2 0.0 copy-start.8
  58.2 0.0 collective-permute-done.2.w_pair_ref
  58.2 0.0 copy-start.6
  58.2 1.6 %copy-done.6 = bf16[256,6144]{1,0:T(8,128)(2,1)} copy-done((bf16[256,6144]{1,0:T(8,128)(2,1)}, bf16[256,6144]{1,0:T(8,128)(2,1)S(1)}, u32[]{:S(2)}) %copy-start.6) | copy-done | bytes 3145752
  59.8 5.0 %partial.2 = (f32[2,192,256]{2,1,0:T(8,128)}, bf16[2,256,1152]{2,1,0:T(8,128)(2,1)}) custom-call(bf16[192,384]{1,0:T(8,128)(2,1)} %get-tuple-element.31.own_ref, bf16[2,192,384]{2,1,0:T(8,128)(2,1)} %copy-done.12, bf16[2,192,384]{2,1,0:T(8,128)(2,1)} %collective-permute-done.1.hop2_ref, bf16[256,6144]{1,0:T(8,128)(2,1)} %w_ref.3, bf16[256,6144]{1,0:T(8,128)(2,1)} %copy-done.6), custom_call_target="tpu_custom_call" | custom-call | bytes 8601600 | tf_op jit(solution)/shard_map/partial/pallas_call | solution.py:237
  64.8 0.0 copy-start.4
  64.8 0.0 collective-permute-done.3.hop3_ref
  64.8 1.0 constant_dynamic-slice_fusion.1
  65.8 1.9 %collective-permute-start.4 = (bf16[1,192,384]{2,1,0:T(8,128)(2,1)S(1)}, bf16[1,192,384]{2,1,0:T(8,128)(2,1)S(1)}, u32[]{:S(2)}, u32[]{:S(2)}) collective-permute-start(bf16[1,192,384]{2,1,0:T(8,128)(2,1)S(1)} %constant_dynamic-slice_fusion.1), channel_id=1, source_target_pairs={{0,2},{1,15},{2,4},{3,1},{4,6},{5,3},{6,8},{7,5},{8,10},{9,7},{10,... | collective-permute-start | bytes 442376 | tf_op jit(solution)/shard_map/ppermute | solution.py:270
  67.7 0.0 copy-done.8
  67.7 2.2 %all-gather.1 = bf16[800,384]{1,0:T(8,128)(2,1)S(1)} all-gather(bf16[400,384]{1,0:T(8,128)(2,1)S(1)} %copy-done.8), channel_id=3, replica_groups={{0,1},{2,3},{4,5},{6,7},{8,9},{10,11},{12,13},{14,15},{16,17},{18,19},{..., dimensions={0}, use_global_device_ids=true | all-gather | bytes 921600 | tf_op jit(solution)/shard_map/all_gather | solution.py:273
  70.0 2.0 %collective-permute-done.4.hop4_ref = bf16[1,192,384]{2,1,0:T(8,128)(2,1)S(1)} collective-permute-done((bf16[1,192,384]{2,1,0:T(8,128)(2,1)S(1)}, bf16[1,192,384]{2,1,0:T(8,128)(2,1)S(1)}, u32[]{:S(2)}, u32[]{:S(2)}) %collective-permute-start.4) | collective-permute-done | bytes 147488 | tf_op jit(solution)/shard_map/ppermute | solution.py:270
  72.0 0.0 copy-start.13
  72.0 3.1 %collective-permute-start.6 = (bf16[2,400,384]{2,1,0:T(8,128)(2,1)S(1)}, bf16[2,400,384]{2,1,0:T(8,128)(2,1)S(1)}, u32[]{:S(2)}, u32[]{:S(2)}) collective-permute-start(bf16[2,400,384]{2,1,0:T(8,128)(2,1)S(1)} %bitcast.15), channel_id=1, source_target_pairs={{0,2},{1,15},{2,4},{3,1},{4,6},{5,3},{6,8},{7,5},{8,10},{9,7},{10,... | collective-permute-start | bytes 1843208 | tf_op jit(solution)/shard_map/ppermute | solution.py:270
  75.1 0.0 copy-done.13
  75.1 2.8 %last.2 = (f32[192,256]{1,0:T(8,128)}, f32[192,256]{1,0:T(8,128)}) custom-call(f32[2,192,256]{2,1,0:T(8,128)} %get-tuple-element.33.acc_ref, bf16[2,192,384]{2,1,0:T(8,128)(2,1)} %collective-permute-done.3.hop3_ref, bf16[1,192,384]{2,1,0:T(8,128)(2,1)} %copy-done.13, bf16[2,256,1152]{2,1,0:T(8,128)(2,1)} %get-tuple-element.35.w_late_ref), custom_call_target="tpu_custom_call" | custom-call | bytes 2408448 | tf_op jit(solution)/shard_map/last/pallas_call | solution.py:237
  78.0 2.8 %collective-permute-start.5 = (f32[192,256]{1,0:T(8,128)}, f32[192,256]{1,0:T(8,128)S(1)}, u32[]{:S(2)}, u32[]{:S(2)}) collective-permute-start(f32[192,256]{1,0:T(8,128)} %get-tuple-element.37), channel_id=1, source_target_pairs={{0,1},{1,0},{2,3},{3,2},{4,5},{5,4},{6,7},{7,6},{8,9},{9,8},{10,11... | collective-permute-start | bytes 589832 | tf_op jit(solution)/shard_map/ppermute | solution.py:291
  80.7 0.0 all-to-all-done
  80.7 1.2 collective-permute-done.5.pair_ref
  82.0 0.0 copy-start.3
  82.0 0.9 copy-done.3
  82.9 0.3 moved.1
  83.2 0.0 collective-permute-done.6.hop1_ref
  83.2 0.0 copy-start.9
  83.2 4.9 %collective-permute-start.7 = (bf16[2,400,384]{2,1,0:T(8,128)(2,1)S(1)}, bf16[2,400,384]{2,1,0:T(8,128)(2,1)S(1)}, u32[]{:S(2)}, u32[]{:S(2)}) collective-permute-start(bf16[2,400,384]{2,1,0:T(8,128)(2,1)S(1)} %collective-permute-done.6.hop1_ref), channel_id=1, source_target_pairs={{0,2},{1,15},{2,4},{3,1},{4,6},{5,3},{6,8},{7,5},{8,10},{9,7},{10,... | collective-permute-start | bytes 1843208 | tf_op jit(solution)/shard_map/ppermute | solution.py:270
  88.1 23.7 %all_to_all.15 = bf16[64,8,128]{2,1,0:T(8,128)(2,1)S(1)} all-to-all(bf16[64,8,128]{2,1,0:T(8,128)(2,1)S(1)} %bitcast.13), channel_id=1, replica_groups=mesh['dp'=64,'mp'=16] {'dp'}, dimensions={0} | all-to-all | bytes 262144 | tf_op jit(solution)/shard_map/all_to_all | solution.py:264
  111.8 0.0 collective-permute-done.7.hop2_ref
  111.8 2.4 %collective-permute-start.8 = (bf16[2,400,384]{2,1,0:T(8,128)(2,1)S(1)}, bf16[2,400,384]{2,1,0:T(8,128)(2,1)S(1)}, u32[]{:S(2)}, u32[]{:S(2)}) collective-permute-start(bf16[2,400,384]{2,1,0:T(8,128)(2,1)S(1)} %collective-permute-done.7.hop2_ref), channel_id=1, source_target_pairs={{0,2},{1,15},{2,4},{3,1},{4,6},{5,3},{6,8},{7,5},{8,10},{9,7},{10,... | collective-permute-start | bytes 1843208 | tf_op jit(solution)/shard_map/ppermute | solution.py:270
  114.3 0.0 copy-done.4
  114.3 2.3 %remote.1 = bf16[512,384]{1,0:T(8,128)(2,1)} custom-call(bf16[512,384]{1,0:T(8,128)(2,1)S(1)} %bitcast.11, bf16[512,128]{1,0:T(8,128)(2,1)S(1)} %bitcast.14, f32[192,128]{1,0:T(8,128)S(1)} %copy-done.4), custom_call_target="tpu_custom_call" | custom-call | bytes 1015808 | tf_op jit(solution)/shard_map/remote/pallas_call | solution.py:237
  116.6 4.6 %all-to-all-start.2 = ((bf16[64,8,384]{2,1,0:T(8,128)(2,1)}), bf16[64,8,384]{2,1,0:T(8,128)(2,1)S(1)}, u32[]{:S(2)}, u32[]{:S(2)}) async-start(bf16[64,8,384]{2,1,0:T(8,128)(2,1)} %bitcast.8), calls=%async_computation.2 | async-start | bytes 786432 | tf_op jit(solution)/shard_map/all_to_all | solution.py:264
  121.2 1.8 %collective-permute-done.8.hop3_ref = bf16[2,400,384]{2,1,0:T(8,128)(2,1)S(1)} collective-permute-done((bf16[2,400,384]{2,1,0:T(8,128)(2,1)S(1)}, bf16[2,400,384]{2,1,0:T(8,128)(2,1)S(1)}, u32[]{:S(2)}, u32[]{:S(2)}) %collective-permute-start.8) | collective-permute-done | bytes 614432 | tf_op jit(solution)/shard_map/ppermute | solution.py:270
  123.0 0.0 copy-start
  123.1 0.0 copy-start.5
  123.1 3.5 %collective-permute-start.9 = (bf16[1,400,384]{2,1,0:T(8,128)(2,1)S(1)}, bf16[1,400,384]{2,1,0:T(8,128)(2,1)S(1)}, u32[]{:S(2)}, u32[]{:S(2)}) collective-permute-start(bf16[1,400,384]{2,1,0:T(8,128)(2,1)S(1)} %constant_dynamic-slice_fusion), channel_id=1, source_target_pairs={{0,2},{1,15},{2,4},{3,1},{4,6},{5,3},{6,8},{7,5},{8,10},{9,7},{10,... | collective-permute-start | bytes 921608 | tf_op jit(solution)/shard_map/ppermute | solution.py:270
  126.5 0.0 copy-done.9
  126.6 0.0 copy-done.10
  126.6 5.9 %partial.3 = (f32[2,400,256]{2,1,0:T(8,128)}, bf16[2,256,1152]{2,1,0:T(8,128)(2,1)}) custom-call(bf16[400,384]{1,0:T(8,128)(2,1)} %get-tuple-element.41.own_ref, bf16[2,400,384]{2,1,0:T(8,128)(2,1)} %copy-done.9, bf16[2,400,384]{2,1,0:T(8,128)(2,1)} %copy-done.10, bf16[256,6144]{1,0:T(8,128)(2,1)} %w_ref.3, bf16[256,6144]{1,0:T(8,128)(2,1)} %copy-done.6), custom_call_target="tpu_custom_call" | custom-call | bytes 9826304 | tf_op jit(solution)/shard_map/partial/pallas_call | solution.py:237
  132.5 0.0 copy-done.7
  132.5 0.0 collective-permute-done.9.hop4_ref
  132.5 0.0 copy-start.11
  132.5 0.7 copy-done.11
  133.3 3.5 %last.3 = (f32[400,256]{1,0:T(8,128)}, f32[400,256]{1,0:T(8,128)}) custom-call(f32[2,400,256]{2,1,0:T(8,128)} %get-tuple-element.44.acc_ref, bf16[2,400,384]{2,1,0:T(8,128)(2,1)} %copy-done.7, bf16[1,400,384]{2,1,0:T(8,128)(2,1)} %copy-done.11, bf16[2,256,1152]{2,1,0:T(8,128)(2,1)} %get-tuple-element.47.w_late_ref), custom_call_target="tpu_custom_call" | custom-call | bytes 3739648 | tf_op jit(solution)/shard_map/last/pallas_call | solution.py:237
  136.8 7.3 %collective-permute-start.10 = (f32[400,256]{1,0:T(8,128)}, f32[400,256]{1,0:T(8,128)S(1)}, u32[]{:S(2)}, u32[]{:S(2)}) collective-permute-start(f32[400,256]{1,0:T(8,128)} %get-tuple-element.49), channel_id=1, source_target_pairs={{0,1},{1,0},{2,3},{3,2},{4,5},{5,4},{6,7},{7,6},{8,9},{9,8},{10,11... | collective-permute-start | bytes 1228808 | tf_op jit(solution)/shard_map/ppermute | solution.py:291
  144.1 1.4 collective-permute-done.10.pair_ref
  145.5 0.0 copy-done
  145.5 0.0 copy-done.5
  145.5 0.0 copy-done.1
  145.5 1.0 copy-done.2
  146.5 2.1 %kept.1 = (bf16[512,256]{1,0:T(8,128)(2,1)S(1)}, bf16[512,256]{1,0:T(8,128)(2,1)S(1)}, bf16[512,256]{1,0:T(8,128)(2,1)S(1)}) custom-call(f32[400,256]{1,0:T(8,128)S(1)} %copy-done.2, f32[400,256]{1,0:T(8,128)S(1)} %collective-permute-done.10.pair_ref, bf16[400,768]{1,0:T(8,128)(2,1)S(1)} %copy-done.1, f32[144,128]{1,0:T(8,128)S(1)} %copy-done.5, ...), custom_call_target="tpu_custom_call" | custom-call | bytes 2555904 | tf_op jit(solution)/shard_map/kept/pallas_call | solution.py:237
  148.6 0.0 all-to-all-done.2
  148.6 1.7 %merge.1 = (bf16[512,256]{1,0:T(8,128)(2,1)}, bf16[512,256]{1,0:T(8,128)(2,1)}, bf16[512,256]{1,0:T(8,128)(2,1)}) custom-call(bf16[512,384]{1,0:T(8,128)(2,1)S(1)} %bitcast.12, s32[512,128]{1,0:T(8,128)S(1)} %copy-done, bf16[512,256]{1,0:T(8,128)(2,1)S(1)} %get-tuple-element.52.q_ref, bf16[512,256]{1,0:T(8,128)(2,1)S(1)} %get-tuple-element.53.k_ref, ...), custom_call_target="tpu_custom_call" | custom-call | bytes 2228224 | tf_op jit(solution)/shard_map/merge/pallas_call | solution.py:237
  (5 shorter events, 0.0 us)
Async XLA Ops:
  0.6 57.6 %collective-permute-start.2 = (bf16[256,6144]{1,0:T(8,128)(2,1)}, bf16[256,6144]{1,0:T(8,128)(2,1)S(1)}, u32[]{:S(2)}, u32[]{:S(2)}) collective-permute-start(bf16[256,6144]{1,0:T(8,128)(2,1)} %w_ref.3), channel_id=1, source_target_pairs={{0,1},{1,0},{2,3},{3,2},{4,5},{5,4},{6,7},{7,6},{8,9},{9,8},{10,11... | collective-permute-start | bytes 9437192 | tf_op jit(solution)/shard_map/ppermute | solution.py:293
  22.4 8.0 %collective-permute-start = (bf16[2,192,384]{2,1,0:T(8,128)(2,1)S(1)}, bf16[2,192,384]{2,1,0:T(8,128)(2,1)S(1)}, u32[]{:S(2)}, u32[]{:S(2)}) collective-permute-start(bf16[2,192,384]{2,1,0:T(8,128)(2,1)S(1)} %bitcast.17), channel_id=1, source_target_pairs={{0,2},{1,15},{2,4},{3,1},{4,6},{5,3},{6,8},{7,5},{8,10},{9,7},{10,... | collective-permute-start | bytes 884744 | tf_op jit(solution)/shard_map/ppermute | solution.py:270
  30.4 0.7 copy-start.12
  31.1 8.7 %collective-permute-start.1 = (bf16[2,192,384]{2,1,0:T(8,128)(2,1)S(1)}, bf16[2,192,384]{2,1,0:T(8,128)(2,1)}, u32[]{:S(2)}, u32[]{:S(2)}) collective-permute-start(bf16[2,192,384]{2,1,0:T(8,128)(2,1)S(1)} %collective-permute-done.hop1_ref), channel_id=1, source_target_pairs={{0,2},{1,15},{2,4},{3,1},{4,6},{5,3},{6,8},{7,5},{8,10},{9,7},{10,... | collective-permute-start | bytes 884744 | tf_op jit(solution)/shard_map/ppermute | solution.py:270
  39.8 25.0 %collective-permute-start.3 = (bf16[2,192,384]{2,1,0:T(8,128)(2,1)}, bf16[2,192,384]{2,1,0:T(8,128)(2,1)}, u32[]{:S(2)}, u32[]{:S(2)}) collective-permute-start(bf16[2,192,384]{2,1,0:T(8,128)(2,1)} %collective-permute-done.1.hop2_ref), channel_id=1, source_target_pairs={{0,2},{1,15},{2,4},{3,1},{4,6},{5,3},{6,8},{7,5},{8,10},{9,7},{10,... | collective-permute-start | bytes 884744 | tf_op jit(solution)/shard_map/ppermute | solution.py:270
  44.9 35.8 %all-to-all-start = ((bf16[64,8,384]{2,1,0:T(8,128)(2,1)}), bf16[64,8,384]{2,1,0:T(8,128)(2,1)S(1)}, u32[]{:S(2)}, u32[]{:S(2)}) async-start(bf16[64,8,384]{2,1,0:T(8,128)(2,1)} %bitcast.16), calls=%async_computation | async-start | bytes 786432 | tf_op jit(solution)/shard_map/all_to_all | solution.py:264
  58.2 9.5 %copy-start.8 = (bf16[400,384]{1,0:T(8,128)(2,1)S(1)}, bf16[400,384]{1,0:T(8,128)(2,1)}, u32[]{:S(2)}) copy-start(bf16[400,384]{1,0:T(8,128)(2,1)} %get-tuple-element.41.own_ref) | copy-start | bytes 921604
  58.2 1.6 %copy-start.6 = (bf16[256,6144]{1,0:T(8,128)(2,1)}, bf16[256,6144]{1,0:T(8,128)(2,1)S(1)}, u32[]{:S(2)}) copy-start(bf16[256,6144]{1,0:T(8,128)(2,1)S(1)} %collective-permute-done.2.w_pair_ref) | copy-start | bytes 9437188
  64.8 49.4 %copy-start.4 = (f32[192,128]{1,0:T(8,128)S(1)}, f32[192,128]{1,0:T(8,128)}, u32[]{:S(2)}) copy-start(f32[192,128]{1,0:T(8,128)} %get-tuple-element.39.valid_ref) | copy-start | bytes 294916
  65.8 6.2 %collective-permute-start.4 = (bf16[1,192,384]{2,1,0:T(8,128)(2,1)S(1)}, bf16[1,192,384]{2,1,0:T(8,128)(2,1)S(1)}, u32[]{:S(2)}, u32[]{:S(2)}) collective-permute-start(bf16[1,192,384]{2,1,0:T(8,128)(2,1)S(1)} %constant_dynamic-slice_fusion.1), channel_id=1, source_target_pairs={{0,2},{1,15},{2,4},{3,1},{4,6},{5,3},{6,8},{7,5},{8,10},{9,7},{10,... | collective-permute-start | bytes 442376 | tf_op jit(solution)/shard_map/ppermute | solution.py:270
  72.0 3.1 %copy-start.13 = (bf16[1,192,384]{2,1,0:T(8,128)(2,1)}, bf16[1,192,384]{2,1,0:T(8,128)(2,1)S(1)}, u32[]{:S(2)}) copy-start(bf16[1,192,384]{2,1,0:T(8,128)(2,1)S(1)} %collective-permute-done.4.hop4_ref) | copy-start | bytes 442372
  72.0 11.2 %collective-permute-start.6 = (bf16[2,400,384]{2,1,0:T(8,128)(2,1)S(1)}, bf16[2,400,384]{2,1,0:T(8,128)(2,1)S(1)}, u32[]{:S(2)}, u32[]{:S(2)}) collective-permute-start(bf16[2,400,384]{2,1,0:T(8,128)(2,1)S(1)} %bitcast.15), channel_id=1, source_target_pairs={{0,2},{1,15},{2,4},{3,1},{4,6},{5,3},{6,8},{7,5},{8,10},{9,7},{10,... | collective-permute-start | bytes 1843208 | tf_op jit(solution)/shard_map/ppermute | solution.py:270
  78.0 4.0 %collective-permute-start.5 = (f32[192,256]{1,0:T(8,128)}, f32[192,256]{1,0:T(8,128)S(1)}, u32[]{:S(2)}, u32[]{:S(2)}) collective-permute-start(f32[192,256]{1,0:T(8,128)} %get-tuple-element.37), channel_id=1, source_target_pairs={{0,1},{1,0},{2,3},{3,2},{4,5},{5,4},{6,7},{7,6},{8,9},{9,8},{10,11... | collective-permute-start | bytes 589832 | tf_op jit(solution)/shard_map/ppermute | solution.py:291
  82.0 0.9 copy-start.3
  83.2 43.3 %copy-start.9 = (bf16[2,400,384]{2,1,0:T(8,128)(2,1)}, bf16[2,400,384]{2,1,0:T(8,128)(2,1)S(1)}, u32[]{:S(2)}) copy-start(bf16[2,400,384]{2,1,0:T(8,128)(2,1)S(1)} %collective-permute-done.6.hop1_ref) | copy-start | bytes 1843204
  83.2 28.6 %collective-permute-start.7 = (bf16[2,400,384]{2,1,0:T(8,128)(2,1)S(1)}, bf16[2,400,384]{2,1,0:T(8,128)(2,1)S(1)}, u32[]{:S(2)}, u32[]{:S(2)}) collective-permute-start(bf16[2,400,384]{2,1,0:T(8,128)(2,1)S(1)} %collective-permute-done.6.hop1_ref), channel_id=1, source_target_pairs={{0,2},{1,15},{2,4},{3,1},{4,6},{5,3},{6,8},{7,5},{8,10},{9,7},{10,... | collective-permute-start | bytes 1843208 | tf_op jit(solution)/shard_map/ppermute | solution.py:270
  111.8 14.7 %copy-start.10 = (bf16[2,400,384]{2,1,0:T(8,128)(2,1)}, bf16[2,400,384]{2,1,0:T(8,128)(2,1)S(1)}, u32[]{:S(2)}) copy-start(bf16[2,400,384]{2,1,0:T(8,128)(2,1)S(1)} %collective-permute-done.7.hop2_ref) | copy-start | bytes 1843204
  111.8 11.2 %collective-permute-start.8 = (bf16[2,400,384]{2,1,0:T(8,128)(2,1)S(1)}, bf16[2,400,384]{2,1,0:T(8,128)(2,1)S(1)}, u32[]{:S(2)}, u32[]{:S(2)}) collective-permute-start(bf16[2,400,384]{2,1,0:T(8,128)(2,1)S(1)} %collective-permute-done.7.hop2_ref), channel_id=1, source_target_pairs={{0,2},{1,15},{2,4},{3,1},{4,6},{5,3},{6,8},{7,5},{8,10},{9,7},{10,... | collective-permute-start | bytes 1843208 | tf_op jit(solution)/shard_map/ppermute | solution.py:270
  116.6 32.0 %all-to-all-start.2 = ((bf16[64,8,384]{2,1,0:T(8,128)(2,1)}), bf16[64,8,384]{2,1,0:T(8,128)(2,1)S(1)}, u32[]{:S(2)}, u32[]{:S(2)}) async-start(bf16[64,8,384]{2,1,0:T(8,128)(2,1)} %bitcast.8), calls=%async_computation.2 | async-start | bytes 786432 | tf_op jit(solution)/shard_map/all_to_all | solution.py:264
  123.0 9.5 %copy-start.7 = (bf16[2,400,384]{2,1,0:T(8,128)(2,1)}, bf16[2,400,384]{2,1,0:T(8,128)(2,1)S(1)}, u32[]{:S(2)}) copy-start(bf16[2,400,384]{2,1,0:T(8,128)(2,1)S(1)} %collective-permute-done.8.hop3_ref) | copy-start | bytes 1843204
  123.0 22.5 %copy-start = (s32[512,128]{1,0:T(8,128)S(1)}, s32[512,128]{1,0:T(8,128)}, u32[]{:S(2)}) copy-start(s32[512,128]{1,0:T(8,128)} %get-tuple-element.40.pos_ref) | copy-start | bytes 786436
  123.1 22.4 %copy-start.5 = (f32[144,128]{1,0:T(8,128)S(1)}, f32[144,128]{1,0:T(8,128)}, u32[]{:S(2)}) copy-start(f32[144,128]{1,0:T(8,128)} %get-tuple-element.51.valid_ref) | copy-start | bytes 221188
  123.1 9.5 %collective-permute-start.9 = (bf16[1,400,384]{2,1,0:T(8,128)(2,1)S(1)}, bf16[1,400,384]{2,1,0:T(8,128)(2,1)S(1)}, u32[]{:S(2)}, u32[]{:S(2)}) collective-permute-start(bf16[1,400,384]{2,1,0:T(8,128)(2,1)S(1)} %constant_dynamic-slice_fusion), channel_id=1, source_target_pairs={{0,2},{1,15},{2,4},{3,1},{4,6},{5,3},{6,8},{7,5},{8,10},{9,7},{10,... | collective-permute-start | bytes 921608 | tf_op jit(solution)/shard_map/ppermute | solution.py:270
  132.5 13.0 %copy-start.1 = (bf16[400,768]{1,0:T(8,128)(2,1)S(1)}, bf16[400,768]{1,0:T(8,128)(2,1)}, u32[]{:S(2)}) copy-start(bf16[400,768]{1,0:T(8,128)(2,1)} %get-tuple-element.50.rows_ref) | copy-start | bytes 1843204
  132.5 0.7 copy-start.11
  136.8 8.7 %collective-permute-start.10 = (f32[400,256]{1,0:T(8,128)}, f32[400,256]{1,0:T(8,128)S(1)}, u32[]{:S(2)}, u32[]{:S(2)}) collective-permute-start(f32[400,256]{1,0:T(8,128)} %get-tuple-element.49), channel_id=1, source_target_pairs={{0,1},{1,0},{2,3},{3,2},{4,5},{5,4},{6,7},{7,6},{8,9},{9,8},{10,11... | collective-permute-start | bytes 1228808 | tf_op jit(solution)/shard_map/ppermute | solution.py:291
  145.5 1.0 copy-start.2

commit v2 on v1

--- a/solution.py
+++ b/solution.py
@@ -59,7 +59,9 @@
     place = jnp.where(member, start.astype(F32) + step * rank, 0.0)
     pos = jnp.sum(place, axis=0, keepdims=True).astype(jnp.int32)
     pos_ref[...] = jnp.broadcast_to(pos, pos_ref.shape)
-    og_moved_ref[...] = pick(one_hot(iota((slots, tok), 0) == pos), og_ref[...])
+    rows = pick(one_hot(iota((slots, tok), 0) == pos), og_ref[...])
+    for copy in range(og_moved_ref.shape[0]):
+        og_moved_ref[copy] = rows
 
 
 def pack_kernel(
@@ -150,30 +152,39 @@
     return one_hot(iota(shape, 0) == slot_row(iota(shape, 1), n_dp) + half)
 
 
-def moved_kernel(n_dp, mine_ref, pair_ref, send_ref):
+def chips_kernel(n_mp, og_ref, w_ref, w_pair_ref, mine_ref, pair_ref):
+    chips, _, feat = og_ref.shape
+    core = lax.axis_index("mp") % 2
+    for weight_ref, out in ((w_ref, mine_ref), (w_pair_ref, pair_ref)):
+        acc = block_dot(og_ref[0], weight_ref, core * feat)
+        for chip in range(1, chips):
+            acc = acc + block_dot(og_ref[chip], weight_ref, (2 * chip + core) * feat)
+        out[...] = acc
+
+
+def moved_kernel(n_dp, mine_ref, pair_ref, rows_ref, send_ref):
     slots = n_dp * CAP
     grad = (mine_ref[...] + pair_ref[...]).astype(BF16)
-    send_ref[...] = (
+    send_ref[:, : 3 * HD] = rows_ref[...]
+    send_ref[:, 3 * HD :] = (
         jnp.dot(spread(n_dp, 0, slots), grad[:, :HD], preferred_element_type=F32)
         + jnp.dot(spread(n_dp, 1, slots), grad[:, HD:], preferred_element_type=F32)
     ).astype(BF16)
 
 
-def remote_kernel(n_dp, tok, img, rows_ref, grad_ref, valid_ref, send_ref):
+def remote_kernel(n_dp, tok, img, rows_ref, valid_ref, send_ref):
     slots = n_dp * CAP
     shape = (slots, n_dp * OCT)
     first = slot_row(iota(shape, 0), n_dp)
     hot0 = one_hot(iota(shape, 1) == first)
     hot1 = one_hot(iota(shape, 1) == first + 1)
-    rows, grad = rows_ref[...], grad_ref[...]
-    a, b = pick(hot0, rows), pick(hot1, rows)
-    g0, g1 = pick(hot0, grad), pick(hot1, grad)
+    a, b = pick(hot0, rows_ref[...]), pick(hot1, rows_ref[...])
     valid = valid_ref[:, 0:1]
     count = jnp.sum(valid, axis=0, keepdims=True)
     weight = tok / (img * count)
     mask = valid > 0.5
-    q0, q1, k0 = a[:, :HD], a[:, HD : 2 * HD], a[:, 2 * HD :]
-    k1, v0, v1 = b[:, :HD], b[:, HD : 2 * HD], b[:, 2 * HD :]
+    q0, q1, k0, g0 = (a[:, i * HD : (i + 1) * HD] for i in range(4))
+    k1, v0, v1, g1 = (b[:, i * HD : (i + 1) * HD] for i in range(4))
     dq0, dk0, dv0 = attend(q0, k0, v0, g0, mask, weight)
     dq1, dk1, dv1 = attend(q1, k1, v1, g1, mask, weight)
     send_ref[...] = (
@@ -290,14 +301,16 @@
         )
         return mine, lax.ppermute(pair, "mp", swap)
 
-    pair_weight = lax.ppermute(out_weight, "mp", swap)
     pos, og_moved = call(
         functools.partial(plan_kernel, n_dp),
         (destinations.reshape(1, tok), image_ids.reshape(1, tok), patch_counts.reshape(1, img), out_grad),
-        (sds((8, tok), jnp.int32), sds((slots, feat), BF16)),
+        (sds((8, tok), jnp.int32), sds((n_mp // 2, slots, feat), BF16)),
         "plan",
     )
-    hop1 = hop(both_cores(og_moved))
+    same_core = [list(range(core, n_mp, 2)) for core in range(2)]
+    og_chips = lax.all_to_all(
+        og_moved, "mp", split_axis=0, concat_axis=0, tiled=True, axis_index_groups=same_core
+    )
     send, og_kept, rows_kept, used, kept_used, pos_col = call(
         functools.partial(pack_kernel, n_dp),
         (pos, out_grad, query_rows, key_rows, value_rows),
@@ -311,24 +324,30 @@
         ),
         "pack",
     )
+    pair_weight = lax.ppermute(after(out_weight, pos), "mp", swap)
     kept_block = both_cores(og_kept)
-    rows_in = exchange(send)
-    hop2 = hop(after(hop1, send))
-    hop3 = hop(hop2)
-    acc, w_late = projected(og_moved, hop1, hop2)
-    hop4 = opposite(after(hop3, acc))
-    kept1 = hop(after(kept_block, hop4))
-    mine, pair = finished(acc, w_late, hop3, hop4)
-    pair = after(pair, rows_in)
-    grad_send = call(
-        functools.partial(moved_kernel, n_dp), (mine, pair), sds((exch, HD), BF16), "moved", 8
-    )
-    grad_in = exchange(grad_send)
-    kept2 = hop(after(kept1, grad_send))
-    kept3 = hop(after(kept2, grad_in))
+    kept1 = hop(after(kept_block, og_chips))
+    mine, pair = call(
+        functools.partial(chips_kernel, n_mp),
+        (og_chips, out_weight, pair_weight),
+        (sds((slots, cols), F32),) * 2,
+        "chips",
+        24,
+    )
+    pair = lax.ppermute(pair, "mp", swap)
+    moved_send = call(
+        functools.partial(moved_kernel, n_dp),
+        (mine, pair, send),
+        sds((exch, 4 * HD), BF16),
+        "moved",
+        8,
+    )
+    rows_in = exchange(moved_send)
+    kept2 = hop(after(kept1, moved_send))
+    kept3 = hop(kept2)
     back_send = call(
         functools.partial(remote_kernel, n_dp, tok, img),
-        (rows_in, grad_in, used),
+        (rows_in, used),
         sds((exch, 3 * HD), BF16),
         "remote",
         12,

time: 151 us -> 135 us (0.89)
  waiting for transfers between devices: 10.2 us -> 42.5 us
  blocking collectives: 29.4 us -> 3.9 us
  starting transfers between devices: 74.3 us -> 58.9 us
  local copies, waits for them, and re-layouts: 6.02 us -> 1.78 us
  Pallas kernels: 29.5 us -> 26.4 us
    all_to_all x0 -> x1, waiting for transfers between devices: none -> 24.7 us  [local(): lax.all_to_all(og_moved, 'mp', split_axis=0, concat_axis=0, tiled=True, a...]
    all_to_all x1 -> x0, blocking collectives: 23.7 us -> none  [exchange(): lax.all_to_all(shaped, 'dp', split_axis=0, concat_axis=0, tiled=True)]
    ppermute x8 -> x4, starting transfers between devices: 30.3 us -> 9.24 us  [hop(): return lax.ppermute(block, 'mp', ring)]
    all_to_all x2, waiting for transfers between devices: 0.01 us -> 14.2 us  [exchange(): lax.all_to_all(shaped, 'dp', split_axis=0, concat_axis=0, tiled=True)]
    ppermute x8 -> x4, waiting for transfers between devices: 7.6 us -> 1 us  [hop(): return lax.ppermute(block, 'mp', ring)]
    all_to_all x0 -> x1, starting transfers between devices: none -> 4.54 us  [local(): lax.all_to_all(og_moved, 'mp', split_axis=0, concat_axis=0, tiled=True, a...]
    ppermute x2 -> x1, starting transfers between devices: 10.1 us -> 5.76 us  [finished(): return (mine, lax.ppermute(pair, 'mp', swap))]
    unnamed x28 -> x20, local copies, waits for them, and re-layouts: 5.03 us -> 1.74 us
  transfers between devices with their start and end apart: 13 -> 10, of which waited for: 6 -> 5; matrix products, arithmetic and copies ran while one was open for 1% -> 0% of each run, Pallas kernels for 18% -> 16%
where the time goes in v2:
time: 135 us; the launch traced here: 134 us
  starting transfers between devices  58.9 us (44%)
  waiting for transfers between devices  42.5 us (31%)
  Pallas kernels  26.4 us (20%)
  blocking collectives  3.9 us (3%)
  local copies, waits for them, and re-layouts  1.78 us (1%)
    pallas_call x9, Pallas kernels, call(): pl.pallas_call(kernel, out_shape=outs, grid=(1,), in_specs=[whole(x) for...  26.4 us
    all_to_all x1, waiting for transfers between devices, local(): lax.all_to_all(og_moved, 'mp', split_axis=0, concat_axis=0, tiled=True, a...  24.7 us
    all_to_all x2, starting transfers between devices, exchange(): lax.all_to_all(shaped, 'dp', split_axis=0, concat_axis=0, tiled=True)  20.5 us
    ppermute x1, starting transfers between devices, local(): pair_weight = lax.ppermute(after(out_weight, pos), 'mp', swap)  16.1 us
    all_to_all x2, waiting for transfers between devices, exchange(): lax.all_to_all(shaped, 'dp', split_axis=0, concat_axis=0, tiled=True)  14.2 us
    ppermute x4, starting transfers between devices, hop(): return lax.ppermute(block, 'mp', ring)  9.24 us
    ppermute x1, starting transfers between devices, finished(): return (mine, lax.ppermute(pair, 'mp', swap))  5.76 us
    all_to_all x1, starting transfers between devices, local(): lax.all_to_all(og_moved, 'mp', split_axis=0, concat_axis=0, tiled=True, a...  4.54 us
  transfers between devices with their start and end apart: 10, of which 5 were waited for; matrix products, arithmetic and copies ran while one was open for 0% of the time, Pallas kernels for 16%

profile of v2, /device:TPU:1, one launch (start us, length us, event | category | flops | bytes accessed | tf_op | source)
XLA Modules:
  0.0 134.3 jit_solution(12670007420460306234)
XLA Ops:
  0.6 2.7 %plan.1 = (s32[8,512]{1,0:T(8,128)}, bf16[8,192,384]{2,1,0:T(8,128)(2,1)}) custom-call(s32[1,512]{1,0:T(1,128)} %bitcast.11, s32[1,512]{1,0:T(1,128)} %bitcast.12, s32[1,3]{1,0:T(1,128)} %bitcast.13, bf16[512,384]{1,0:T(8,128)(2,1)} %og_ref.3), custom_call_target="tpu_custom_call" | custom-call | bytes 1593356 | tf_op jit(solution)/shard_map/plan/pallas_call | solution.py:248
  3.3 16.1 %collective-permute-start = (bf16[256,6144]{1,0:T(8,128)(2,1)}, bf16[256,6144]{1,0:T(8,128)(2,1)}, u32[]{:S(2)}, u32[]{:S(2)}) collective-permute-start(bf16[256,6144]{1,0:T(8,128)(2,1)} %w_ref.3), channel_id=1, source_target_pairs={{0,1},{1,0},{2,3},{3,2},{4,5},{5,4},{6,7},{7,6},{8,9},{9,8},{10,11... | collective-permute-start | bytes 9437192 | tf_op jit(solution)/shard_map/ppermute | solution.py:327
  19.4 0.0 copy-start
  19.4 4.5 %all-to-all-start = ((bf16[8,192,384]{2,1,0:T(8,128)(2,1)}), bf16[8,192,384]{2,1,0:T(8,128)(2,1)}, u32[]{:S(2)}, u32[]{:S(2)}) async-start(bf16[8,192,384]{2,1,0:T(8,128)(2,1)} %get-tuple-element.24), calls=%async_computation | async-start | bytes 2359296 | tf_op jit(solution)/shard_map/all_to_all | solution.py:311
  23.9 3.5 %pack.1 = (bf16[512,384]{1,0:T(8,128)(2,1)}, bf16[400,384]{1,0:T(8,128)(2,1)}, bf16[400,768]{1,0:T(8,128)(2,1)}, f32[192,128]{1,0:T(8,128)}, f32[144,128]{1,0:T(8,128)}, /*index=5*/s32[512,128]{1,0:T(8,128)}) custom-call(s32[8,512]{1,0:T(8,128)} %get-tuple-element.25.pos_ref, bf16[512,384]{1,0:T(8,128)(2,1)} %og_ref.3, bf16[512,256]{1,0:T(8,128)(2,1)} %q_ref.1, ...), custom_call_target="tpu_custom_call" | custom-call | bytes 2945024 | tf_op jit(solution)/shard_map/pack/pallas_call | solution.py:248
  27.4 3.9 %all-gather = bf16[800,384]{1,0:T(8,128)(2,1)} all-gather(bf16[400,384]{1,0:T(8,128)(2,1)} %get-tuple-element.32.own_ref), channel_id=2, replica_groups={{0,1},{2,3},{4,5},{6,7},{8,9},{10,11},{12,13},{14,15},{16,17},{18,19},{..., dimensions={0}, use_global_device_ids=true | all-gather | bytes 921600 | tf_op jit(solution)/shard_map/all_gather | solution.py:284
  31.3 24.7 %all-to-all-done.og_ref = bf16[8,192,384]{2,1,0:T(8,128)(2,1)} async-done(((bf16[8,192,384]{2,1,0:T(8,128)(2,1)}), bf16[8,192,384]{2,1,0:T(8,128)(2,1)}, u32[]{:S(2)}, u32[]{:S(2)}) %all-to-all-start) | async-done | bytes 1179680 | tf_op jit(solution)/shard_map/all_to_all | solution.py:311
  56.0 0.0 copy-start.4
  56.0 2.0 %collective-permute-start.2 = (bf16[2,400,384]{2,1,0:T(8,128)(2,1)}, bf16[2,400,384]{2,1,0:T(8,128)(2,1)}, u32[]{:S(2)}, u32[]{:S(2)}) collective-permute-start(bf16[2,400,384]{2,1,0:T(8,128)(2,1)} %bitcast.10), channel_id=1, source_target_pairs={{0,2},{1,15},{2,4},{3,1},{4,6},{5,3},{6,8},{7,5},{8,10},{9,7},{10,... | collective-permute-start | bytes 1843208 | tf_op jit(solution)/shard_map/ppermute | solution.py:281
  58.1 0.0 collective-permute-done.w_pair_ref
  58.1 0.0 copy-done
  58.1 3.5 %chips.1 = (f32[192,256]{1,0:T(8,128)S(1)}, f32[192,256]{1,0:T(8,128)S(1)}) custom-call(bf16[8,192,384]{2,1,0:T(8,128)(2,1)} %all-to-all-done.og_ref, bf16[256,6144]{1,0:T(8,128)(2,1)S(1)} %copy-done, bf16[256,6144]{1,0:T(8,128)(2,1)} %collective-permute-done.w_pair_ref), custom_call_target="tpu_custom_call" | custom-call | bytes 7864320 | tf_op jit(solution)/shard_map/chips/pallas_call | solution.py:248
  61.6 2.9 %collective-permute-start.1 = (f32[192,256]{1,0:T(8,128)S(1)}, f32[192,256]{1,0:T(8,128)S(1)}, u32[]{:S(2)}, u32[]{:S(2)}) collective-permute-start(f32[192,256]{1,0:T(8,128)S(1)} %get-tuple-element.28), channel_id=1, source_target_pairs={{0,1},{1,0},{2,3},{3,2},{4,5},{5,4},{6,7},{7,6},{8,9},{9,8},{10,11... | collective-permute-start | bytes 589832 | tf_op jit(solution)/shard_map/ppermute | solution.py:337
  64.5 1.0 collective-permute-done.1.pair_ref
  65.5 0.0 copy-done.4
  65.5 0.0 copy-start.5
  65.5 1.1 moved.1
  66.7 1.0 collective-permute-done.2.hop1_ref
  67.6 3.4 %collective-permute-start.3 = (bf16[2,400,384]{2,1,0:T(8,128)(2,1)}, bf16[2,400,384]{2,1,0:T(8,128)(2,1)S(1)}, u32[]{:S(2)}, u32[]{:S(2)}) collective-permute-start(bf16[2,400,384]{2,1,0:T(8,128)(2,1)} %collective-permute-done.2.hop1_ref), channel_id=1, source_target_pairs={{0,2},{1,15},{2,4},{3,1},{4,6},{5,3},{6,8},{7,5},{8,10},{9,7},{10,... | collective-permute-start | bytes 1843208 | tf_op jit(solution)/shard_map/ppermute | solution.py:281
  71.0 12.8 %all-to-all-start.1 = ((bf16[64,8,512]{2,1,0:T(8,128)(2,1)}), bf16[64,8,512]{2,1,0:T(8,128)(2,1)S(1)}, u32[]{:S(2)}, u32[]{:S(2)}) async-start(bf16[64,8,512]{2,1,0:T(8,128)(2,1)} %bitcast.3), calls=%async_computation.1 | async-start | bytes 1048576 | tf_op jit(solution)/shard_map/all_to_all | solution.py:275
  83.8 0.0 collective-permute-done.3.hop2_ref
  83.8 0.0 copy-start.8
  83.8 1.9 %collective-permute-start.4 = (bf16[2,400,384]{2,1,0:T(8,128)(2,1)S(1)}, bf16[2,400,384]{2,1,0:T(8,128)(2,1)S(1)}, u32[]{:S(2)}, u32[]{:S(2)}) collective-permute-start(bf16[2,400,384]{2,1,0:T(8,128)(2,1)S(1)} %collective-permute-done.3.hop2_ref), channel_id=1, source_target_pairs={{0,2},{1,15},{2,4},{3,1},{4,6},{5,3},{6,8},{7,5},{8,10},{9,7},{10,... | collective-permute-start | bytes 1843208 | tf_op jit(solution)/shard_map/ppermute | solution.py:281
  85.8 14.2 %all-to-all-done.1 = bf16[64,8,512]{2,1,0:T(8,128)(2,1)S(1)} async-done(((bf16[64,8,512]{2,1,0:T(8,128)(2,1)}), bf16[64,8,512]{2,1,0:T(8,128)(2,1)S(1)}, u32[]{:S(2)}, u32[]{:S(2)}) %all-to-all-start.1) | async-done | bytes 524320 | tf_op jit(solution)/shard_map/all_to_all | solution.py:275
  100.0 0.0 copy-done.5
  100.0 2.2 %remote.1 = bf16[512,384]{1,0:T(8,128)(2,1)} custom-call(bf16[512,512]{1,0:T(8,128)(2,1)S(1)} %bitcast.8, f32[192,128]{1,0:T(8,128)S(1)} %copy-done.5), custom_call_target="tpu_custom_call" | custom-call | bytes 1015808 | tf_op jit(solution)/shard_map/remote/pallas_call | solution.py:248
  102.2 7.6 %all-to-all-start.2 = ((bf16[64,8,384]{2,1,0:T(8,128)(2,1)}), bf16[64,8,384]{2,1,0:T(8,128)(2,1)S(1)}, u32[]{:S(2)}, u32[]{:S(2)}) async-start(bf16[64,8,384]{2,1,0:T(8,128)(2,1)} %bitcast.5), calls=%async_computation.2 | async-start | bytes 786432 | tf_op jit(solution)/shard_map/all_to_all | solution.py:275
  109.8 0.0 collective-permute-done.4.hop3_ref
  109.8 0.0 copy-start.7
  109.9 0.0 copy-done.8
  109.9 1.9 %collective-permute-start.5 = (bf16[1,400,384]{2,1,0:T(8,128)(2,1)S(1)}, bf16[1,400,384]{2,1,0:T(8,128)(2,1)S(1)}, u32[]{:S(2)}, u32[]{:S(2)}) collective-permute-start(bf16[1,400,384]{2,1,0:T(8,128)(2,1)S(1)} %constant_dynamic-slice_fusion), channel_id=1, source_target_pairs={{0,2},{1,15},{2,4},{3,1},{4,6},{5,3},{6,8},{7,5},{8,10},{9,7},{10,... | collective-permute-start | bytes 921608 | tf_op jit(solution)/shard_map/ppermute | solution.py:281
  111.8 5.9 %partial.1 = (f32[2,400,256]{2,1,0:T(8,128)}, bf16[2,256,1152]{2,1,0:T(8,128)(2,1)}) custom-call(bf16[400,384]{1,0:T(8,128)(2,1)} %get-tuple-element.32.own_ref, bf16[2,400,384]{2,1,0:T(8,128)(2,1)} %collective-permute-done.2.hop1_ref, bf16[2,400,384]{2,1,0:T(8,128)(2,1)} %copy-done.8, bf16[256,6144]{1,0:T(8,128)(2,1)} %w_ref.3, ...), custom_call_target="tpu_custom_call" | custom-call | bytes 9826304 | tf_op jit(solution)/shard_map/partial/pallas_call | solution.py:248
  117.8 0.0 copy-done.7
  117.8 0.0 collective-permute-done.5.hop4_ref
  117.8 0.0 copy-start.9
  117.8 0.7 copy-done.9
  118.5 0.0 copy-start.1
  118.5 0.0 copy-start.2
  118.5 0.0 copy-start.6
  118.5 3.6 %last.1 = (f32[400,256]{1,0:T(8,128)}, f32[400,256]{1,0:T(8,128)}) custom-call(f32[2,400,256]{2,1,0:T(8,128)} %get-tuple-element.35.acc_ref, bf16[2,400,384]{2,1,0:T(8,128)(2,1)} %copy-done.7, bf16[1,400,384]{2,1,0:T(8,128)(2,1)} %copy-done.9, bf16[2,256,1152]{2,1,0:T(8,128)(2,1)} %get-tuple-element.37.w_late_ref), custom_call_target="tpu_custom_call" | custom-call | bytes 3739648 | tf_op jit(solution)/shard_map/last/pallas_call | solution.py:248
  122.1 5.8 %collective-permute-start.6 = (f32[400,256]{1,0:T(8,128)}, f32[400,256]{1,0:T(8,128)S(1)}, u32[]{:S(2)}, u32[]{:S(2)}) collective-permute-start(f32[400,256]{1,0:T(8,128)} %get-tuple-element.39), channel_id=1, source_target_pairs={{0,1},{1,0},{2,3},{3,2},{4,5},{5,4},{6,7},{7,6},{8,9},{9,8},{10,11... | collective-permute-start | bytes 1228808 | tf_op jit(solution)/shard_map/ppermute | solution.py:302
  127.9 1.6 %collective-permute-done.6.pair_ref = f32[400,256]{1,0:T(8,128)S(1)} collective-permute-done((f32[400,256]{1,0:T(8,128)}, f32[400,256]{1,0:T(8,128)S(1)}, u32[]{:S(2)}, u32[]{:S(2)}) %collective-permute-start.6) | collective-permute-done | bytes 409632 | tf_op jit(solution)/shard_map/ppermute | solution.py:302
  129.4 0.0 copy-done.1
  129.4 0.0 copy-done.2
  129.4 0.0 copy-done.6
  129.4 0.0 copy-start.3
  129.5 1.0 copy-done.3
  130.5 2.1 %kept.1 = (bf16[512,256]{1,0:T(8,128)(2,1)S(1)}, bf16[512,256]{1,0:T(8,128)(2,1)S(1)}, bf16[512,256]{1,0:T(8,128)(2,1)S(1)}) custom-call(f32[400,256]{1,0:T(8,128)S(1)} %copy-done.3, f32[400,256]{1,0:T(8,128)S(1)} %collective-permute-done.6.pair_ref, bf16[400,768]{1,0:T(8,128)(2,1)S(1)} %copy-done.2, f32[144,128]{1,0:T(8,128)S(1)} %copy-done.6, ...), custom_call_target="tpu_custom_call" | custom-call | bytes 2555904 | tf_op jit(solution)/shard_map/kept/pallas_call | solution.py:248
  132.6 0.0 all-to-all-done.2
  132.6 1.7 %merge.1 = (bf16[512,256]{1,0:T(8,128)(2,1)}, bf16[512,256]{1,0:T(8,128)(2,1)}, bf16[512,256]{1,0:T(8,128)(2,1)}) custom-call(bf16[512,384]{1,0:T(8,128)(2,1)S(1)} %bitcast.9, s32[512,128]{1,0:T(8,128)S(1)} %copy-done.1, bf16[512,256]{1,0:T(8,128)(2,1)S(1)} %get-tuple-element.42.q_ref, bf16[512,256]{1,0:T(8,128)(2,1)S(1)} %get-tuple-element.43.k_ref, ...), custom_call_target="tpu_custom_call" | custom-call | bytes 2228224 | tf_op jit(solution)/shard_map/merge/pallas_call | solution.py:248
  (1 shorter events, 0.0 us)
Async XLA Ops:
  3.3 54.8 %collective-permute-start = (bf16[256,6144]{1,0:T(8,128)(2,1)}, bf16[256,6144]{1,0:T(8,128)(2,1)}, u32[]{:S(2)}, u32[]{:S(2)}) collective-permute-start(bf16[256,6144]{1,0:T(8,128)(2,1)} %w_ref.3), channel_id=1, source_target_pairs={{0,1},{1,0},{2,3},{3,2},{4,5},{5,4},{6,7},{7,6},{8,9},{9,8},{10,11... | collective-permute-start | bytes 9437192 | tf_op jit(solution)/shard_map/ppermute | solution.py:327
  19.4 38.7 %copy-start = (bf16[256,6144]{1,0:T(8,128)(2,1)S(1)}, bf16[256,6144]{1,0:T(8,128)(2,1)}, u32[]{:S(2)}) copy-start(bf16[256,6144]{1,0:T(8,128)(2,1)} %w_ref.3) | copy-start | bytes 9437188
  19.4 36.6 %all-to-all-start = ((bf16[8,192,384]{2,1,0:T(8,128)(2,1)}), bf16[8,192,384]{2,1,0:T(8,128)(2,1)}, u32[]{:S(2)}, u32[]{:S(2)}) async-start(bf16[8,192,384]{2,1,0:T(8,128)(2,1)} %get-tuple-element.24), calls=%async_computation | async-start | bytes 2359296 | tf_op jit(solution)/shard_map/all_to_all | solution.py:311
  56.0 9.5 %copy-start.4 = (bf16[512,384]{1,0:T(8,128)(2,1)S(1)}, bf16[512,384]{1,0:T(8,128)(2,1)}, u32[]{:S(2)}) copy-start(bf16[512,384]{1,0:T(8,128)(2,1)} %get-tuple-element.29.rows_ref) | copy-start | bytes 1179652
  56.0 11.6 %collective-permute-start.2 = (bf16[2,400,384]{2,1,0:T(8,128)(2,1)}, bf16[2,400,384]{2,1,0:T(8,128)(2,1)}, u32[]{:S(2)}, u32[]{:S(2)}) collective-permute-start(bf16[2,400,384]{2,1,0:T(8,128)(2,1)} %bitcast.10), channel_id=1, source_target_pairs={{0,2},{1,15},{2,4},{3,1},{4,6},{5,3},{6,8},{7,5},{8,10},{9,7},{10,... | collective-permute-start | bytes 1843208 | tf_op jit(solution)/shard_map/ppermute | solution.py:281
  61.6 3.9 %collective-permute-start.1 = (f32[192,256]{1,0:T(8,128)S(1)}, f32[192,256]{1,0:T(8,128)S(1)}, u32[]{:S(2)}, u32[]{:S(2)}) collective-permute-start(f32[192,256]{1,0:T(8,128)S(1)} %get-tuple-element.28), channel_id=1, source_target_pairs={{0,1},{1,0},{2,3},{3,2},{4,5},{5,4},{6,7},{7,6},{8,9},{9,8},{10,11... | collective-permute-start | bytes 589832 | tf_op jit(solution)/shard_map/ppermute | solution.py:337
  65.5 34.4 %copy-start.5 = (f32[192,128]{1,0:T(8,128)S(1)}, f32[192,128]{1,0:T(8,128)}, u32[]{:S(2)}) copy-start(f32[192,128]{1,0:T(8,128)} %get-tuple-element.30.valid_ref) | copy-start | bytes 294916
  67.6 16.2 %collective-permute-start.3 = (bf16[2,400,384]{2,1,0:T(8,128)(2,1)}, bf16[2,400,384]{2,1,0:T(8,128)(2,1)S(1)}, u32[]{:S(2)}, u32[]{:S(2)}) collective-permute-start(bf16[2,400,384]{2,1,0:T(8,128)(2,1)} %collective-permute-done.2.hop1_ref), channel_id=1, source_target_pairs={{0,2},{1,15},{2,4},{3,1},{4,6},{5,3},{6,8},{7,5},{8,10},{9,7},{10,... | collective-permute-start | bytes 1843208 | tf_op jit(solution)/shard_map/ppermute | solution.py:281
  71.0 29.0 %all-to-all-start.1 = ((bf16[64,8,512]{2,1,0:T(8,128)(2,1)}), bf16[64,8,512]{2,1,0:T(8,128)(2,1)S(1)}, u32[]{:S(2)}, u32[]{:S(2)}) async-start(bf16[64,8,512]{2,1,0:T(8,128)(2,1)} %bitcast.3), calls=%async_computation.1 | async-start | bytes 1048576 | tf_op jit(solution)/shard_map/all_to_all | solution.py:275
  83.8 26.1 %copy-start.8 = (bf16[2,400,384]{2,1,0:T(8,128)(2,1)}, bf16[2,400,384]{2,1,0:T(8,128)(2,1)S(1)}, u32[]{:S(2)}) copy-start(bf16[2,400,384]{2,1,0:T(8,128)(2,1)S(1)} %collective-permute-done.3.hop2_ref) | copy-start | bytes 1843204
  83.8 26.0 %collective-permute-start.4 = (bf16[2,400,384]{2,1,0:T(8,128)(2,1)S(1)}, bf16[2,400,384]{2,1,0:T(8,128)(2,1)S(1)}, u32[]{:S(2)}, u32[]{:S(2)}) collective-permute-start(bf16[2,400,384]{2,1,0:T(8,128)(2,1)S(1)} %collective-permute-done.3.hop2_ref), channel_id=1, source_target_pairs={{0,2},{1,15},{2,4},{3,1},{4,6},{5,3},{6,8},{7,5},{8,10},{9,7},{10,... | collective-permute-start | bytes 1843208 | tf_op jit(solution)/shard_map/ppermute | solution.py:281
  102.2 30.4 %all-to-all-start.2 = ((bf16[64,8,384]{2,1,0:T(8,128)(2,1)}), bf16[64,8,384]{2,1,0:T(8,128)(2,1)S(1)}, u32[]{:S(2)}, u32[]{:S(2)}) async-start(bf16[64,8,384]{2,1,0:T(8,128)(2,1)} %bitcast.5), calls=%async_computation.2 | async-start | bytes 786432 | tf_op jit(solution)/shard_map/all_to_all | solution.py:275
  109.8 7.9 %copy-start.7 = (bf16[2,400,384]{2,1,0:T(8,128)(2,1)}, bf16[2,400,384]{2,1,0:T(8,128)(2,1)S(1)}, u32[]{:S(2)}) copy-start(bf16[2,400,384]{2,1,0:T(8,128)(2,1)S(1)} %collective-permute-done.4.hop3_ref) | copy-start | bytes 1843204
  109.9 7.9 %collective-permute-start.5 = (bf16[1,400,384]{2,1,0:T(8,128)(2,1)S(1)}, bf16[1,400,384]{2,1,0:T(8,128)(2,1)S(1)}, u32[]{:S(2)}, u32[]{:S(2)}) collective-permute-start(bf16[1,400,384]{2,1,0:T(8,128)(2,1)S(1)} %constant_dynamic-slice_fusion), channel_id=1, source_target_pairs={{0,2},{1,15},{2,4},{3,1},{4,6},{5,3},{6,8},{7,5},{8,10},{9,7},{10,... | collective-permute-start | bytes 921608 | tf_op jit(solution)/shard_map/ppermute | solution.py:281
  117.8 0.7 copy-start.9
  118.5 10.9 %copy-start.1 = (s32[512,128]{1,0:T(8,128)S(1)}, s32[512,128]{1,0:T(8,128)}, u32[]{:S(2)}) copy-start(s32[512,128]{1,0:T(8,128)} %get-tuple-element.31.pos_ref) | copy-start | bytes 786436
  118.5 10.9 %copy-start.2 = (bf16[400,768]{1,0:T(8,128)(2,1)S(1)}, bf16[400,768]{1,0:T(8,128)(2,1)}, u32[]{:S(2)}) copy-start(bf16[400,768]{1,0:T(8,128)(2,1)} %get-tuple-element.40.rows_ref) | copy-start | bytes 1843204
  118.5 10.9 %copy-start.6 = (f32[144,128]{1,0:T(8,128)S(1)}, f32[144,128]{1,0:T(8,128)}, u32[]{:S(2)}) copy-start(f32[144,128]{1,0:T(8,128)} %get-tuple-element.41.valid_ref) | copy-start | bytes 221188
  122.1 7.3 %collective-permute-start.6 = (f32[400,256]{1,0:T(8,128)}, f32[400,256]{1,0:T(8,128)S(1)}, u32[]{:S(2)}, u32[]{:S(2)}) collective-permute-start(f32[400,256]{1,0:T(8,128)} %get-tuple-element.39), channel_id=1, source_target_pairs={{0,1},{1,0},{2,3},{3,2},{4,5},{5,4},{6,7},{7,6},{8,9},{9,8},{10,11... | collective-permute-start | bytes 1228808 | tf_op jit(solution)/shard_map/ppermute | solution.py:302
  129.4 1.0 copy-start.3

commit v3 on v2

--- a/solution.py
+++ b/solution.py
@@ -110,61 +110,21 @@
     return query_grad.astype(BF16), key_grad.astype(BF16), value_grad.astype(BF16)
 
 
-def block_dot(rows, w_ref, start):
-    cols = rows.shape[1]
-    weight = w_ref[:, pl.ds(pl.multiple_of(start, HD), cols)]
-    return lax.dot_general(rows, weight, NT, preferred_element_type=F32)
-
-
-def partial_kernel(n_mp, own_ref, hop1_ref, hop2_ref, w_ref, w_pair_ref, acc_ref, w_late_ref):
-    feat = own_ref.shape[1]
-    me = lax.axis_index("mp")
-    chips = n_mp // 2
-    chip, core = me // 2, me % 2
-
-    def start(away):
-        return (jnp.where(core == 0, chip - away, chip + away) + chips) % chips * (2 * feat)
-
-    third = pl.multiple_of(start(3), HD)
-    last = pl.multiple_of((me + chips) % n_mp * feat, HD)
-    for side, weight_ref in enumerate((w_ref, w_pair_ref)):
-        acc = block_dot(own_ref[...], weight_ref, me * feat)
-        for away, hop_ref in ((1, hop1_ref), (2, hop2_ref)):
-            for half in range(2):
-                acc = acc + block_dot(hop_ref[half], weight_ref, start(away) + half * feat)
-        acc_ref[side] = acc
-        w_late_ref[side, :, : 2 * feat] = weight_ref[:, pl.ds(third, 2 * feat)]
-        w_late_ref[side, :, 2 * feat :] = weight_ref[:, pl.ds(last, feat)]
-
-
-def last_kernel(acc_ref, hop3_ref, hop4_ref, w_late_ref, mine_ref, pair_ref):
-    feat = hop4_ref.shape[2]
-    for side, out in enumerate((mine_ref, pair_ref)):
-        acc = acc_ref[side]
-        for part, rows in enumerate((hop3_ref[0], hop3_ref[1], hop4_ref[0])):
-            weight = w_late_ref[side, :, part * feat : (part + 1) * feat]
-            acc = acc + lax.dot_general(rows, weight, NT, preferred_element_type=F32)
-        out[...] = acc
-
-
 def spread(n_dp, half, slots):
     shape = (n_dp * OCT, slots)
     return one_hot(iota(shape, 0) == slot_row(iota(shape, 1), n_dp) + half)
 
 
-def chips_kernel(n_mp, og_ref, w_ref, w_pair_ref, mine_ref, pair_ref):
-    chips, _, feat = og_ref.shape
+def moved_kernel(n_dp, own_ref, pair_ref, w_ref, rows_ref, send_ref):
+    chips, slots, feat = own_ref.shape
     core = lax.axis_index("mp") % 2
-    for weight_ref, out in ((w_ref, mine_ref), (w_pair_ref, pair_ref)):
-        acc = block_dot(og_ref[0], weight_ref, core * feat)
-        for chip in range(1, chips):
-            acc = acc + block_dot(og_ref[chip], weight_ref, (2 * chip + core) * feat)
-        out[...] = acc
-
-
-def moved_kernel(n_dp, mine_ref, pair_ref, rows_ref, send_ref):
-    slots = n_dp * CAP
-    grad = (mine_ref[...] + pair_ref[...]).astype(BF16)
+    acc = jnp.zeros((slots, w_ref.shape[0]), F32)
+    for chip in range(chips):
+        for block_ref, parity in ((own_ref, core), (pair_ref, 1 - core)):
+            start = pl.multiple_of((2 * chip + parity) * feat, HD)
+            weight = w_ref[:, pl.ds(start, feat)]
+            acc = acc + lax.dot_general(block_ref[chip], weight, NT, preferred_element_type=F32)
+    grad = acc.astype(BF16)
     send_ref[:, : 3 * HD] = rows_ref[...]
     send_ref[:, 3 * HD :] = (
         jnp.dot(spread(n_dp, 0, slots), grad[:, :HD], preferred_element_type=F32)
@@ -193,31 +153,51 @@
     ).astype(BF16)
 
 
+def project(og_ref, w_ref, acc_ref):
+    blocks, _, cols = og_ref.shape
+
+    @pl.when(pl.program_id(0) == 0)
+    def _():
+        acc_ref[...] = jnp.zeros_like(acc_ref)
+
+    acc = acc_ref[...]
+    for b in range(blocks):
+        acc = acc + lax.dot_general(
+            og_ref[b], w_ref[:, b * cols : (b + 1) * cols], NT, preferred_element_type=F32
+        )
+    acc_ref[...] = acc
+
+
 def local_kernel(
-    n_dp, tok, img, mine_ref, pair_ref, rows_ref, valid_ref, pos_ref, dq_ref, dk_ref, dv_ref
+    n_dp, tok, img, og_ref, w_ref, rows_ref, valid_ref, pos_ref,
+    dq_ref, dk_ref, dv_ref, acc_ref,
 ):
-    slots = n_dp * CAP
-    grad = (mine_ref[...] + pair_ref[...]).astype(BF16)
-    valid = valid_ref[:, 0:1]
-    count = jnp.sum(valid, axis=0, keepdims=True)
-    images = (
-        (slice(0, BIG), None, tok / (img * BIG)),
-        (slice(BIG, KEPT), valid > 0.5, tok / (img * count)),
-    )
-    parts = []
-    for head in range(2):
-        lanes = slice(head * HD, (head + 1) * HD)
-        pieces = []
-        for span, mask, weight in images:
-            q = rows_ref[span, head * HD : (head + 1) * HD]
-            k = rows_ref[span, (2 + head) * HD : (3 + head) * HD]
-            v = rows_ref[span, (4 + head) * HD : (5 + head) * HD]
-            pieces.append(attend(q, k, v, grad[span, lanes], mask, weight))
-        parts.append([jnp.concatenate(p, 0) for p in zip(*pieces)])
-    pos = pos_ref[:, 0:1] - slots
-    hot = one_hot(iota((tok, KEPT), 1) == pos)
-    for name, out in enumerate((dq_ref, dk_ref, dv_ref)):
-        out[...] = pick(hot, jnp.concatenate([parts[0][name], parts[1][name]], 1))
+    project(og_ref, w_ref, acc_ref)
+
+    @pl.when(pl.program_id(0) == pl.num_programs(0) - 1)
+    def _():
+        slots = n_dp * CAP
+        grad = acc_ref[...].astype(BF16)
+        valid = valid_ref[:, 0:1]
+        count = jnp.sum(valid, axis=0, keepdims=True)
+        images = (
+            (slice(0, BIG), None, tok / (img * BIG)),
+            (slice(BIG, KEPT), valid > 0.5, tok / (img * count)),
+        )
+        parts = []
+        for head in range(2):
+            lanes = slice(head * HD, (head + 1) * HD)
+            pieces = []
+            for span, mask, weight in images:
+                q = rows_ref[span, head * HD : (head + 1) * HD]
+                k = rows_ref[span, (2 + head) * HD : (3 + head) * HD]
+                v = rows_ref[span, (4 + head) * HD : (5 + head) * HD]
+                pieces.append(attend(q, k, v, grad[span, lanes], mask, weight))
+            parts.append([jnp.concatenate(p, 0) for p in zip(*pieces)])
+        pos = pos_ref[:, 0:1] - slots
+        hot = one_hot(iota((tok, KEPT), 1) == pos)
+        for out, name in zip((dq_ref, dk_ref, dv_ref), range(3)):
+            out[...] = pick(hot, jnp.concatenate([parts[0][name], parts[1][name]], 1))
 
 
 def merge_kernel(n_dp, back_ref, pos_ref, q_ref, k_ref, v_ref, dq_ref, dk_ref, dv_ref):
@@ -239,22 +219,29 @@
 
 
 def call(kernel, ins, outs, name, vmem=56, flops=0):
-    def whole(x):
-        zeros = (0,) * len(x.shape)
-        return pl.BlockSpec(x.shape, lambda i: zeros)
-
     many = isinstance(outs, tuple)
-    moved = sum(math.prod(x.shape) * x.dtype.itemsize for x in (*ins, *(outs if many else (outs,))))
     return pl.pallas_call(
         kernel,
         out_shape=outs,
         grid=(1,),
         in_specs=[whole(x) for x in ins],
         out_specs=tuple(whole(x) for x in outs) if many else whole(outs),
+        **options(ins, outs if many else (outs,), name, vmem, flops),
+    )(*ins)
+
+
+def whole(x):
+    zeros = (0,) * len(x.shape)
+    return pl.BlockSpec(x.shape, lambda i: zeros)
+
+
+def options(ins, outs, name, vmem, flops):
+    size = sum(math.prod(x.shape) * x.dtype.itemsize for x in (*ins, *outs))
+    return dict(
         compiler_params=pltpu.CompilerParams(vmem_limit_bytes=vmem * MIB),
-        cost_estimate=pl.CostEstimate(flops=flops, bytes_accessed=moved, transcendentals=0),
+        cost_estimate=pl.CostEstimate(flops=flops, bytes_accessed=size, transcendentals=0),
         name=name,
-    )(*ins)
+    )
 
 
 def local(
@@ -266,9 +253,8 @@
     slots = n_dp * CAP
     img = patch_counts.shape[0]
     exch = n_dp * OCT
-    pairs = [[2 * i, 2 * i + 1] for i in range(n_mp // 2)]
     swap = [(i, i ^ 1) for i in range(n_mp)]
-    ring = [(i, (i + (2 if i % 2 == 0 else -2)) % n_mp) for i in range(n_mp)]
+    same_core = [list(range(core, n_mp, 2)) for core in range(2)]
 
     def exchange(rows):
         shaped = rows.reshape(n_dp, OCT, rows.shape[1])
@@ -276,30 +262,6 @@
 
     def after(value, earlier):
         return lax.optimization_barrier((value, earlier))[0]
-
-    def hop(block):
-        return lax.ppermute(block, "mp", ring)
-
-    def both_cores(rows):
-        return lax.all_gather(rows, "mp", axis=0, axis_index_groups=pairs)
-
-    def opposite(block):
-        half = lax.dynamic_slice_in_dim(block, lax.axis_index("mp") % 2, 1, 0)
-        return hop(half)
-
-    def projected(own, hop1, hop2):
-        return call(
-            functools.partial(partial_kernel, n_mp),
-            (own, hop1, hop2, out_weight, pair_weight),
-            (sds((2, own.shape[0], cols), F32), sds((2, cols, 3 * feat), BF16)),
-            "partial",
-        )
-
-    def finished(acc, w_late, hop3, hop4):
-        mine, pair = call(
-            last_kernel, (acc, hop3, hop4, w_late), (sds((hop4.shape[1], cols), F32),) * 2, "last"
-        )
-        return mine, lax.ppermute(pair, "mp", swap)
 
     pos, og_moved = call(
         functools.partial(plan_kernel, n_dp),
@@ -307,10 +269,10 @@
         (sds((8, tok), jnp.int32), sds((n_mp // 2, slots, feat), BF16)),
         "plan",
     )
-    same_core = [list(range(core, n_mp, 2)) for core in range(2)]
     og_chips = lax.all_to_all(
         og_moved, "mp", split_axis=0, concat_axis=0, tiled=True, axis_index_groups=same_core
     )
+    og_pair = lax.ppermute(og_chips, "mp", swap)
     send, og_kept, rows_kept, used, kept_used, pos_col = call(
         functools.partial(pack_kernel, n_dp),
         (pos, out_grad, query_rows, key_rows, value_rows),
@@ -324,27 +286,15 @@
         ),
         "pack",
     )
-    pair_weight = lax.ppermute(after(out_weight, pos), "mp", swap)
-    kept_block = both_cores(og_kept)
-    kept1 = hop(after(kept_block, og_chips))
-    mine, pair = call(
-        functools.partial(chips_kernel, n_mp),
-        (og_chips, out_weight, pair_weight),
-        (sds((slots, cols), F32),) * 2,
-        "chips",
-        24,
-    )
-    pair = lax.ppermute(pair, "mp", swap)
+    kept_all = lax.all_gather(after(og_kept, og_chips), "mp", axis=0)
     moved_send = call(
         functools.partial(moved_kernel, n_dp),
-        (mine, pair, send),
+        (og_chips, og_pair, out_weight, send),
         sds((exch, 4 * HD), BF16),
         "moved",
-        8,
+        24,
     )
     rows_in = exchange(moved_send)
-    kept2 = hop(after(kept1, moved_send))
-    kept3 = hop(kept2)
     back_send = call(
         functools.partial(remote_kernel, n_dp, tok, img),
         (rows_in, used),
@@ -353,21 +303,28 @@
         12,
     )
     back = exchange(back_send)
-    kept4 = opposite(after(kept3, back_send))
-    mine, pair = finished(*projected(og_kept, kept1, kept2), kept3, kept4)
-    kept_grads = call(
+    ins = (kept_all, out_weight, rows_kept, kept_used, pos_col)
+    outs = (sds((tok, cols), BF16),) * 3
+    per_step = 4 if n_mp % 4 == 0 else 1
+    kept_grads = pl.pallas_call(
         functools.partial(local_kernel, n_dp, tok, img),
-        (mine, pair, rows_kept, kept_used, pos_col),
-        (sds((tok, cols), BF16),) * 3,
-        "kept",
-        24,
-    )
+        out_shape=outs,
+        grid=(n_mp // per_step,),
+        in_specs=[
+            pl.BlockSpec((per_step, KEPT, feat), lambda i: (i, 0, 0)),
+            pl.BlockSpec((cols, per_step * feat), lambda i: (0, i)),
+            *(whole(x) for x in ins[2:]),
+        ],
+        out_specs=tuple(whole(x) for x in outs),
+        scratch_shapes=[pltpu.VMEM((KEPT, cols), F32)],
+        **options(ins, outs, "kept", 56, 2 * KEPT * n_mp * feat * cols),
+    )(*ins)
     return call(
         functools.partial(merge_kernel, n_dp),
         (back, pos_col) + kept_grads,
         (sds((tok, cols), BF16),) * 3,
         "merge",
-        12,
+        56,
     )
 
 

time: 135 us -> 136 us (level); the launches traced: 134 us -> 133 us
  starting transfers between devices: 58.9 us -> 27.6 us
  blocking collectives: 3.9 us -> 29.7 us
  between operations: 0.84 us -> 14.1 us
  waiting for transfers between devices: 42.5 us -> 37.3 us
  Pallas kernels: 26.4 us -> 22.9 us
    ppermute x7 -> x1, starting transfers between devices: 33.9 us -> 2.4 us  [local(): og_pair = lax.ppermute(og_chips, 'mp', swap)]
    all_to_all x0 -> x1, blocking collectives: none -> 29.7 us  [exchange(): lax.all_to_all(shaped, 'dp', split_axis=0, concat_axis=0, tiled=True)]
    all_to_all x1, starting transfers between devices: 4.54 us -> 17.5 us  [local(): lax.all_to_all(og_moved, 'mp', split_axis=0, concat_axis=0, tiled=True, a...]
    all_to_all x2 -> x1, starting transfers between devices: 20.5 us -> 7.72 us  [exchange(): lax.all_to_all(shaped, 'dp', split_axis=0, concat_axis=0, tiled=True)]
    pallas_call x9 -> x5, Pallas kernels: 26.4 us -> 14.5 us  [call(): pl.pallas_call(kernel, out_shape=outs, grid=(1,), in_specs=[whole(x) for...]
    pallas_call x0 -> x1, Pallas kernels: none -> 8.36 us  [local(): pl.pallas_call(functools.partial(local_kernel, n_dp, tok, img), out_shape...]
    all_to_all x2 -> x1, waiting for transfers between devices: 14.2 us -> 5.98 us  [exchange(): lax.all_to_all(shaped, 'dp', split_axis=0, concat_axis=0, tiled=True)]
    all_to_all x1, waiting for transfers between devices: 24.7 us -> 28.6 us  [local(): lax.all_to_all(og_moved, 'mp', split_axis=0, concat_axis=0, tiled=True, a...]
  transfers between devices with their start and end apart: 10 -> 4, of which waited for: 5 -> 3; matrix products, arithmetic and copies ran while one was open for 0% -> 0% of each run, Pallas kernels for 16% -> 13%
where the time goes in v3:
time: 136 us; the launch traced here: 133 us
  waiting for transfers between devices  37.3 us (27%)
  blocking collectives  29.7 us (22%)
  starting transfers between devices  27.6 us (20%)
  Pallas kernels  22.9 us (17%)
  between operations  14.1 us (10%)
  local copies, waits for them, and re-layouts  1.74 us (1%)
    all_to_all x1, blocking collectives, exchange(): lax.all_to_all(shaped, 'dp', split_axis=0, concat_axis=0, tiled=True)  29.7 us
    all_to_all x1, waiting for transfers between devices, local(): lax.all_to_all(og_moved, 'mp', split_axis=0, concat_axis=0, tiled=True, a...  28.6 us
    all_to_all x1, starting transfers between devices, local(): lax.all_to_all(og_moved, 'mp', split_axis=0, concat_axis=0, tiled=True, a...  17.5 us
    pallas_call x5, Pallas kernels, call(): pl.pallas_call(kernel, out_shape=outs, grid=(1,), in_specs=[whole(x) for...  14.5 us
    pallas_call x1, Pallas kernels, local(): pl.pallas_call(functools.partial(local_kernel, n_dp, tok, img), out_shape...  8.36 us
    all_to_all x1, starting transfers between devices, exchange(): lax.all_to_all(shaped, 'dp', split_axis=0, concat_axis=0, tiled=True)  7.72 us
    all_to_all x1, waiting for transfers between devices, exchange(): lax.all_to_all(shaped, 'dp', split_axis=0, concat_axis=0, tiled=True)  5.98 us
  transfers between devices with their start and end apart: 4, of which 3 were waited for; matrix products, arithmetic and copies ran while one was open for 0% of the time, Pallas kernels for 13%

profile of v3, /device:TPU:1, one launch (start us, length us, event | category | flops | bytes accessed | tf_op | source)
XLA Modules:
  0.0 133.4 jit_solution(12733670496884576772)
XLA Ops:
  7.2 2.7 %plan.1 = (s32[8,512]{1,0:T(8,128)}, bf16[8,192,384]{2,1,0:T(8,128)(2,1)}) custom-call(s32[1,512]{1,0:T(1,128)} %bitcast.12, s32[1,512]{1,0:T(1,128)} %bitcast.13, s32[1,3]{1,0:T(1,128)} %bitcast.14, bf16[512,384]{1,0:T(8,128)(2,1)} %og_ref.3), custom_call_target="tpu_custom_call" | custom-call | bytes 1593356 | tf_op jit(solution)/shard_map/plan/pallas_call | solution.py:223
  9.9 0.0 copy-start
  9.9 17.5 %all-to-all-start = ((bf16[8,192,384]{2,1,0:T(8,128)(2,1)}), bf16[8,192,384]{2,1,0:T(8,128)(2,1)}, u32[]{:S(2)}, u32[]{:S(2)}) async-start(bf16[8,192,384]{2,1,0:T(8,128)(2,1)} %get-tuple-element.15), calls=%async_computation | async-start | bytes 2359296 | tf_op jit(solution)/shard_map/all_to_all | solution.py:272
  27.4 0.0 all-gather.3.cloned.1.call-start
  27.4 3.5 %pack.1 = (bf16[512,384]{1,0:T(8,128)(2,1)}, bf16[400,384]{1,0:T(8,128)(2,1)}, bf16[400,768]{1,0:T(8,128)(2,1)}, f32[192,128]{1,0:T(8,128)}, f32[144,128]{1,0:T(8,128)}, /*index=5*/s32[512,128]{1,0:T(8,128)}) custom-call(s32[8,512]{1,0:T(8,128)} %get-tuple-element.16.pos_ref, bf16[512,384]{1,0:T(8,128)(2,1)} %og_ref.3, bf16[512,256]{1,0:T(8,128)(2,1)} %q_ref.1, ...), custom_call_target="tpu_custom_call" | custom-call | bytes 2945024 | tf_op jit(solution)/shard_map/pack/pallas_call | solution.py:223
  30.9 28.6 %all-to-all-done.own_ref = bf16[8,192,384]{2,1,0:T(8,128)(2,1)} async-done(((bf16[8,192,384]{2,1,0:T(8,128)(2,1)}), bf16[8,192,384]{2,1,0:T(8,128)(2,1)}, u32[]{:S(2)}, u32[]{:S(2)}) %all-to-all-start) | async-done | bytes 1179680 | tf_op jit(solution)/shard_map/all_to_all | solution.py:272
  59.5 0.0 all-gather.3.cloned.1.call-update
  59.5 2.4 %collective-permute-start = (bf16[8,192,384]{2,1,0:T(8,128)(2,1)}, bf16[8,192,384]{2,1,0:T(8,128)(2,1)S(1)}, u32[]{:S(2)}, u32[]{:S(2)}) collective-permute-start(bf16[8,192,384]{2,1,0:T(8,128)(2,1)} %all-to-all-done.own_ref), channel_id=1, source_target_pairs={{0,1},{1,0},{2,3},{3,2},{4,5},{5,4},{6,7},{7,6},{8,9},{9,8},{10,11... | collective-permute-start | bytes 3538952 | tf_op jit(solution)/shard_map/ppermute | solution.py:275
  61.9 2.7 %collective-permute-done.pair_ref = bf16[8,192,384]{2,1,0:T(8,128)(2,1)S(1)} collective-permute-done((bf16[8,192,384]{2,1,0:T(8,128)(2,1)}, bf16[8,192,384]{2,1,0:T(8,128)(2,1)S(1)}, u32[]{:S(2)}, u32[]{:S(2)}) %collective-permute-start) | collective-permute-done | bytes 1179680 | tf_op jit(solution)/shard_map/ppermute | solution.py:275
  64.6 0.0 copy-done
  64.6 0.0 copy-start.1
  64.6 1.0 copy-done.1
  65.6 0.0 copy-start.2
  65.6 3.1 %moved.1 = bf16[512,512]{1,0:T(8,128)(2,1)S(1)} custom-call(bf16[8,192,384]{2,1,0:T(8,128)(2,1)} %all-to-all-done.own_ref, bf16[8,192,384]{2,1,0:T(8,128)(2,1)S(1)} %collective-permute-done.pair_ref, bf16[256,6144]{1,0:T(8,128)(2,1)S(1)} %copy-done, bf16[512,384]{1,0:T(8,128)(2,1)S(1)} %copy-done.1), custom_call_target="tpu_custom_call" | custom-call | bytes 6422528 | tf_op jit(solution)/shard_map/moved/pallas_call | solution.py:223
  68.7 29.7 %all_to_all.15 = bf16[64,8,512]{2,1,0:T(8,128)(2,1)S(1)} all-to-all(bf16[64,8,512]{2,1,0:T(8,128)(2,1)S(1)} %bitcast.8), channel_id=1, replica_groups=mesh['dp'=64,'mp'=16] {'dp'}, dimensions={0} | all-to-all | bytes 1048576 | tf_op jit(solution)/shard_map/all_to_all | solution.py:261
  98.4 0.0 copy-done.2
  98.4 2.2 %remote.1 = bf16[512,384]{1,0:T(8,128)(2,1)} custom-call(bf16[512,512]{1,0:T(8,128)(2,1)S(1)} %bitcast.9, f32[192,128]{1,0:T(8,128)S(1)} %copy-done.2), custom_call_target="tpu_custom_call" | custom-call | bytes 1015808 | tf_op jit(solution)/shard_map/remote/pallas_call | solution.py:223
  100.7 7.7 %all-to-all-start.2 = ((bf16[64,8,384]{2,1,0:T(8,128)(2,1)}), bf16[64,8,384]{2,1,0:T(8,128)(2,1)S(1)}, u32[]{:S(2)}, u32[]{:S(2)}) async-start(bf16[64,8,384]{2,1,0:T(8,128)(2,1)} %bitcast.5), calls=%async_computation.2 | async-start | bytes 786432 | tf_op jit(solution)/shard_map/all_to_all | solution.py:261
  108.4 0.0 all-gather.3.cloned.1.call-done
  108.4 8.4 %kept.1 = (bf16[512,256]{1,0:T(8,128)(2,1)}, bf16[512,256]{1,0:T(8,128)(2,1)}, bf16[512,256]{1,0:T(8,128)(2,1)}) custom-call(bf16[16,400,384]{2,1,0:T(8,128)(2,1)} %bitcast.10, bf16[256,6144]{1,0:T(8,128)(2,1)} %w_ref.3, bf16[400,768]{1,0:T(8,128)(2,1)} %get-tuple-element.22.rows_ref, f32[144,128]{1,0:T(8,128)} %get-tuple-element.23.valid_ref, ...), custom_call_target="tpu_custom_call" | custom-call | flops 1258291200 | bytes 9797632 | tf_op jit(solution)/shard_map/kept/pallas_call | solution.py:309
  116.8 6.0 %all-to-all-done.2 = bf16[64,8,384]{2,1,0:T(8,128)(2,1)S(1)} async-done(((bf16[64,8,384]{2,1,0:T(8,128)(2,1)}), bf16[64,8,384]{2,1,0:T(8,128)(2,1)S(1)}, u32[]{:S(2)}, u32[]{:S(2)}) %all-to-all-start.2) | async-done | bytes 393248 | tf_op jit(solution)/shard_map/all_to_all | solution.py:261
  122.8 0.0 copy-start.3
  122.8 0.7 copy-done.3
  123.5 3.0 %merge.1 = (bf16[512,256]{1,0:T(8,128)(2,1)}, bf16[512,256]{1,0:T(8,128)(2,1)}, bf16[512,256]{1,0:T(8,128)(2,1)}) custom-call(bf16[512,384]{1,0:T(8,128)(2,1)} %bitcast.11, s32[512,128]{1,0:T(8,128)} %get-tuple-element.19.pos_ref, bf16[512,256]{1,0:T(8,128)(2,1)} %get-tuple-element.24.q_ref, bf16[512,256]{1,0:T(8,128)(2,1)} %get-tuple-element.25.k_ref, ...), custom_call_target="tpu_custom_call" | custom-call | bytes 2228224 | tf_op jit(solution)/shard_map/merge/pallas_call | solution.py:223
Async XLA Ops:
  9.9 54.7 %copy-start = (bf16[256,6144]{1,0:T(8,128)(2,1)S(1)}, bf16[256,6144]{1,0:T(8,128)(2,1)}, u32[]{:S(2)}) copy-start(bf16[256,6144]{1,0:T(8,128)(2,1)} %w_ref.3) | copy-start | bytes 9437188
  9.9 49.6 %all-to-all-start = ((bf16[8,192,384]{2,1,0:T(8,128)(2,1)}), bf16[8,192,384]{2,1,0:T(8,128)(2,1)}, u32[]{:S(2)}, u32[]{:S(2)}) async-start(bf16[8,192,384]{2,1,0:T(8,128)(2,1)} %get-tuple-element.15), calls=%async_computation | async-start | bytes 2359296 | tf_op jit(solution)/shard_map/all_to_all | solution.py:272
  27.4 81.0 %all-gather.3.cloned.1.call-start = ((), (), s32[]{:S(2)}) async-start(), calls=%async_computation.3 | async-start | bytes 5222400 | tf_op jit(solution)/shard_map/all_gather | solution.py:289
  59.5 5.1 %collective-permute-start = (bf16[8,192,384]{2,1,0:T(8,128)(2,1)}, bf16[8,192,384]{2,1,0:T(8,128)(2,1)S(1)}, u32[]{:S(2)}, u32[]{:S(2)}) collective-permute-start(bf16[8,192,384]{2,1,0:T(8,128)(2,1)} %all-to-all-done.own_ref), channel_id=1, source_target_pairs={{0,1},{1,0},{2,3},{3,2},{4,5},{5,4},{6,7},{7,6},{8,9},{9,8},{10,11... | collective-permute-start | bytes 3538952 | tf_op jit(solution)/shard_map/ppermute | solution.py:275
  64.6 1.0 copy-start.1
  65.6 32.8 %copy-start.2 = (f32[192,128]{1,0:T(8,128)S(1)}, f32[192,128]{1,0:T(8,128)}, u32[]{:S(2)}) copy-start(f32[192,128]{1,0:T(8,128)} %get-tuple-element.18.valid_ref) | copy-start | bytes 294916
  100.7 22.1 %all-to-all-start.2 = ((bf16[64,8,384]{2,1,0:T(8,128)(2,1)}), bf16[64,8,384]{2,1,0:T(8,128)(2,1)S(1)}, u32[]{:S(2)}, u32[]{:S(2)}) async-start(bf16[64,8,384]{2,1,0:T(8,128)(2,1)} %bitcast.5), calls=%async_computation.2 | async-start | bytes 786432 | tf_op jit(solution)/shard_map/all_to_all | solution.py:261
  122.8 0.7 copy-start.3
Sparse Core Ops, SparseCore 0:
  59.7 46.6 all-gather.2

commit v4 on v3

--- a/solution.py
+++ b/solution.py
@@ -34,8 +34,17 @@
     return jnp.dot(hot, rows, preferred_element_type=F32).astype(BF16)
 
 
-def slot_row(slot, n_dp):
-    return OCT * (slot % n_dp) + 2 * (slot // n_dp)
+def to_octets(out_ref, wide_ref, first, blocks):
+    slots = blocks[0].shape[0]
+    for i, block in enumerate(blocks):
+        wide_ref[pl.ds(first + i, slots, stride=OCT), :] = block.astype(F32)
+    out_ref[...] = wide_ref[...].astype(BF16)
+
+
+def from_octets(in_ref, wide_ref, count):
+    wide_ref[...] = in_ref[...].astype(F32)
+    slots = in_ref.shape[0] // OCT
+    return [wide_ref[pl.ds(i, slots, stride=OCT), :].astype(BF16) for i in range(count)]
 
 
 def plan_kernel(n_dp, dest_ref, ids_ref, counts_ref, og_ref, pos_ref, og_moved_ref):
@@ -54,9 +63,8 @@
     member = row == group
     before = one_hot(iota((tok, tok), 0) < iota((tok, tok), 1))
     rank = jnp.dot(one_hot(member), before, preferred_element_type=F32)
-    start = jnp.where(row < n_dp, row, jnp.where(row == n_dp, slots, slots + BIG))
-    step = jnp.where(row < n_dp, float(n_dp), 1.0)
-    place = jnp.where(member, start.astype(F32) + step * rank, 0.0)
+    start = jnp.where(row < n_dp, CAP * row, jnp.where(row == n_dp, slots, slots + BIG))
+    place = jnp.where(member, start.astype(F32) + rank, 0.0)
     pos = jnp.sum(place, axis=0, keepdims=True).astype(jnp.int32)
     pos_ref[...] = jnp.broadcast_to(pos, pos_ref.shape)
     rows = pick(one_hot(iota((slots, tok), 0) == pos), og_ref[...])
@@ -66,25 +74,21 @@
 
 def pack_kernel(
     n_dp, pos_ref, og_ref, q_ref, k_ref, v_ref,
-    send_ref, og_kept_ref, rows_kept_ref, used_ref, kept_used_ref, pos_col_ref,
+    send_ref, og_kept_ref, rows_kept_ref, used_ref, kept_used_ref, pos_col_ref, wide_ref,
 ):
     tok = og_ref.shape[0]
     slots = n_dp * CAP
     pos = pos_ref[0:1, :]
     q, k, v = q_ref[...], k_ref[...], v_ref[...]
-    first = jnp.where(pos < slots, slot_row(pos, n_dp), -OCT)
-    row = iota((n_dp * OCT, tok), 0)
-    left = jnp.concatenate([q, k[:, :HD]], 1)
-    right = jnp.concatenate([k[:, HD:], v], 1)
-    send_ref[...] = (
-        jnp.dot(one_hot(row == first), left, preferred_element_type=F32)
-        + jnp.dot(one_hot(row == first + 1), right, preferred_element_type=F32)
-    ).astype(BF16)
+    rows = jnp.concatenate([q, k, v], 1)
+    slot_hot = one_hot(iota((slots, tok), 0) == pos)
+    sent = jnp.dot(slot_hot, rows, preferred_element_type=F32)
+    wide_ref[...] = jnp.zeros_like(wide_ref)
+    to_octets(send_ref, wide_ref, 0, [sent[:, i * HD : (i + 1) * HD] for i in range(6)])
     kept_hot = one_hot(iota((KEPT, tok), 0) + slots == pos)
     og_kept_ref[...] = pick(kept_hot, og_ref[...])
-    rows_kept_ref[...] = pick(kept_hot, jnp.concatenate([q, k, v], 1))
+    rows_kept_ref[...] = pick(kept_hot, rows)
     ones = jnp.ones((tok, HD), BF16)
-    slot_hot = one_hot(iota((slots, tok), 0) == pos)
     used_ref[...] = jnp.dot(slot_hot, ones, preferred_element_type=F32)
     kept_used_ref[...] = jnp.dot(kept_hot[BIG:], ones, preferred_element_type=F32)
     wide = jnp.broadcast_to(pos.astype(F32), (HD, tok))
@@ -110,12 +114,7 @@
     return query_grad.astype(BF16), key_grad.astype(BF16), value_grad.astype(BF16)
 
 
-def spread(n_dp, half, slots):
-    shape = (n_dp * OCT, slots)
-    return one_hot(iota(shape, 0) == slot_row(iota(shape, 1), n_dp) + half)
-
-
-def moved_kernel(n_dp, own_ref, pair_ref, w_ref, rows_ref, send_ref):
+def moved_kernel(own_ref, pair_ref, w_ref, rows_ref, send_ref, wide_ref):
     chips, slots, feat = own_ref.shape
     core = lax.axis_index("mp") % 2
     acc = jnp.zeros((slots, w_ref.shape[0]), F32)
@@ -125,32 +124,20 @@
             weight = w_ref[:, pl.ds(start, feat)]
             acc = acc + lax.dot_general(block_ref[chip], weight, NT, preferred_element_type=F32)
     grad = acc.astype(BF16)
-    send_ref[:, : 3 * HD] = rows_ref[...]
-    send_ref[:, 3 * HD :] = (
-        jnp.dot(spread(n_dp, 0, slots), grad[:, :HD], preferred_element_type=F32)
-        + jnp.dot(spread(n_dp, 1, slots), grad[:, HD:], preferred_element_type=F32)
-    ).astype(BF16)
-
-
-def remote_kernel(n_dp, tok, img, rows_ref, valid_ref, send_ref):
-    slots = n_dp * CAP
-    shape = (slots, n_dp * OCT)
-    first = slot_row(iota(shape, 0), n_dp)
-    hot0 = one_hot(iota(shape, 1) == first)
-    hot1 = one_hot(iota(shape, 1) == first + 1)
-    a, b = pick(hot0, rows_ref[...]), pick(hot1, rows_ref[...])
+    wide_ref[...] = rows_ref[...].astype(F32)
+    to_octets(send_ref, wide_ref, 6, [grad[:, :HD], grad[:, HD:]])
+
+
+def remote_kernel(tok, img, rows_ref, valid_ref, send_ref, wide_ref):
+    q0, q1, k0, k1, v0, v1, g0, g1 = from_octets(rows_ref, wide_ref, OCT)
     valid = valid_ref[:, 0:1]
     count = jnp.sum(valid, axis=0, keepdims=True)
     weight = tok / (img * count)
     mask = valid > 0.5
-    q0, q1, k0, g0 = (a[:, i * HD : (i + 1) * HD] for i in range(4))
-    k1, v0, v1, g1 = (b[:, i * HD : (i + 1) * HD] for i in range(4))
     dq0, dk0, dv0 = attend(q0, k0, v0, g0, mask, weight)
     dq1, dk1, dv1 = attend(q1, k1, v1, g1, mask, weight)
-    send_ref[...] = (
-        jnp.dot(spread(n_dp, 0, slots), jnp.concatenate([dq0, dq1, dk0], 1), preferred_element_type=F32)
-        + jnp.dot(spread(n_dp, 1, slots), jnp.concatenate([dk1, dv0, dv1], 1), preferred_element_type=F32)
-    ).astype(BF16)
+    wide_ref[...] = jnp.zeros_like(wide_ref)
+    to_octets(send_ref, wide_ref, 0, [dq0, dq1, dk0, dk1, dv0, dv1])
 
 
 def project(og_ref, w_ref, acc_ref):
@@ -200,25 +187,21 @@
             out[...] = pick(hot, jnp.concatenate([parts[0][name], parts[1][name]], 1))
 
 
-def merge_kernel(n_dp, back_ref, pos_ref, q_ref, k_ref, v_ref, dq_ref, dk_ref, dv_ref):
+def merge_kernel(back_ref, pos_ref, q_ref, k_ref, v_ref, dq_ref, dk_ref, dv_ref, wide_ref):
     tok = q_ref.shape[0]
-    slots = n_dp * CAP
-    pos = pos_ref[:, 0:1]
-    first = jnp.where(pos < slots, slot_row(pos, n_dp), -OCT)
-    col = iota((tok, n_dp * OCT), 1)
-    back = back_ref[...]
-    a = pick(one_hot(col == first), back)
-    b = pick(one_hot(col == first + 1), back)
-    dq_ref[...] = q_ref[...] + a[:, : 2 * HD]
-    dk_ref[...] = k_ref[...] + jnp.concatenate([a[:, 2 * HD :], b[:, :HD]], 1)
-    dv_ref[...] = v_ref[...] + b[:, HD:]
+    slots = back_ref.shape[0] // OCT
+    hot = one_hot(iota((tok, slots), 1) == pos_ref[:, 0:1])
+    back = from_octets(back_ref, wide_ref, 6)
+    for i, (kept_ref, out) in enumerate(((q_ref, dq_ref), (k_ref, dk_ref), (v_ref, dv_ref))):
+        rows = jnp.concatenate(back[2 * i : 2 * i + 2], 1)
+        out[...] = kept_ref[...] + pick(hot, rows)
 
 
 def sds(shape, dtype):
     return jax.ShapeDtypeStruct(shape, dtype)
 
 
-def call(kernel, ins, outs, name, vmem=56, flops=0):
+def call(kernel, ins, outs, name, vmem=56, flops=0, scratch=()):
     many = isinstance(outs, tuple)
     return pl.pallas_call(
         kernel,
@@ -226,6 +209,7 @@
         grid=(1,),
         in_specs=[whole(x) for x in ins],
         out_specs=tuple(whole(x) for x in outs) if many else whole(outs),
+        scratch_shapes=scratch,
         **options(ins, outs if many else (outs,), name, vmem, flops),
     )(*ins)
 
@@ -252,12 +236,13 @@
     n_dp, n_mp = lax.axis_size("dp"), lax.axis_size("mp")
     slots = n_dp * CAP
     img = patch_counts.shape[0]
-    exch = n_dp * OCT
+    exch = slots * OCT
+    wide = [pltpu.VMEM((exch, HD), F32)]
     swap = [(i, i ^ 1) for i in range(n_mp)]
     same_core = [list(range(core, n_mp, 2)) for core in range(2)]
 
     def exchange(rows):
-        shaped = rows.reshape(n_dp, OCT, rows.shape[1])
+        shaped = rows.reshape(n_dp, CAP * OCT, HD)
         return lax.all_to_all(shaped, "dp", split_axis=0, concat_axis=0, tiled=True).reshape(rows.shape)
 
     def after(value, earlier):
@@ -277,7 +262,7 @@
         functools.partial(pack_kernel, n_dp),
         (pos, out_grad, query_rows, key_rows, value_rows),
         (
-            sds((exch, 3 * HD), BF16),
+            sds((exch, HD), BF16),
             sds((KEPT, feat), BF16),
             sds((KEPT, 3 * cols), BF16),
             sds((slots, HD), F32),
@@ -285,22 +270,25 @@
             sds((tok, HD), jnp.int32),
         ),
         "pack",
+        scratch=wide,
     )
     kept_all = lax.all_gather(after(og_kept, og_chips), "mp", axis=0)
     moved_send = call(
-        functools.partial(moved_kernel, n_dp),
+        moved_kernel,
         (og_chips, og_pair, out_weight, send),
-        sds((exch, 4 * HD), BF16),
+        sds((exch, HD), BF16),
         "moved",
         24,
+        scratch=wide,
     )
     rows_in = exchange(moved_send)
     back_send = call(
-        functools.partial(remote_kernel, n_dp, tok, img),
+        functools.partial(remote_kernel, tok, img),
         (rows_in, used),
-        sds((exch, 3 * HD), BF16),
+        sds((exch, HD), BF16),
         "remote",
         12,
+        scratch=wide,
     )
     back = exchange(back_send)
     ins = (kept_all, out_weight, rows_kept, kept_used, pos_col)
@@ -320,11 +308,12 @@
         **options(ins, outs, "kept", 56, 2 * KEPT * n_mp * feat * cols),
     )(*ins)
     return call(
-        functools.partial(merge_kernel, n_dp),
+        merge_kernel,
         (back, pos_col) + kept_grads,
         (sds((tok, cols), BF16),) * 3,
         "merge",
         56,
+        scratch=wide,
     )
 
 

time: 136 us -> 131 us (0.963)
  blocking collectives: 29.7 us -> 27.9 us
  Pallas kernels: 22.9 us -> 21.1 us
    all_to_all x1, waiting for transfers between devices: 5.98 us -> 4.04 us  [exchange(): lax.all_to_all(shaped, 'dp', split_axis=0, concat_axis=0, tiled=True)]
    all_gather x1, waiting for transfers between devices: 0.02 us -> 1.94 us  [local(): kept_all = lax.all_gather(after(og_kept, og_chips), 'mp', axis=0)]
    all_to_all x1, blocking collectives: 29.7 us -> 27.9 us  [exchange(): lax.all_to_all(shaped, 'dp', split_axis=0, concat_axis=0, tiled=True)]
    pallas_call x5, Pallas kernels: 14.5 us -> 12.8 us  [call(): pl.pallas_call(kernel, out_shape=outs, grid=(1,), in_specs=[whole(x) for...]
  transfers between devices with their start and end apart: 4 -> 4, of which waited for: 3 -> 4; matrix products, arithmetic and copies ran while one was open for 0% -> 0% of each run, Pallas kernels for 13% -> 12%
where the time goes in v4:
time: 131 us; the launch traced here: 129 us
  waiting for transfers between devices  37.5 us (29%)
  blocking collectives  27.9 us (21%)
  starting transfers between devices  26.5 us (20%)
  Pallas kernels  21.1 us (16%)
  between operations  14.1 us (11%)
  local copies, waits for them, and re-layouts  1.74 us (1%)
    all_to_all x1, waiting for transfers between devices, local(): lax.all_to_all(og_moved, 'mp', split_axis=0, concat_axis=0, tiled=True, a...  28.9 us
    all_to_all x1, blocking collectives, exchange(): lax.all_to_all(shaped, 'dp', split_axis=0, concat_axis=0, tiled=True)  27.9 us
    all_to_all x1, starting transfers between devices, local(): lax.all_to_all(og_moved, 'mp', split_axis=0, concat_axis=0, tiled=True, a...  17.5 us
    pallas_call x5, Pallas kernels, call(): pl.pallas_call(kernel, out_shape=outs, grid=(1,), in_specs=[whole(x) for...  12.8 us
    pallas_call x1, Pallas kernels, local(): pl.pallas_call(functools.partial(local_kernel, n_dp, tok, img), out_shape...  8.35 us
    all_to_all x1, starting transfers between devices, exchange(): lax.all_to_all(shaped, 'dp', split_axis=0, concat_axis=0, tiled=True)  6.54 us
    all_to_all x1, waiting for transfers between devices, exchange(): lax.all_to_all(shaped, 'dp', split_axis=0, concat_axis=0, tiled=True)  4.04 us
    ppermute x1, waiting for transfers between devices, local(): og_pair = lax.ppermute(og_chips, 'mp', swap)  2.66 us
  transfers between devices with their start and end apart: 4, of which 4 were waited for; matrix products, arithmetic and copies ran while one was open for 0% of the time, Pallas kernels for 12%

profile of v4, /device:TPU:1, one launch (start us, length us, event | category | flops | bytes accessed | tf_op | source)
XLA Modules:
  0.0 128.9 jit_solution(8742240049716712604)
XLA Ops:
  7.2 2.7 %plan.1 = (s32[8,512]{1,0:T(8,128)}, bf16[8,192,384]{2,1,0:T(8,128)(2,1)}) custom-call(s32[1,512]{1,0:T(1,128)} %bitcast.12, s32[1,512]{1,0:T(1,128)} %bitcast.13, s32[1,3]{1,0:T(1,128)} %bitcast.14, bf16[512,384]{1,0:T(8,128)(2,1)} %og_ref.3), custom_call_target="tpu_custom_call" | custom-call | bytes 1593356 | tf_op jit(solution)/shard_map/plan/pallas_call | solution.py:206
  9.9 0.0 copy-start
  9.9 17.5 %all-to-all-start = ((bf16[8,192,384]{2,1,0:T(8,128)(2,1)}), bf16[8,192,384]{2,1,0:T(8,128)(2,1)}, u32[]{:S(2)}, u32[]{:S(2)}) async-start(bf16[8,192,384]{2,1,0:T(8,128)(2,1)} %get-tuple-element.15), calls=%async_computation | async-start | bytes 2359296 | tf_op jit(solution)/shard_map/all_to_all | solution.py:257
  27.4 0.0 all-gather.3.cloned.1.call-start
  27.4 3.2 %pack.1 = (bf16[1536,128]{1,0:T(8,128)(2,1)}, bf16[400,384]{1,0:T(8,128)(2,1)}, bf16[400,768]{1,0:T(8,128)(2,1)}, f32[192,128]{1,0:T(8,128)}, f32[144,128]{1,0:T(8,128)}, /*index=5*/s32[512,128]{1,0:T(8,128)}) custom-call(s32[8,512]{1,0:T(8,128)} %get-tuple-element.16.pos_ref, bf16[512,384]{1,0:T(8,128)(2,1)} %og_ref.3, bf16[512,256]{1,0:T(8,128)(2,1)} %q_ref.1, ...), custom_call_target="tpu_custom_call" | custom-call | bytes 2945024 | tf_op jit(solution)/shard_map/pack/pallas_call | solution.py:206
  30.6 28.9 %all-to-all-done.own_ref = bf16[8,192,384]{2,1,0:T(8,128)(2,1)} async-done(((bf16[8,192,384]{2,1,0:T(8,128)(2,1)}), bf16[8,192,384]{2,1,0:T(8,128)(2,1)}, u32[]{:S(2)}, u32[]{:S(2)}) %all-to-all-start) | async-done | bytes 1179680 | tf_op jit(solution)/shard_map/all_to_all | solution.py:257
  59.5 0.0 all-gather.3.cloned.1.call-update
  59.5 2.4 %collective-permute-start = (bf16[8,192,384]{2,1,0:T(8,128)(2,1)}, bf16[8,192,384]{2,1,0:T(8,128)(2,1)S(1)}, u32[]{:S(2)}, u32[]{:S(2)}) collective-permute-start(bf16[8,192,384]{2,1,0:T(8,128)(2,1)} %all-to-all-done.own_ref), channel_id=1, source_target_pairs={{0,1},{1,0},{2,3},{3,2},{4,5},{5,4},{6,7},{7,6},{8,9},{9,8},{10,11... | collective-permute-start | bytes 3538952 | tf_op jit(solution)/shard_map/ppermute | solution.py:260
  61.9 2.7 %collective-permute-done.pair_ref = bf16[8,192,384]{2,1,0:T(8,128)(2,1)S(1)} collective-permute-done((bf16[8,192,384]{2,1,0:T(8,128)(2,1)}, bf16[8,192,384]{2,1,0:T(8,128)(2,1)S(1)}, u32[]{:S(2)}, u32[]{:S(2)}) %collective-permute-start) | collective-permute-done | bytes 1179680 | tf_op jit(solution)/shard_map/ppermute | solution.py:260
  64.6 0.0 copy-done
  64.6 0.0 copy-start.1
  64.6 1.0 copy-done.1
  65.6 0.0 copy-start.2
  65.6 2.6 %moved.1 = bf16[1536,128]{1,0:T(8,128)(2,1)S(1)} custom-call(bf16[8,192,384]{2,1,0:T(8,128)(2,1)} %all-to-all-done.own_ref, bf16[8,192,384]{2,1,0:T(8,128)(2,1)S(1)} %collective-permute-done.pair_ref, bf16[256,6144]{1,0:T(8,128)(2,1)S(1)} %copy-done, bf16[1536,128]{1,0:T(8,128)(2,1)S(1)} %copy-done.1), custom_call_target="tpu_custom_call" | custom-call | bytes 6291456 | tf_op jit(solution)/shard_map/moved/pallas_call | solution.py:206
  68.2 27.9 %all_to_all.15 = bf16[64,24,128]{2,1,0:T(8,128)(2,1)S(1)} all-to-all(bf16[64,24,128]{2,1,0:T(8,128)(2,1)S(1)} %bitcast.8), channel_id=1, replica_groups=mesh['dp'=64,'mp'=16] {'dp'}, dimensions={0} | all-to-all | bytes 786432 | tf_op jit(solution)/shard_map/all_to_all | solution.py:246
  96.2 0.0 copy-done.2
  96.2 1.7 %remote.1 = bf16[1536,128]{1,0:T(8,128)(2,1)} custom-call(bf16[1536,128]{1,0:T(8,128)(2,1)S(1)} %bitcast.9, f32[192,128]{1,0:T(8,128)S(1)} %copy-done.2), custom_call_target="tpu_custom_call" | custom-call | bytes 884736 | tf_op jit(solution)/shard_map/remote/pallas_call | solution.py:206
  97.9 6.5 %all-to-all-start.2 = ((bf16[64,24,128]{2,1,0:T(8,128)(2,1)}), bf16[64,24,128]{2,1,0:T(8,128)(2,1)S(1)}, u32[]{:S(2)}, u32[]{:S(2)}) async-start(bf16[64,24,128]{2,1,0:T(8,128)(2,1)} %bitcast.5), calls=%async_computation.2 | async-start | bytes 786432 | tf_op jit(solution)/shard_map/all_to_all | solution.py:246
  104.4 1.9 %all-gather.3.cloned.1.call-done = bf16[6400,384]{1,0:T(8,128)(2,1)} async-done(((bf16[400,384]{1,0:T(8,128)(2,1)}), bf16[6400,384]{1,0:T(8,128)(2,1)}) %all-gather.3.cloned.1.call-update) | async-done | bytes 4915216 | tf_op jit(solution)/shard_map/all_gather | solution.py:275
  106.4 8.3 %kept.1 = (bf16[512,256]{1,0:T(8,128)(2,1)}, bf16[512,256]{1,0:T(8,128)(2,1)}, bf16[512,256]{1,0:T(8,128)(2,1)}) custom-call(bf16[16,400,384]{2,1,0:T(8,128)(2,1)} %bitcast.10, bf16[256,6144]{1,0:T(8,128)(2,1)} %w_ref.3, bf16[400,768]{1,0:T(8,128)(2,1)} %get-tuple-element.22.rows_ref, f32[144,128]{1,0:T(8,128)} %get-tuple-element.23.valid_ref, ...), custom_call_target="tpu_custom_call" | custom-call | flops 1258291200 | bytes 9797632 | tf_op jit(solution)/shard_map/kept/pallas_call | solution.py:297
  114.7 4.0 %all-to-all-done.2 = bf16[64,24,128]{2,1,0:T(8,128)(2,1)S(1)} async-done(((bf16[64,24,128]{2,1,0:T(8,128)(2,1)}), bf16[64,24,128]{2,1,0:T(8,128)(2,1)S(1)}, u32[]{:S(2)}, u32[]{:S(2)}) %all-to-all-start.2) | async-done | bytes 393248 | tf_op jit(solution)/shard_map/all_to_all | solution.py:246
  118.8 0.0 copy-start.3
  118.8 0.7 copy-done.3
  119.5 2.5 %merge.1 = (bf16[512,256]{1,0:T(8,128)(2,1)}, bf16[512,256]{1,0:T(8,128)(2,1)}, bf16[512,256]{1,0:T(8,128)(2,1)}) custom-call(bf16[1536,128]{1,0:T(8,128)(2,1)} %bitcast.11, s32[512,128]{1,0:T(8,128)} %get-tuple-element.19.pos_ref, bf16[512,256]{1,0:T(8,128)(2,1)} %get-tuple-element.24.q_ref, bf16[512,256]{1,0:T(8,128)(2,1)} %get-tuple-element.25.k_ref, ...), custom_call_target="tpu_custom_call" | custom-call | bytes 2228224 | tf_op jit(solution)/shard_map/merge/pallas_call | solution.py:206
Async XLA Ops:
  9.9 54.7 %copy-start = (bf16[256,6144]{1,0:T(8,128)(2,1)S(1)}, bf16[256,6144]{1,0:T(8,128)(2,1)}, u32[]{:S(2)}) copy-start(bf16[256,6144]{1,0:T(8,128)(2,1)} %w_ref.3) | copy-start | bytes 9437188
  9.9 49.6 %all-to-all-start = ((bf16[8,192,384]{2,1,0:T(8,128)(2,1)}), bf16[8,192,384]{2,1,0:T(8,128)(2,1)}, u32[]{:S(2)}, u32[]{:S(2)}) async-start(bf16[8,192,384]{2,1,0:T(8,128)(2,1)} %get-tuple-element.15), calls=%async_computation | async-start | bytes 2359296 | tf_op jit(solution)/shard_map/all_to_all | solution.py:257
  27.4 79.0 %all-gather.3.cloned.1.call-start = ((), (), s32[]{:S(2)}) async-start(), calls=%async_computation.3 | async-start | bytes 5222400 | tf_op jit(solution)/shard_map/all_gather | solution.py:275
  59.5 5.1 %collective-permute-start = (bf16[8,192,384]{2,1,0:T(8,128)(2,1)}, bf16[8,192,384]{2,1,0:T(8,128)(2,1)S(1)}, u32[]{:S(2)}, u32[]{:S(2)}) collective-permute-start(bf16[8,192,384]{2,1,0:T(8,128)(2,1)} %all-to-all-done.own_ref), channel_id=1, source_target_pairs={{0,1},{1,0},{2,3},{3,2},{4,5},{5,4},{6,7},{7,6},{8,9},{9,8},{10,11... | collective-permute-start | bytes 3538952 | tf_op jit(solution)/shard_map/ppermute | solution.py:260
  64.6 1.0 copy-start.1
  65.6 30.6 %copy-start.2 = (f32[192,128]{1,0:T(8,128)S(1)}, f32[192,128]{1,0:T(8,128)}, u32[]{:S(2)}) copy-start(f32[192,128]{1,0:T(8,128)} %get-tuple-element.18.valid_ref) | copy-start | bytes 294916
  97.9 20.9 %all-to-all-start.2 = ((bf16[64,24,128]{2,1,0:T(8,128)(2,1)}), bf16[64,24,128]{2,1,0:T(8,128)(2,1)S(1)}, u32[]{:S(2)}, u32[]{:S(2)}) async-start(bf16[64,24,128]{2,1,0:T(8,128)(2,1)} %bitcast.5), calls=%async_computation.2 | async-start | bytes 786432 | tf_op jit(solution)/shard_map/all_to_all | solution.py:246
  118.8 0.7 copy-start.3
Sparse Core Ops, SparseCore 0:
  59.7 46.6 all-gather.2

commit v5 on v4

--- a/solution.py
+++ b/solution.py
@@ -15,6 +15,7 @@
 KEPT = BIG + SMALL
 OCT = 8
 LOG2E = 1.4426950408889634
+CHUNKS = ((0, 208), (208, 192))
 F32 = jnp.float32
 BF16 = jnp.bfloat16
 MIB = 1024 * 1024
@@ -114,16 +115,70 @@
     return query_grad.astype(BF16), key_grad.astype(BF16), value_grad.astype(BF16)
 
 
-def moved_kernel(own_ref, pair_ref, w_ref, rows_ref, send_ref, wide_ref):
-    chips, slots, feat = own_ref.shape
+def block_dot(rows, w_ref, start):
+    cols = rows.shape[1]
+    weight = w_ref[:, pl.ds(pl.multiple_of(start, HD), cols)]
+    return lax.dot_general(rows, weight, NT, preferred_element_type=F32)
+
+
+def source_start(n_mp, me, away, feat):
+    chips = n_mp // 2
+    chip, core = me // 2, me % 2
+    return (jnp.where(core == 0, chip - away, chip + away) + chips) % chips * (2 * feat)
+
+
+def partial_kernel(n_mp, own_ref, *refs):
+    *hop_refs, w_ref, w_pair_ref, acc_ref, w_late_ref = refs
+    chunks = len(hop_refs) // 2
+    feat = own_ref.shape[1]
+    me = lax.axis_index("mp")
+    third = pl.multiple_of(source_start(n_mp, me, 3, feat), HD)
+    last = pl.multiple_of((me + n_mp // 2) % n_mp * feat, HD)
+    for side, weight_ref in enumerate((w_ref, w_pair_ref)):
+        row = 0
+        for chunk in range(chunks):
+            rows = hop_refs[chunk].shape[1]
+            acc = block_dot(own_ref[row : row + rows], weight_ref, me * feat)
+            for hop in range(2):
+                block_ref = hop_refs[hop * chunks + chunk]
+                start = source_start(n_mp, me, hop + 1, feat)
+                for half in range(2):
+                    acc = acc + block_dot(block_ref[half], weight_ref, start + half * feat)
+            acc_ref[side, row : row + rows] = acc
+            row += rows
+        w_late_ref[side, :, : 2 * feat] = weight_ref[:, pl.ds(third, 2 * feat)]
+        w_late_ref[side, :, 2 * feat :] = weight_ref[:, pl.ds(last, feat)]
+
+
+def last_kernel(acc_ref, *refs):
+    *hop_refs, w_late_ref, mine_ref, pair_ref = refs
+    chunks = len(hop_refs) // 2
+    feat = hop_refs[0].shape[2]
+    for side, out in enumerate((mine_ref, pair_ref)):
+        row = 0
+        for chunk in range(chunks):
+            hop3_ref, hop4_ref = hop_refs[chunk], hop_refs[chunks + chunk]
+            rows = hop3_ref.shape[1]
+            acc = acc_ref[side, row : row + rows]
+            for part, block in enumerate((hop3_ref[0], hop3_ref[1], hop4_ref[0])):
+                weight = w_late_ref[side, :, part * feat : (part + 1) * feat]
+                acc = acc + lax.dot_general(block, weight, NT, preferred_element_type=F32)
+            out[row : row + rows] = acc
+            row += rows
+
+
+def chips_kernel(n_mp, og_ref, w_ref, w_pair_ref, mine_ref, pair_ref):
+    chips, _, feat = og_ref.shape
     core = lax.axis_index("mp") % 2
-    acc = jnp.zeros((slots, w_ref.shape[0]), F32)
-    for chip in range(chips):
-        for block_ref, parity in ((own_ref, core), (pair_ref, 1 - core)):
-            start = pl.multiple_of((2 * chip + parity) * feat, HD)
-            weight = w_ref[:, pl.ds(start, feat)]
-            acc = acc + lax.dot_general(block_ref[chip], weight, NT, preferred_element_type=F32)
-    grad = acc.astype(BF16)
+    for weight_ref, out in ((w_ref, mine_ref), (w_pair_ref, pair_ref)):
+        acc = block_dot(og_ref[0], weight_ref, core * feat)
+        for chip in range(1, chips):
+            acc = acc + block_dot(og_ref[chip], weight_ref, (2 * chip + core) * feat)
+        out[...] = acc
+
+
+def moved_kernel(mine_ref, pair_ref, rows_ref, send_ref, wide_ref):
+    grad = mine_ref[...] + pair_ref[...]
     wide_ref[...] = rows_ref[...].astype(F32)
     to_octets(send_ref, wide_ref, 6, [grad[:, :HD], grad[:, HD:]])
 
@@ -140,51 +195,31 @@
     to_octets(send_ref, wide_ref, 0, [dq0, dq1, dk0, dk1, dv0, dv1])
 
 
-def project(og_ref, w_ref, acc_ref):
-    blocks, _, cols = og_ref.shape
-
-    @pl.when(pl.program_id(0) == 0)
-    def _():
-        acc_ref[...] = jnp.zeros_like(acc_ref)
-
-    acc = acc_ref[...]
-    for b in range(blocks):
-        acc = acc + lax.dot_general(
-            og_ref[b], w_ref[:, b * cols : (b + 1) * cols], NT, preferred_element_type=F32
-        )
-    acc_ref[...] = acc
-
-
 def local_kernel(
-    n_dp, tok, img, og_ref, w_ref, rows_ref, valid_ref, pos_ref,
-    dq_ref, dk_ref, dv_ref, acc_ref,
+    n_dp, tok, img, mine_ref, pair_ref, rows_ref, valid_ref, pos_ref, dq_ref, dk_ref, dv_ref
 ):
-    project(og_ref, w_ref, acc_ref)
-
-    @pl.when(pl.program_id(0) == pl.num_programs(0) - 1)
-    def _():
-        slots = n_dp * CAP
-        grad = acc_ref[...].astype(BF16)
-        valid = valid_ref[:, 0:1]
-        count = jnp.sum(valid, axis=0, keepdims=True)
-        images = (
-            (slice(0, BIG), None, tok / (img * BIG)),
-            (slice(BIG, KEPT), valid > 0.5, tok / (img * count)),
-        )
-        parts = []
-        for head in range(2):
-            lanes = slice(head * HD, (head + 1) * HD)
-            pieces = []
-            for span, mask, weight in images:
-                q = rows_ref[span, head * HD : (head + 1) * HD]
-                k = rows_ref[span, (2 + head) * HD : (3 + head) * HD]
-                v = rows_ref[span, (4 + head) * HD : (5 + head) * HD]
-                pieces.append(attend(q, k, v, grad[span, lanes], mask, weight))
-            parts.append([jnp.concatenate(p, 0) for p in zip(*pieces)])
-        pos = pos_ref[:, 0:1] - slots
-        hot = one_hot(iota((tok, KEPT), 1) == pos)
-        for out, name in zip((dq_ref, dk_ref, dv_ref), range(3)):
-            out[...] = pick(hot, jnp.concatenate([parts[0][name], parts[1][name]], 1))
+    slots = n_dp * CAP
+    grad = (mine_ref[...] + pair_ref[...]).astype(BF16)
+    valid = valid_ref[:, 0:1]
+    count = jnp.sum(valid, axis=0, keepdims=True)
+    images = (
+        (slice(0, BIG), None, tok / (img * BIG)),
+        (slice(BIG, KEPT), valid > 0.5, tok / (img * count)),
+    )
+    parts = []
+    for head in range(2):
+        lanes = slice(head * HD, (head + 1) * HD)
+        pieces = []
+        for span, mask, weight in images:
+            q = rows_ref[span, head * HD : (head + 1) * HD]
+            k = rows_ref[span, (2 + head) * HD : (3 + head) * HD]
+            v = rows_ref[span, (4 + head) * HD : (5 + head) * HD]
+            pieces.append(attend(q, k, v, grad[span, lanes], mask, weight))
+        parts.append([jnp.concatenate(p, 0) for p in zip(*pieces)])
+    pos = pos_ref[:, 0:1] - slots
+    hot = one_hot(iota((tok, KEPT), 1) == pos)
+    for name, out in enumerate((dq_ref, dk_ref, dv_ref)):
+        out[...] = pick(hot, jnp.concatenate([parts[0][name], parts[1][name]], 1))
 
 
 def merge_kernel(back_ref, pos_ref, q_ref, k_ref, v_ref, dq_ref, dk_ref, dv_ref, wide_ref):
@@ -239,6 +274,8 @@
     exch = slots * OCT
     wide = [pltpu.VMEM((exch, HD), F32)]
     swap = [(i, i ^ 1) for i in range(n_mp)]
+    pairs = [[2 * i, 2 * i + 1] for i in range(n_mp // 2)]
+    ring = [(i, (i + (2 if i % 2 == 0 else -2)) % n_mp) for i in range(n_mp)]
     same_core = [list(range(core, n_mp, 2)) for core in range(2)]
 
     def exchange(rows):
@@ -248,6 +285,16 @@
     def after(value, earlier):
         return lax.optimization_barrier((value, earlier))[0]
 
+    def hop(block):
+        return lax.ppermute(block, "mp", ring)
+
+    def opposite(block):
+        return hop(lax.dynamic_slice_in_dim(block, lax.axis_index("mp") % 2, 1, 0))
+
+    def in_chunks(block):
+        return [block[:, start : start + size] for start, size in CHUNKS]
+
+    pair_weight = lax.ppermute(out_weight, "mp", swap)
     pos, og_moved = call(
         functools.partial(plan_kernel, n_dp),
         (destinations.reshape(1, tok), image_ids.reshape(1, tok), patch_counts.reshape(1, img), out_grad),
@@ -257,7 +304,6 @@
     og_chips = lax.all_to_all(
         og_moved, "mp", split_axis=0, concat_axis=0, tiled=True, axis_index_groups=same_core
     )
-    og_pair = lax.ppermute(og_chips, "mp", swap)
     send, og_kept, rows_kept, used, kept_used, pos_col = call(
         functools.partial(pack_kernel, n_dp),
         (pos, out_grad, query_rows, key_rows, value_rows),
@@ -272,16 +318,29 @@
         "pack",
         scratch=wide,
     )
-    kept_all = lax.all_gather(after(og_kept, og_chips), "mp", axis=0)
+    kept_block = lax.all_gather(og_kept, "mp", axis=0, axis_index_groups=pairs)
+    og_chips = after(og_chips, kept_block)
+    kept_blocks = in_chunks(kept_block)
+    mine, pair = call(
+        functools.partial(chips_kernel, n_mp),
+        (og_chips, out_weight, pair_weight),
+        (sds((slots, cols), F32),) * 2,
+        "chips",
+        24,
+    )
+    pair = lax.ppermute(pair, "mp", swap)
+    kept1 = [hop(after(x, mine)) for x in kept_blocks]
     moved_send = call(
         moved_kernel,
-        (og_chips, og_pair, out_weight, send),
+        (mine, pair, send),
         sds((exch, HD), BF16),
         "moved",
-        24,
+        8,
         scratch=wide,
     )
     rows_in = exchange(moved_send)
+    kept2 = [hop(after(x, moved_send)) for x in kept1]
+    kept3 = [hop(x) for x in kept2]
     back_send = call(
         functools.partial(remote_kernel, tok, img),
         (rows_in, used),
@@ -291,28 +350,32 @@
         scratch=wide,
     )
     back = exchange(back_send)
-    ins = (kept_all, out_weight, rows_kept, kept_used, pos_col)
-    outs = (sds((tok, cols), BF16),) * 3
-    per_step = 4 if n_mp % 4 == 0 else 1
-    kept_grads = pl.pallas_call(
+    kept4 = [opposite(x) for x in kept3]
+    acc, w_late = call(
+        functools.partial(partial_kernel, n_mp),
+        (og_kept, *kept1, *kept2, out_weight, pair_weight),
+        (sds((2, KEPT, cols), F32), sds((2, cols, 3 * feat), BF16)),
+        "partial",
+        56,
+        2 * KEPT * n_mp * feat * cols,
+    )
+    mine, pair = call(
+        last_kernel, (acc, *kept3, *kept4, w_late), (sds((KEPT, cols), F32),) * 2, "last"
+    )
+    pair = lax.ppermute(pair, "mp", swap)
+    kept_grads = call(
         functools.partial(local_kernel, n_dp, tok, img),
-        out_shape=outs,
-        grid=(n_mp // per_step,),
-        in_specs=[
-            pl.BlockSpec((per_step, KEPT, feat), lambda i: (i, 0, 0)),
-            pl.BlockSpec((cols, per_step * feat), lambda i: (0, i)),
-            *(whole(x) for x in ins[2:]),
-        ],
-        out_specs=tuple(whole(x) for x in outs),
-        scratch_shapes=[pltpu.VMEM((KEPT, cols), F32)],
-        **options(ins, outs, "kept", 56, 2 * KEPT * n_mp * feat * cols),
-    )(*ins)
+        (mine, pair, rows_kept, kept_used, pos_col),
+        (sds((tok, cols), BF16),) * 3,
+        "kept",
+        24,
+    )
     return call(
         merge_kernel,
         (back, pos_col) + kept_grads,
         (sds((tok, cols), BF16),) * 3,
         "merge",
-        56,
+        12,
         scratch=wide,
     )
 

time: 131 us -> 139 us (1.061)
  starting transfers between devices: 26.5 us -> 74.8 us
  blocking collectives: 27.9 us -> 3.87 us
  between operations: 14.1 us -> 1 us
  waiting for transfers between devices: 37.5 us -> 30.5 us
  Pallas kernels: 21.1 us -> 25.1 us
    ppermute x1 -> x11, starting transfers between devices: 2.4 us -> 45.3 us  [the longest x8 21.8 us: hop(): return lax.ppermute(block, 'mp', ring)]
    all_to_all x1 -> x0, blocking collectives: 27.9 us -> none  [exchange(): lax.all_to_all(shaped, 'dp', split_axis=0, concat_axis=0, tiled=True)]
    all_to_all x1 -> x2, starting transfers between devices: 6.54 us -> 24.9 us  [exchange(): lax.all_to_all(shaped, 'dp', split_axis=0, concat_axis=0, tiled=True)]
    all_to_all x1, starting transfers between devices: 17.5 us -> 4.54 us  [local(): lax.all_to_all(og_moved, 'mp', split_axis=0, concat_axis=0, tiled=True, a...]
    pallas_call x5 -> x9, Pallas kernels: 12.8 us -> 25.1 us  [call(): pl.pallas_call(kernel, out_shape=outs, grid=(1,), in_specs=[whole(x) for...]
    pallas_call x1 -> x0, Pallas kernels: 8.35 us -> none  [local(): pl.pallas_call(functools.partial(local_kernel, n_dp, tok, img), out_shape...]
    all_to_all x1 -> x2, waiting for transfers between devices: 4.04 us -> 0.01 us  [exchange(): lax.all_to_all(shaped, 'dp', split_axis=0, concat_axis=0, tiled=True)]
    all_to_all x1, waiting for transfers between devices: 28.9 us -> 25 us  [local(): lax.all_to_all(og_moved, 'mp', split_axis=0, concat_axis=0, tiled=True, a...]
  transfers between devices with their start and end apart: 4 -> 14, of which waited for: 4 -> 4; matrix products, arithmetic and copies ran while one was open for 0% -> 1% of each run, Pallas kernels for 12% -> 15%
where the time goes in v5:
time: 139 us; the launch traced here: 138 us
  starting transfers between devices  74.8 us (54%)
  waiting for transfers between devices  30.5 us (22%)
  Pallas kernels  25.1 us (18%)
  blocking collectives  3.87 us (3%)
  local copies, waits for them, and re-layouts  2.82 us (2%)
    pallas_call x9, Pallas kernels, call(): pl.pallas_call(kernel, out_shape=outs, grid=(1,), in_specs=[whole(x) for...  25.1 us
    all_to_all x1, waiting for transfers between devices, local(): lax.all_to_all(og_moved, 'mp', split_axis=0, concat_axis=0, tiled=True, a...  25 us
    all_to_all x2, starting transfers between devices, exchange(): lax.all_to_all(shaped, 'dp', split_axis=0, concat_axis=0, tiled=True)  24.9 us
    ppermute x8, starting transfers between devices, hop(): return lax.ppermute(block, 'mp', ring)  21.8 us
    ppermute x1, starting transfers between devices, local(): pair_weight = lax.ppermute(out_weight, 'mp', swap)  16.1 us
    ppermute x2, starting transfers between devices, local(): pair = lax.ppermute(pair, 'mp', swap)  7.5 us
    all_to_all x1, starting transfers between devices, local(): lax.all_to_all(og_moved, 'mp', split_axis=0, concat_axis=0, tiled=True, a...  4.54 us
    ppermute x8, waiting for transfers between devices, hop(): return lax.ppermute(block, 'mp', ring)  3.91 us
  transfers between devices with their start and end apart: 14, of which 4 were waited for; matrix products, arithmetic and copies ran while one was open for 1% of the time, Pallas kernels for 15%

profile of v5, /device:TPU:1, one launch (start us, length us, event | category | flops | bytes accessed | tf_op | source)
XLA Modules:
  0.0 138.0 jit_solution(11248841016394591425)
XLA Ops:
  0.6 16.1 %collective-permute-start = (bf16[256,6144]{1,0:T(8,128)(2,1)}, bf16[256,6144]{1,0:T(8,128)(2,1)}, u32[]{:S(2)}, u32[]{:S(2)}) collective-permute-start(bf16[256,6144]{1,0:T(8,128)(2,1)} %refs_4_.1), channel_id=1, source_target_pairs={{0,1},{1,0},{2,3},{3,2},{4,5},{5,4},{6,7},{7,6},{8,9},{9,8},{10,11... | collective-permute-start | bytes 9437192 | tf_op jit(solution)/shard_map/ppermute | solution.py:297
  16.7 2.7 %plan.1 = (s32[8,512]{1,0:T(8,128)}, bf16[8,192,384]{2,1,0:T(8,128)(2,1)}) custom-call(s32[1,512]{1,0:T(1,128)} %bitcast.12, s32[1,512]{1,0:T(1,128)} %bitcast.13, s32[1,3]{1,0:T(1,128)} %bitcast.14, bf16[512,384]{1,0:T(8,128)(2,1)} %og_ref.3), custom_call_target="tpu_custom_call" | custom-call | bytes 1593356 | tf_op jit(solution)/shard_map/plan/pallas_call | solution.py:241
  19.4 0.0 copy-start
  19.4 4.5 %all-to-all-start = ((bf16[8,192,384]{2,1,0:T(8,128)(2,1)}), bf16[8,192,384]{2,1,0:T(8,128)(2,1)}, u32[]{:S(2)}, u32[]{:S(2)}) async-start(bf16[8,192,384]{2,1,0:T(8,128)(2,1)} %get-tuple-element.25), calls=%async_computation | async-start | bytes 2359296 | tf_op jit(solution)/shard_map/all_to_all | solution.py:304
  23.9 3.2 %pack.1 = (bf16[1536,128]{1,0:T(8,128)(2,1)}, bf16[400,384]{1,0:T(8,128)(2,1)}, bf16[400,768]{1,0:T(8,128)(2,1)}, f32[192,128]{1,0:T(8,128)}, f32[144,128]{1,0:T(8,128)}, /*index=5*/s32[512,128]{1,0:T(8,128)}) custom-call(s32[8,512]{1,0:T(8,128)} %get-tuple-element.26.pos_ref, bf16[512,384]{1,0:T(8,128)(2,1)} %og_ref.3, bf16[512,256]{1,0:T(8,128)(2,1)} %q_ref.1, ...), custom_call_target="tpu_custom_call" | custom-call | bytes 2945024 | tf_op jit(solution)/shard_map/pack/pallas_call | solution.py:241
  27.2 3.9 %all-gather = bf16[800,384]{1,0:T(8,128)(2,1)} all-gather(bf16[400,384]{1,0:T(8,128)(2,1)} %get-tuple-element.27.own_ref), channel_id=2, replica_groups={{0,1},{2,3},{4,5},{6,7},{8,9},{10,11},{12,13},{14,15},{16,17},{18,19},{..., dimensions={0}, use_global_device_ids=true | all-gather | bytes 921600 | tf_op jit(solution)/shard_map/all_gather | solution.py:321
  31.0 25.0 %all-to-all-done.og_ref = bf16[8,192,384]{2,1,0:T(8,128)(2,1)} async-done(((bf16[8,192,384]{2,1,0:T(8,128)(2,1)}), bf16[8,192,384]{2,1,0:T(8,128)(2,1)}, u32[]{:S(2)}, u32[]{:S(2)}) %all-to-all-start) | async-done | bytes 1179680 | tf_op jit(solution)/shard_map/all_to_all | solution.py:304
  56.0 0.0 copy-start.7
  56.0 0.0 collective-permute-done.w_pair_ref.refs_5_
  56.0 0.0 copy-done
  56.0 3.6 %chips.1 = (f32[192,256]{1,0:T(8,128)S(1)}, f32[192,256]{1,0:T(8,128)S(1)}) custom-call(bf16[8,192,384]{2,1,0:T(8,128)(2,1)} %all-to-all-done.og_ref, bf16[256,6144]{1,0:T(8,128)(2,1)S(1)} %copy-done, bf16[256,6144]{1,0:T(8,128)(2,1)} %collective-permute-done.w_pair_ref.refs_5_), custom_call_target="tpu_custom_call" | custom-call | bytes 7864320 | tf_op jit(solution)/shard_map/chips/pallas_call | solution.py:241
  59.7 2.3 %collective-permute-start.1 = (f32[192,256]{1,0:T(8,128)S(1)}, f32[192,256]{1,0:T(8,128)S(1)}, u32[]{:S(2)}, u32[]{:S(2)}) collective-permute-start(f32[192,256]{1,0:T(8,128)S(1)} %get-tuple-element.30), channel_id=1, source_target_pairs={{0,1},{1,0},{2,3},{3,2},{4,5},{5,4},{6,7},{7,6},{8,9},{9,8},{10,11... | collective-permute-start | bytes 589832 | tf_op jit(solution)/shard_map/ppermute | solution.py:331
  62.0 0.0 copy-done.7
  62.1 1.9 %collective-permute-start.2 = (bf16[2,208,384]{2,1,0:T(8,128)(2,1)S(1)}, bf16[2,208,384]{2,1,0:T(8,128)(2,1)S(1)}, u32[]{:S(2)}, u32[]{:S(2)}) collective-permute-start(bf16[2,208,384]{2,1,0:T(8,128)(2,1)S(1)} %slice.8), channel_id=1, source_target_pairs={{0,2},{1,15},{2,4},{3,1},{4,6},{5,3},{6,8},{7,5},{8,10},{9,7},{10,... | collective-permute-start | bytes 958472 | tf_op jit(solution)/shard_map/ppermute | solution.py:289
  64.0 0.0 collective-permute-done.1.pair_ref
  64.0 0.0 copy-done.4
  64.0 0.0 copy-start.5
  64.0 0.9 moved.1
  64.9 12.8 %all-to-all-start.1 = ((bf16[64,24,128]{2,1,0:T(8,128)(2,1)}), bf16[64,24,128]{2,1,0:T(8,128)(2,1)S(1)}, u32[]{:S(2)}, u32[]{:S(2)}) async-start(bf16[64,24,128]{2,1,0:T(8,128)(2,1)} %bitcast.4), calls=%async_computation.1 | async-start | bytes 786432 | tf_op jit(solution)/shard_map/all_to_all | solution.py:283
  77.7 1.0 slice.9
  78.7 2.3 %collective-permute-start.3 = (bf16[2,192,384]{2,1,0:T(8,128)(2,1)S(1)}, bf16[2,192,384]{2,1,0:T(8,128)(2,1)S(1)}, u32[]{:S(2)}, u32[]{:S(2)}) collective-permute-start(bf16[2,192,384]{2,1,0:T(8,128)(2,1)S(1)} %slice.9), channel_id=1, source_target_pairs={{0,2},{1,15},{2,4},{3,1},{4,6},{5,3},{6,8},{7,5},{8,10},{9,7},{10,... | collective-permute-start | bytes 884744 | tf_op jit(solution)/shard_map/ppermute | solution.py:289
  81.1 0.0 collective-permute-done.2.refs_0_
  81.1 0.0 copy-start.10
  81.1 2.3 %collective-permute-start.4 = (bf16[2,208,384]{2,1,0:T(8,128)(2,1)S(1)}, bf16[2,208,384]{2,1,0:T(8,128)(2,1)S(1)}, u32[]{:S(2)}, u32[]{:S(2)}) collective-permute-start(bf16[2,208,384]{2,1,0:T(8,128)(2,1)S(1)} %collective-permute-done.2.refs_0_), channel_id=1, source_target_pairs={{0,2},{1,15},{2,4},{3,1},{4,6},{5,3},{6,8},{7,5},{8,10},{9,7},{10,... | collective-permute-start | bytes 958472 | tf_op jit(solution)/shard_map/ppermute | solution.py:289
  83.4 3.1 %collective-permute-done.3.refs_1_ = bf16[2,192,384]{2,1,0:T(8,128)(2,1)S(1)} collective-permute-done((bf16[2,192,384]{2,1,0:T(8,128)(2,1)S(1)}, bf16[2,192,384]{2,1,0:T(8,128)(2,1)S(1)}, u32[]{:S(2)}, u32[]{:S(2)}) %collective-permute-start.3) | collective-permute-done | bytes 294944 | tf_op jit(solution)/shard_map/ppermute | solution.py:289
  86.5 3.5 %collective-permute-start.5 = (bf16[2,192,384]{2,1,0:T(8,128)(2,1)S(1)}, bf16[2,192,384]{2,1,0:T(8,128)(2,1)S(1)}, u32[]{:S(2)}, u32[]{:S(2)}) collective-permute-start(bf16[2,192,384]{2,1,0:T(8,128)(2,1)S(1)} %collective-permute-done.3.refs_1_), channel_id=1, source_target_pairs={{0,2},{1,15},{2,4},{3,1},{4,6},{5,3},{6,8},{7,5},{8,10},{9,7},{10,... | collective-permute-start | bytes 884744 | tf_op jit(solution)/shard_map/ppermute | solution.py:289
  90.0 0.0 collective-permute-done.4.refs_2_
  90.0 0.0 copy-start.11
  90.0 3.4 %collective-permute-start.6 = (bf16[2,208,384]{2,1,0:T(8,128)(2,1)S(1)}, bf16[2,208,384]{2,1,0:T(8,128)(2,1)S(1)}, u32[]{:S(2)}, u32[]{:S(2)}) collective-permute-start(bf16[2,208,384]{2,1,0:T(8,128)(2,1)S(1)} %collective-permute-done.4.refs_2_), channel_id=1, source_target_pairs={{0,2},{1,15},{2,4},{3,1},{4,6},{5,3},{6,8},{7,5},{8,10},{9,7},{10,... | collective-permute-start | bytes 958472 | tf_op jit(solution)/shard_map/ppermute | solution.py:289
  93.4 0.8 collective-permute-done.5.refs_3_
  94.2 4.5 %collective-permute-start.7 = (bf16[2,192,384]{2,1,0:T(8,128)(2,1)S(1)}, bf16[2,192,384]{2,1,0:T(8,128)(2,1)S(1)}, u32[]{:S(2)}, u32[]{:S(2)}) collective-permute-start(bf16[2,192,384]{2,1,0:T(8,128)(2,1)S(1)} %collective-permute-done.5.refs_3_), channel_id=1, source_target_pairs={{0,2},{1,15},{2,4},{3,1},{4,6},{5,3},{6,8},{7,5},{8,10},{9,7},{10,... | collective-permute-start | bytes 884744 | tf_op jit(solution)/shard_map/ppermute | solution.py:289
  98.7 0.0 all-to-all-done.1
  98.7 0.0 copy-done.5
  98.7 1.7 %remote.1 = bf16[1536,128]{1,0:T(8,128)(2,1)} custom-call(bf16[1536,128]{1,0:T(8,128)(2,1)S(1)} %bitcast.8, f32[192,128]{1,0:T(8,128)S(1)} %copy-done.5), custom_call_target="tpu_custom_call" | custom-call | bytes 884736 | tf_op jit(solution)/shard_map/remote/pallas_call | solution.py:241
  100.4 12.1 %all-to-all-start.2 = ((bf16[64,24,128]{2,1,0:T(8,128)(2,1)}), bf16[64,24,128]{2,1,0:T(8,128)(2,1)S(1)}, u32[]{:S(2)}, u32[]{:S(2)}) async-start(bf16[64,24,128]{2,1,0:T(8,128)(2,1)} %bitcast.6), calls=%async_computation.2 | async-start | bytes 786432 | tf_op jit(solution)/shard_map/all_to_all | solution.py:283
  112.5 0.0 collective-permute-done.6.refs_0_
  112.6 0.0 copy-start.8
  112.6 1.9 %collective-permute-start.8 = (bf16[1,208,384]{2,1,0:T(8,128)(2,1)S(1)}, bf16[1,208,384]{2,1,0:T(8,128)(2,1)S(1)}, u32[]{:S(2)}, u32[]{:S(2)}) collective-permute-start(bf16[1,208,384]{2,1,0:T(8,128)(2,1)S(1)} %constant_dynamic-slice_fusion.1), channel_id=1, source_target_pairs={{0,2},{1,15},{2,4},{3,1},{4,6},{5,3},{6,8},{7,5},{8,10},{9,7},{10,... | collective-permute-start | bytes 479240 | tf_op jit(solution)/shard_map/ppermute | solution.py:289
  114.5 0.0 collective-permute-done.7.refs_1_
  114.5 0.0 copy-start.9
  114.6 1.9 %collective-permute-start.9 = (bf16[1,192,384]{2,1,0:T(8,128)(2,1)S(1)}, bf16[1,192,384]{2,1,0:T(8,128)(2,1)S(1)}, u32[]{:S(2)}, u32[]{:S(2)}) collective-permute-start(bf16[1,192,384]{2,1,0:T(8,128)(2,1)S(1)} %constant_dynamic-slice_fusion), channel_id=1, source_target_pairs={{0,2},{1,15},{2,4},{3,1},{4,6},{5,3},{6,8},{7,5},{8,10},{9,7},{10,... | collective-permute-start | bytes 442376 | tf_op jit(solution)/shard_map/ppermute | solution.py:289
  116.5 0.0 copy-done.10
  116.5 0.0 copy-done.12
  116.5 0.0 copy-done.11
  116.5 0.0 copy-done.13
  116.6 6.0 %partial.1 = (f32[2,400,256]{2,1,0:T(8,128)}, bf16[2,256,1152]{2,1,0:T(8,128)(2,1)}) custom-call(bf16[400,384]{1,0:T(8,128)(2,1)} %get-tuple-element.27.own_ref, bf16[2,208,384]{2,1,0:T(8,128)(2,1)} %copy-done.10, bf16[2,192,384]{2,1,0:T(8,128)(2,1)} %copy-done.12, bf16[2,208,384]{2,1,0:T(8,128)(2,1)} %copy-done.11, bf16[2,192,384]{2,1,0:T(8,128)(2,1)} %copy-done.13, ...), custom_call_target="tpu_custom_call" | custom-call | flops 1258291200 | bytes 9826304 | tf_op jit(solution)/shard_map/partial/pallas_call | solution.py:241
  122.6 0.0 copy-done.8
  122.6 0.0 copy-done.9
  122.6 0.0 collective-permute-done.9.refs_3_
  122.6 0.0 copy-start.15
  122.6 0.0 collective-permute-done.8.refs_2_
  122.6 0.0 copy-start.14
  122.6 0.6 copy-done.15
  123.2 0.1 copy-done.14
  123.3 3.6 %last.1 = (f32[400,256]{1,0:T(8,128)}, f32[400,256]{1,0:T(8,128)}) custom-call(f32[2,400,256]{2,1,0:T(8,128)} %get-tuple-element.38.acc_ref, bf16[2,208,384]{2,1,0:T(8,128)(2,1)} %copy-done.8, bf16[2,192,384]{2,1,0:T(8,128)(2,1)} %copy-done.9, bf16[1,208,384]{2,1,0:T(8,128)(2,1)} %copy-done.14, bf16[1,192,384]{2,1,0:T(8,128)(2,1)} %copy-done.15, ...), custom_call_target="tpu_custom_call" | custom-call | bytes 3739648 | tf_op jit(solution)/shard_map/last/pallas_call | solution.py:241
  126.9 5.2 %collective-permute-start.10 = (f32[400,256]{1,0:T(8,128)}, f32[400,256]{1,0:T(8,128)S(1)}, u32[]{:S(2)}, u32[]{:S(2)}) collective-permute-start(f32[400,256]{1,0:T(8,128)} %get-tuple-element.41), channel_id=1, source_target_pairs={{0,1},{1,0},{2,3},{3,2},{4,5},{5,4},{6,7},{7,6},{8,9},{9,8},{10,11... | collective-permute-start | bytes 1228808 | tf_op jit(solution)/shard_map/ppermute | solution.py:365
  132.1 1.6 %collective-permute-done.10.pair_ref = f32[400,256]{1,0:T(8,128)S(1)} collective-permute-done((f32[400,256]{1,0:T(8,128)}, f32[400,256]{1,0:T(8,128)S(1)}, u32[]{:S(2)}, u32[]{:S(2)}) %collective-permute-start.10) | collective-permute-done | bytes 409632 | tf_op jit(solution)/shard_map/ppermute | solution.py:365
  133.6 0.0 copy-done.1
  133.6 0.0 copy-done.2
  133.6 0.0 copy-done.6
  133.6 1.0 copy-done.3
  134.6 2.1 %kept.1 = (bf16[512,256]{1,0:T(8,128)(2,1)S(1)}, bf16[512,256]{1,0:T(8,128)(2,1)S(1)}, bf16[512,256]{1,0:T(8,128)(2,1)S(1)}) custom-call(f32[400,256]{1,0:T(8,128)S(1)} %copy-done.3, f32[400,256]{1,0:T(8,128)S(1)} %collective-permute-done.10.pair_ref, bf16[400,768]{1,0:T(8,128)(2,1)S(1)} %copy-done.2, f32[144,128]{1,0:T(8,128)S(1)} %copy-done.6, ...), custom_call_target="tpu_custom_call" | custom-call | bytes 2555904 | tf_op jit(solution)/shard_map/kept/pallas_call | solution.py:241
  136.7 0.0 all-to-all-done.2
  136.8 1.2 merge.1
  (10 shorter events, 0.1 us)
Async XLA Ops:
  0.6 55.4 %collective-permute-start = (bf16[256,6144]{1,0:T(8,128)(2,1)}, bf16[256,6144]{1,0:T(8,128)(2,1)}, u32[]{:S(2)}, u32[]{:S(2)}) collective-permute-start(bf16[256,6144]{1,0:T(8,128)(2,1)} %refs_4_.1), channel_id=1, source_target_pairs={{0,1},{1,0},{2,3},{3,2},{4,5},{5,4},{6,7},{7,6},{8,9},{9,8},{10,11... | collective-permute-start | bytes 9437192 | tf_op jit(solution)/shard_map/ppermute | solution.py:297
  19.4 36.7 %copy-start = (bf16[256,6144]{1,0:T(8,128)(2,1)S(1)}, bf16[256,6144]{1,0:T(8,128)(2,1)}, u32[]{:S(2)}) copy-start(bf16[256,6144]{1,0:T(8,128)(2,1)} %refs_4_.1) | copy-start | bytes 9437188
  19.4 36.6 %all-to-all-start = ((bf16[8,192,384]{2,1,0:T(8,128)(2,1)}), bf16[8,192,384]{2,1,0:T(8,128)(2,1)}, u32[]{:S(2)}, u32[]{:S(2)}) async-start(bf16[8,192,384]{2,1,0:T(8,128)(2,1)} %get-tuple-element.25), calls=%async_computation | async-start | bytes 2359296 | tf_op jit(solution)/shard_map/all_to_all | solution.py:304
  56.0 6.0 %copy-start.7 = (bf16[800,384]{1,0:T(8,128)(2,1)S(1)}, bf16[800,384]{1,0:T(8,128)(2,1)}, u32[]{:S(2)}) copy-start(bf16[800,384]{1,0:T(8,128)(2,1)} %all-gather) | copy-start | bytes 1843204
  56.0 8.0 %copy-start.4 = (bf16[1536,128]{1,0:T(8,128)(2,1)S(1)}, bf16[1536,128]{1,0:T(8,128)(2,1)}, u32[]{:S(2)}) copy-start(bf16[1536,128]{1,0:T(8,128)(2,1)} %get-tuple-element.31.rows_ref) | copy-start | bytes 1179652
  59.7 4.3 %collective-permute-start.1 = (f32[192,256]{1,0:T(8,128)S(1)}, f32[192,256]{1,0:T(8,128)S(1)}, u32[]{:S(2)}, u32[]{:S(2)}) collective-permute-start(f32[192,256]{1,0:T(8,128)S(1)} %get-tuple-element.30), channel_id=1, source_target_pairs={{0,1},{1,0},{2,3},{3,2},{4,5},{5,4},{6,7},{7,6},{8,9},{9,8},{10,11... | collective-permute-start | bytes 589832 | tf_op jit(solution)/shard_map/ppermute | solution.py:331
  62.1 19.0 %collective-permute-start.2 = (bf16[2,208,384]{2,1,0:T(8,128)(2,1)S(1)}, bf16[2,208,384]{2,1,0:T(8,128)(2,1)S(1)}, u32[]{:S(2)}, u32[]{:S(2)}) collective-permute-start(bf16[2,208,384]{2,1,0:T(8,128)(2,1)S(1)} %slice.8), channel_id=1, source_target_pairs={{0,2},{1,15},{2,4},{3,1},{4,6},{5,3},{6,8},{7,5},{8,10},{9,7},{10,... | collective-permute-start | bytes 958472 | tf_op jit(solution)/shard_map/ppermute | solution.py:289
  64.0 34.7 %copy-start.5 = (f32[192,128]{1,0:T(8,128)S(1)}, f32[192,128]{1,0:T(8,128)}, u32[]{:S(2)}) copy-start(f32[192,128]{1,0:T(8,128)} %get-tuple-element.32.valid_ref) | copy-start | bytes 294916
  64.9 33.8 %all-to-all-start.1 = ((bf16[64,24,128]{2,1,0:T(8,128)(2,1)}), bf16[64,24,128]{2,1,0:T(8,128)(2,1)S(1)}, u32[]{:S(2)}, u32[]{:S(2)}) async-start(bf16[64,24,128]{2,1,0:T(8,128)(2,1)} %bitcast.4), calls=%async_computation.1 | async-start | bytes 786432 | tf_op jit(solution)/shard_map/all_to_all | solution.py:283
  78.7 7.8 %collective-permute-start.3 = (bf16[2,192,384]{2,1,0:T(8,128)(2,1)S(1)}, bf16[2,192,384]{2,1,0:T(8,128)(2,1)S(1)}, u32[]{:S(2)}, u32[]{:S(2)}) collective-permute-start(bf16[2,192,384]{2,1,0:T(8,128)(2,1)S(1)} %slice.9), channel_id=1, source_target_pairs={{0,2},{1,15},{2,4},{3,1},{4,6},{5,3},{6,8},{7,5},{8,10},{9,7},{10,... | collective-permute-start | bytes 884744 | tf_op jit(solution)/shard_map/ppermute | solution.py:289
  81.1 35.4 %copy-start.10 = (bf16[2,208,384]{2,1,0:T(8,128)(2,1)}, bf16[2,208,384]{2,1,0:T(8,128)(2,1)S(1)}, u32[]{:S(2)}) copy-start(bf16[2,208,384]{2,1,0:T(8,128)(2,1)S(1)} %collective-permute-done.2.refs_0_) | copy-start | bytes 958468
  81.1 8.9 %collective-permute-start.4 = (bf16[2,208,384]{2,1,0:T(8,128)(2,1)S(1)}, bf16[2,208,384]{2,1,0:T(8,128)(2,1)S(1)}, u32[]{:S(2)}, u32[]{:S(2)}) collective-permute-start(bf16[2,208,384]{2,1,0:T(8,128)(2,1)S(1)} %collective-permute-done.2.refs_0_), channel_id=1, source_target_pairs={{0,2},{1,15},{2,4},{3,1},{4,6},{5,3},{6,8},{7,5},{8,10},{9,7},{10,... | collective-permute-start | bytes 958472 | tf_op jit(solution)/shard_map/ppermute | solution.py:289
  86.5 30.0 %copy-start.12 = (bf16[2,192,384]{2,1,0:T(8,128)(2,1)}, bf16[2,192,384]{2,1,0:T(8,128)(2,1)S(1)}, u32[]{:S(2)}) copy-start(bf16[2,192,384]{2,1,0:T(8,128)(2,1)S(1)} %collective-permute-done.3.refs_1_) | copy-start | bytes 884740
  86.5 7.8 %collective-permute-start.5 = (bf16[2,192,384]{2,1,0:T(8,128)(2,1)S(1)}, bf16[2,192,384]{2,1,0:T(8,128)(2,1)S(1)}, u32[]{:S(2)}, u32[]{:S(2)}) collective-permute-start(bf16[2,192,384]{2,1,0:T(8,128)(2,1)S(1)} %collective-permute-done.3.refs_1_), channel_id=1, source_target_pairs={{0,2},{1,15},{2,4},{3,1},{4,6},{5,3},{6,8},{7,5},{8,10},{9,7},{10,... | collective-permute-start | bytes 884744 | tf_op jit(solution)/shard_map/ppermute | solution.py:289
  90.0 26.5 %copy-start.11 = (bf16[2,208,384]{2,1,0:T(8,128)(2,1)}, bf16[2,208,384]{2,1,0:T(8,128)(2,1)S(1)}, u32[]{:S(2)}) copy-start(bf16[2,208,384]{2,1,0:T(8,128)(2,1)S(1)} %collective-permute-done.4.refs_2_) | copy-start | bytes 958468
  90.0 22.5 %collective-permute-start.6 = (bf16[2,208,384]{2,1,0:T(8,128)(2,1)S(1)}, bf16[2,208,384]{2,1,0:T(8,128)(2,1)S(1)}, u32[]{:S(2)}, u32[]{:S(2)}) collective-permute-start(bf16[2,208,384]{2,1,0:T(8,128)(2,1)S(1)} %collective-permute-done.4.refs_2_), channel_id=1, source_target_pairs={{0,2},{1,15},{2,4},{3,1},{4,6},{5,3},{6,8},{7,5},{8,10},{9,7},{10,... | collective-permute-start | bytes 958472 | tf_op jit(solution)/shard_map/ppermute | solution.py:289
  94.2 22.3 %copy-start.13 = (bf16[2,192,384]{2,1,0:T(8,128)(2,1)}, bf16[2,192,384]{2,1,0:T(8,128)(2,1)S(1)}, u32[]{:S(2)}) copy-start(bf16[2,192,384]{2,1,0:T(8,128)(2,1)S(1)} %collective-permute-done.5.refs_3_) | copy-start | bytes 884740
  94.2 20.3 %collective-permute-start.7 = (bf16[2,192,384]{2,1,0:T(8,128)(2,1)S(1)}, bf16[2,192,384]{2,1,0:T(8,128)(2,1)S(1)}, u32[]{:S(2)}, u32[]{:S(2)}) collective-permute-start(bf16[2,192,384]{2,1,0:T(8,128)(2,1)S(1)} %collective-permute-done.5.refs_3_), channel_id=1, source_target_pairs={{0,2},{1,15},{2,4},{3,1},{4,6},{5,3},{6,8},{7,5},{8,10},{9,7},{10,... | collective-permute-start | bytes 884744 | tf_op jit(solution)/shard_map/ppermute | solution.py:289
  100.4 36.3 %all-to-all-start.2 = ((bf16[64,24,128]{2,1,0:T(8,128)(2,1)}), bf16[64,24,128]{2,1,0:T(8,128)(2,1)S(1)}, u32[]{:S(2)}, u32[]{:S(2)}) async-start(bf16[64,24,128]{2,1,0:T(8,128)(2,1)} %bitcast.6), calls=%async_computation.2 | async-start | bytes 786432 | tf_op jit(solution)/shard_map/all_to_all | solution.py:283
  112.6 10.0 %copy-start.8 = (bf16[2,208,384]{2,1,0:T(8,128)(2,1)}, bf16[2,208,384]{2,1,0:T(8,128)(2,1)S(1)}, u32[]{:S(2)}) copy-start(bf16[2,208,384]{2,1,0:T(8,128)(2,1)S(1)} %collective-permute-done.6.refs_0_) | copy-start | bytes 958468
  112.6 10.0 %collective-permute-start.8 = (bf16[1,208,384]{2,1,0:T(8,128)(2,1)S(1)}, bf16[1,208,384]{2,1,0:T(8,128)(2,1)S(1)}, u32[]{:S(2)}, u32[]{:S(2)}) collective-permute-start(bf16[1,208,384]{2,1,0:T(8,128)(2,1)S(1)} %constant_dynamic-slice_fusion.1), channel_id=1, source_target_pairs={{0,2},{1,15},{2,4},{3,1},{4,6},{5,3},{6,8},{7,5},{8,10},{9,7},{10,... | collective-permute-start | bytes 479240 | tf_op jit(solution)/shard_map/ppermute | solution.py:289
  114.5 8.0 %copy-start.9 = (bf16[2,192,384]{2,1,0:T(8,128)(2,1)}, bf16[2,192,384]{2,1,0:T(8,128)(2,1)S(1)}, u32[]{:S(2)}) copy-start(bf16[2,192,384]{2,1,0:T(8,128)(2,1)S(1)} %collective-permute-done.7.refs_1_) | copy-start | bytes 884740
  114.6 8.0 %collective-permute-start.9 = (bf16[1,192,384]{2,1,0:T(8,128)(2,1)S(1)}, bf16[1,192,384]{2,1,0:T(8,128)(2,1)S(1)}, u32[]{:S(2)}, u32[]{:S(2)}) collective-permute-start(bf16[1,192,384]{2,1,0:T(8,128)(2,1)S(1)} %constant_dynamic-slice_fusion), channel_id=1, source_target_pairs={{0,2},{1,15},{2,4},{3,1},{4,6},{5,3},{6,8},{7,5},{8,10},{9,7},{10,... | collective-permute-start | bytes 442376 | tf_op jit(solution)/shard_map/ppermute | solution.py:289
  122.6 0.7 copy-start.15
  122.6 0.7 copy-start.14
  123.3 10.3 %copy-start.1 = (s32[512,128]{1,0:T(8,128)S(1)}, s32[512,128]{1,0:T(8,128)}, u32[]{:S(2)}) copy-start(s32[512,128]{1,0:T(8,128)} %get-tuple-element.33.pos_ref) | copy-start | bytes 786436
  123.3 10.3 %copy-start.2 = (bf16[400,768]{1,0:T(8,128)(2,1)S(1)}, bf16[400,768]{1,0:T(8,128)(2,1)}, u32[]{:S(2)}) copy-start(bf16[400,768]{1,0:T(8,128)(2,1)} %get-tuple-element.42.rows_ref) | copy-start | bytes 1843204
  123.3 10.3 %copy-start.6 = (f32[144,128]{1,0:T(8,128)S(1)}, f32[144,128]{1,0:T(8,128)}, u32[]{:S(2)}) copy-start(f32[144,128]{1,0:T(8,128)} %get-tuple-element.43.valid_ref) | copy-start | bytes 221188
  126.9 6.7 %collective-permute-start.10 = (f32[400,256]{1,0:T(8,128)}, f32[400,256]{1,0:T(8,128)S(1)}, u32[]{:S(2)}, u32[]{:S(2)}) collective-permute-start(f32[400,256]{1,0:T(8,128)} %get-tuple-element.41), channel_id=1, source_target_pairs={{0,1},{1,0},{2,3},{3,2},{4,5},{5,4},{6,7},{7,6},{8,9},{9,8},{10,11... | collective-permute-start | bytes 1228808 | tf_op jit(solution)/shard_map/ppermute | solution.py:365
  133.6 1.0 copy-start.3

commit v6 on v4

--- a/solution.py
+++ b/solution.py
@@ -114,16 +114,25 @@
     return query_grad.astype(BF16), key_grad.astype(BF16), value_grad.astype(BF16)
 
 
-def moved_kernel(own_ref, pair_ref, w_ref, rows_ref, send_ref, wide_ref):
-    chips, slots, feat = own_ref.shape
-    core = lax.axis_index("mp") % 2
-    acc = jnp.zeros((slots, w_ref.shape[0]), F32)
+def parity_dot(block_ref, w_ref, parity):
+    chips, rows, feat = block_ref.shape
+    acc = jnp.zeros((rows, w_ref.shape[0]), F32)
     for chip in range(chips):
-        for block_ref, parity in ((own_ref, core), (pair_ref, 1 - core)):
-            start = pl.multiple_of((2 * chip + parity) * feat, HD)
-            weight = w_ref[:, pl.ds(start, feat)]
-            acc = acc + lax.dot_general(block_ref[chip], weight, NT, preferred_element_type=F32)
-    grad = acc.astype(BF16)
+        start = pl.multiple_of((2 * chip + parity) * feat, HD)
+        weight = w_ref[:, pl.ds(start, feat)]
+        acc = acc + lax.dot_general(block_ref[chip], weight, NT, preferred_element_type=F32)
+    return acc
+
+
+def own_kernel(own_ref, w_ref, acc_ref):
+    acc_ref[...] = parity_dot(own_ref, w_ref, lax.axis_index("mp") % 2)
+
+
+def moved_kernel(acc_ref, pair_ref, w_ref, rows_hbm, send_ref, wide_ref, rows_ref, sem):
+    fetch = pltpu.make_async_copy(rows_hbm, rows_ref, sem)
+    fetch.start()
+    grad = acc_ref[...] + parity_dot(pair_ref, w_ref, 1 - lax.axis_index("mp") % 2)
+    fetch.wait()
     wide_ref[...] = rows_ref[...].astype(F32)
     to_octets(send_ref, wide_ref, 6, [grad[:, :HD], grad[:, HD:]])
 
@@ -148,16 +157,16 @@
         acc_ref[...] = jnp.zeros_like(acc_ref)
 
     acc = acc_ref[...]
-    for b in range(blocks):
-        acc = acc + lax.dot_general(
-            og_ref[b], w_ref[:, b * cols : (b + 1) * cols], NT, preferred_element_type=F32
-        )
+    for b in range(0, blocks, 2):
+        rows = jnp.concatenate([og_ref[i] for i in range(b, min(b + 2, blocks))], 1)
+        weight = w_ref[:, b * cols : b * cols + rows.shape[1]]
+        acc = acc + lax.dot_general(rows, weight, NT, preferred_element_type=F32)
     acc_ref[...] = acc
 
 
 def local_kernel(
     n_dp, tok, img, og_ref, w_ref, rows_ref, valid_ref, pos_ref,
-    dq_ref, dk_ref, dv_ref, acc_ref,
+    grads_ref, acc_ref,
 ):
     project(og_ref, w_ref, acc_ref)
 
@@ -183,31 +192,41 @@
             parts.append([jnp.concatenate(p, 0) for p in zip(*pieces)])
         pos = pos_ref[:, 0:1] - slots
         hot = one_hot(iota((tok, KEPT), 1) == pos)
-        for out, name in zip((dq_ref, dk_ref, dv_ref), range(3)):
-            out[...] = pick(hot, jnp.concatenate([parts[0][name], parts[1][name]], 1))
-
-
-def merge_kernel(back_ref, pos_ref, q_ref, k_ref, v_ref, dq_ref, dk_ref, dv_ref, wide_ref):
-    tok = q_ref.shape[0]
+        for name in range(3):
+            grads_ref[name] = pick(hot, jnp.concatenate([parts[0][name], parts[1][name]], 1))
+
+
+def merge_kernel(back_ref, pos_hbm, kept_hbm, dq_ref, dk_ref, dv_ref, wide_ref, pos_ref, kept_ref, sems):
+    fetches = [
+        pltpu.make_async_copy(pos_hbm, pos_ref, sems.at[0]),
+        pltpu.make_async_copy(kept_hbm, kept_ref, sems.at[1]),
+    ]
+    for fetch in fetches:
+        fetch.start()
+    back = from_octets(back_ref, wide_ref, 6)
+    fetches[0].wait()
     slots = back_ref.shape[0] // OCT
-    hot = one_hot(iota((tok, slots), 1) == pos_ref[:, 0:1])
-    back = from_octets(back_ref, wide_ref, 6)
-    for i, (kept_ref, out) in enumerate(((q_ref, dq_ref), (k_ref, dk_ref), (v_ref, dv_ref))):
-        rows = jnp.concatenate(back[2 * i : 2 * i + 2], 1)
-        out[...] = kept_ref[...] + pick(hot, rows)
+    hot = one_hot(iota((pos_ref.shape[0], slots), 1) == pos_ref[:, 0:1])
+    added = [pick(hot, jnp.concatenate(back[2 * i : 2 * i + 2], 1)) for i in range(3)]
+    fetches[1].wait()
+    for i, out in enumerate((dq_ref, dk_ref, dv_ref)):
+        out[...] = kept_ref[i] + added[i]
 
 
 def sds(shape, dtype):
     return jax.ShapeDtypeStruct(shape, dtype)
 
 
-def call(kernel, ins, outs, name, vmem=56, flops=0, scratch=()):
+def call(kernel, ins, outs, name, vmem=56, flops=0, scratch=(), in_hbm=()):
     many = isinstance(outs, tuple)
     return pl.pallas_call(
         kernel,
         out_shape=outs,
         grid=(1,),
-        in_specs=[whole(x) for x in ins],
+        in_specs=[
+            pl.BlockSpec(memory_space=pltpu.HBM) if i in in_hbm else whole(x)
+            for i, x in enumerate(ins)
+        ],
         out_specs=tuple(whole(x) for x in outs) if many else whole(outs),
         scratch_shapes=scratch,
         **options(ins, outs if many else (outs,), name, vmem, flops),
@@ -273,13 +292,17 @@
         scratch=wide,
     )
     kept_all = lax.all_gather(after(og_kept, og_chips), "mp", axis=0)
+    own = call(
+        own_kernel, (og_chips, out_weight), sds((slots, cols), F32), "own", 24, 10**9
+    )
     moved_send = call(
         moved_kernel,
-        (og_chips, og_pair, out_weight, send),
+        (own, og_pair, out_weight, send),
         sds((exch, HD), BF16),
         "moved",
         24,
-        scratch=wide,
+        scratch=wide + [pltpu.VMEM((exch, HD), BF16), pltpu.SemaphoreType.DMA],
+        in_hbm=(3,),
     )
     rows_in = exchange(moved_send)
     back_send = call(
@@ -292,7 +315,7 @@
     )
     back = exchange(back_send)
     ins = (kept_all, out_weight, rows_kept, kept_used, pos_col)
-    outs = (sds((tok, cols), BF16),) * 3
+    outs = sds((3, tok, cols), BF16)
     per_step = 4 if n_mp % 4 == 0 else 1
     kept_grads = pl.pallas_call(
         functools.partial(local_kernel, n_dp, tok, img),
@@ -303,17 +326,23 @@
             pl.BlockSpec((cols, per_step * feat), lambda i: (0, i)),
             *(whole(x) for x in ins[2:]),
         ],
-        out_specs=tuple(whole(x) for x in outs),
+        out_specs=whole(outs),
         scratch_shapes=[pltpu.VMEM((KEPT, cols), F32)],
-        **options(ins, outs, "kept", 56, 2 * KEPT * n_mp * feat * cols),
+        **options(ins, (outs,), "kept", 56, 2 * KEPT * n_mp * feat * cols),
     )(*ins)
     return call(
         merge_kernel,
-        (back, pos_col) + kept_grads,
+        (back, pos_col, kept_grads),
         (sds((tok, cols), BF16),) * 3,
         "merge",
         56,
-        scratch=wide,
+        scratch=wide
+        + [
+            pltpu.VMEM((tok, HD), jnp.int32),
+            pltpu.VMEM((3, tok, cols), BF16),
+            pltpu.SemaphoreType.DMA((2,)),
+        ],
+        in_hbm=(1, 2),
     )
 
 

time: 131 us -> 129 us (0.985)
  waiting for transfers between devices: 37.5 us -> 35.8 us
    all_gather x1, waiting for transfers between devices: 1.94 us -> 4.38 us  [local(): kept_all = lax.all_gather(after(og_kept, og_chips), 'mp', axis=0)]
    all_to_all x1, waiting for transfers between devices: 4.04 us -> 1.83 us  [exchange(): lax.all_to_all(shaped, 'dp', split_axis=0, concat_axis=0, tiled=True)]
    ppermute x1, waiting for transfers between devices: 2.66 us -> 0.69 us  [local(): og_pair = lax.ppermute(og_chips, 'mp', swap)]
    pallas_call x5 -> x6, Pallas kernels: 12.8 us -> 13.9 us  [call(): pl.pallas_call(kernel, out_shape=outs, grid=(1,), in_specs=[pl.BlockSpec(...]
  transfers between devices with their start and end apart: 4 -> 4, of which waited for: 4 -> 4; matrix products, arithmetic and copies ran while one was open for 0% -> 0% of each run, Pallas kernels for 12% -> 13%
where the time goes in v6:
time: 129 us; the launch traced here: 127 us
  waiting for transfers between devices  35.8 us (28%)
  blocking collectives  28 us (22%)
  starting transfers between devices  26.6 us (21%)
  Pallas kernels  22 us (17%)
  between operations  14.1 us (11%)
    all_to_all x1, waiting for transfers between devices, local(): lax.all_to_all(og_moved, 'mp', split_axis=0, concat_axis=0, tiled=True, a...  28.9 us
    all_to_all x1, blocking collectives, exchange(): lax.all_to_all(shaped, 'dp', split_axis=0, concat_axis=0, tiled=True)  28 us
    all_to_all x1, starting transfers between devices, local(): lax.all_to_all(og_moved, 'mp', split_axis=0, concat_axis=0, tiled=True, a...  17.5 us
    pallas_call x6, Pallas kernels, call(): pl.pallas_call(kernel, out_shape=outs, grid=(1,), in_specs=[pl.BlockSpec(...  13.9 us
    pallas_call x1, Pallas kernels, local(): pl.pallas_call(functools.partial(local_kernel, n_dp, tok, img), out_shape...  8.15 us
    all_to_all x1, starting transfers between devices, exchange(): lax.all_to_all(shaped, 'dp', split_axis=0, concat_axis=0, tiled=True)  6.54 us
    all_gather x1, waiting for transfers between devices, local(): kept_all = lax.all_gather(after(og_kept, og_chips), 'mp', axis=0)  4.38 us
  transfers between devices with their start and end apart: 4, of which 4 were waited for; matrix products, arithmetic and copies ran while one was open for 0% of the time, Pallas kernels for 13%

profile of v6, /device:TPU:1, one launch (start us, length us, event | category | flops | bytes accessed | tf_op | source)
XLA Modules:
  0.0 127.2 jit_solution(14517976291456782115)
XLA Ops:
  7.2 2.7 %plan.1 = (s32[8,512]{1,0:T(8,128)}, bf16[8,192,384]{2,1,0:T(8,128)(2,1)}) custom-call(s32[1,512]{1,0:T(1,128)} %bitcast.12, s32[1,512]{1,0:T(1,128)} %bitcast.13, s32[1,3]{1,0:T(1,128)} %bitcast.14, bf16[512,384]{1,0:T(8,128)(2,1)} %og_ref.3), custom_call_target="tpu_custom_call" | custom-call | bytes 1593356 | tf_op jit(solution)/shard_map/plan/pallas_call | solution.py:222
  9.8 0.0 copy-start
  9.9 17.5 %all-to-all-start = ((bf16[8,192,384]{2,1,0:T(8,128)(2,1)}), bf16[8,192,384]{2,1,0:T(8,128)(2,1)}, u32[]{:S(2)}, u32[]{:S(2)}) async-start(bf16[8,192,384]{2,1,0:T(8,128)(2,1)} %get-tuple-element.12), calls=%async_computation | async-start | bytes 2359296 | tf_op jit(solution)/shard_map/all_to_all | solution.py:276
  27.3 0.0 all-gather.3.cloned.1.call-start
  27.4 3.2 %pack.1 = (bf16[1536,128]{1,0:T(8,128)(2,1)}, bf16[400,384]{1,0:T(8,128)(2,1)}, bf16[400,768]{1,0:T(8,128)(2,1)}, f32[192,128]{1,0:T(8,128)}, f32[144,128]{1,0:T(8,128)}, /*index=5*/s32[512,128]{1,0:T(8,128)}) custom-call(s32[8,512]{1,0:T(8,128)} %get-tuple-element.13.pos_ref, bf16[512,384]{1,0:T(8,128)(2,1)} %og_ref.3, bf16[512,256]{1,0:T(8,128)(2,1)} %q_ref.1, ...), custom_call_target="tpu_custom_call" | custom-call | bytes 2945024 | tf_op jit(solution)/shard_map/pack/pallas_call | solution.py:222
  30.6 28.9 %all-to-all-done.own_ref = bf16[8,192,384]{2,1,0:T(8,128)(2,1)} async-done(((bf16[8,192,384]{2,1,0:T(8,128)(2,1)}), bf16[8,192,384]{2,1,0:T(8,128)(2,1)}, u32[]{:S(2)}, u32[]{:S(2)}) %all-to-all-start) | async-done | bytes 1179680 | tf_op jit(solution)/shard_map/all_to_all | solution.py:276
  59.5 0.0 all-gather.3.cloned.1.call-update
  59.5 0.0 copy-start.1
  59.5 2.5 %collective-permute-start = (bf16[8,192,384]{2,1,0:T(8,128)(2,1)}, bf16[8,192,384]{2,1,0:T(8,128)(2,1)S(1)}, u32[]{:S(2)}, u32[]{:S(2)}) collective-permute-start(bf16[8,192,384]{2,1,0:T(8,128)(2,1)} %all-to-all-done.own_ref), channel_id=1, source_target_pairs={{0,1},{1,0},{2,3},{3,2},{4,5},{5,4},{6,7},{7,6},{8,9},{9,8},{10,11... | collective-permute-start | bytes 3538952 | tf_op jit(solution)/shard_map/ppermute | solution.py:279
  62.1 0.0 copy-done
  62.1 2.0 %own.1.acc_ref = f32[192,256]{1,0:T(8,128)S(1)} custom-call(bf16[8,192,384]{2,1,0:T(8,128)(2,1)} %all-to-all-done.own_ref, bf16[256,6144]{1,0:T(8,128)(2,1)S(1)} %copy-done), custom_call_target="tpu_custom_call" | custom-call | flops 1000000000 | bytes 4521984 | tf_op jit(solution)/shard_map/own/pallas_call | solution.py:222
  64.0 0.7 collective-permute-done.pair_ref
  64.7 0.0 copy-done.1
  64.7 0.0 copy-start.2
  64.7 1.0 moved.1
  65.8 28.0 %all_to_all.15 = bf16[64,24,128]{2,1,0:T(8,128)(2,1)S(1)} all-to-all(bf16[64,24,128]{2,1,0:T(8,128)(2,1)S(1)} %bitcast.9), channel_id=1, replica_groups=mesh['dp'=64,'mp'=16] {'dp'}, dimensions={0} | all-to-all | bytes 786432 | tf_op jit(solution)/shard_map/all_to_all | solution.py:265
  93.7 0.0 copy-done.2
  93.7 1.7 %remote.1 = bf16[1536,128]{1,0:T(8,128)(2,1)} custom-call(bf16[1536,128]{1,0:T(8,128)(2,1)S(1)} %bitcast.8, f32[192,128]{1,0:T(8,128)S(1)} %copy-done.2), custom_call_target="tpu_custom_call" | custom-call | bytes 884736 | tf_op jit(solution)/shard_map/remote/pallas_call | solution.py:222
  95.4 6.5 %all-to-all-start.2 = ((bf16[64,24,128]{2,1,0:T(8,128)(2,1)}), bf16[64,24,128]{2,1,0:T(8,128)(2,1)S(1)}, u32[]{:S(2)}, u32[]{:S(2)}) async-start(bf16[64,24,128]{2,1,0:T(8,128)(2,1)} %bitcast.5), calls=%async_computation.2 | async-start | bytes 786432 | tf_op jit(solution)/shard_map/all_to_all | solution.py:265
  102.0 4.4 %all-gather.3.cloned.1.call-done = bf16[6400,384]{1,0:T(8,128)(2,1)} async-done(((bf16[400,384]{1,0:T(8,128)(2,1)}), bf16[6400,384]{1,0:T(8,128)(2,1)}) %all-gather.3.cloned.1.call-update) | async-done | bytes 4915216 | tf_op jit(solution)/shard_map/all_gather | solution.py:294
  106.4 8.1 %kept.1.kept_hbm = bf16[3,512,256]{2,1,0:T(8,128)(2,1)} custom-call(bf16[16,400,384]{2,1,0:T(8,128)(2,1)} %bitcast.10, bf16[256,6144]{1,0:T(8,128)(2,1)} %w_ref.5, bf16[400,768]{1,0:T(8,128)(2,1)} %get-tuple-element.19.rows_ref, f32[144,128]{1,0:T(8,128)} %get-tuple-element.20.valid_ref, s32[512,128]{1,0:T(8,128)} %get-tuple-element.16.pos_ref.pos_hbm), custom_call_target="tpu_custom_call" | custom-call | flops 1258291200 | bytes 9797632 | tf_op jit(solution)/shard_map/kept/pallas_call | solution.py:320
  114.5 1.8 %all-to-all-done.2 = bf16[64,24,128]{2,1,0:T(8,128)(2,1)S(1)} async-done(((bf16[64,24,128]{2,1,0:T(8,128)(2,1)}), bf16[64,24,128]{2,1,0:T(8,128)(2,1)S(1)}, u32[]{:S(2)}, u32[]{:S(2)}) %all-to-all-start.2) | async-done | bytes 393248 | tf_op jit(solution)/shard_map/all_to_all | solution.py:265
  116.3 0.0 copy-start.3
  116.3 0.7 copy-done.3
  117.1 3.3 %merge.1 = (bf16[512,256]{1,0:T(8,128)(2,1)}, bf16[512,256]{1,0:T(8,128)(2,1)}, bf16[512,256]{1,0:T(8,128)(2,1)}) custom-call(bf16[1536,128]{1,0:T(8,128)(2,1)} %bitcast.11, s32[512,128]{1,0:T(8,128)} %get-tuple-element.16.pos_ref.pos_hbm, bf16[3,512,256]{2,1,0:T(8,128)(2,1)} %kept.1.kept_hbm), custom_call_target="tpu_custom_call" | custom-call | bytes 2228224 | tf_op jit(solution)/shard_map/merge/pallas_call | solution.py:222
Async XLA Ops:
  9.8 52.2 %copy-start = (bf16[256,6144]{1,0:T(8,128)(2,1)S(1)}, bf16[256,6144]{1,0:T(8,128)(2,1)}, u32[]{:S(2)}) copy-start(bf16[256,6144]{1,0:T(8,128)(2,1)} %w_ref.5) | copy-start | bytes 9437188
  9.9 49.6 %all-to-all-start = ((bf16[8,192,384]{2,1,0:T(8,128)(2,1)}), bf16[8,192,384]{2,1,0:T(8,128)(2,1)}, u32[]{:S(2)}, u32[]{:S(2)}) async-start(bf16[8,192,384]{2,1,0:T(8,128)(2,1)} %get-tuple-element.12), calls=%async_computation | async-start | bytes 2359296 | tf_op jit(solution)/shard_map/all_to_all | solution.py:276
  27.3 79.0 %all-gather.3.cloned.1.call-start = ((), (), s32[]{:S(2)}) async-start(), calls=%async_computation.3 | async-start | bytes 5222400 | tf_op jit(solution)/shard_map/all_gather | solution.py:294
  59.5 5.2 %copy-start.1 = (bf16[1536,128]{1,0:T(8,128)(2,1)S(1)}, bf16[1536,128]{1,0:T(8,128)(2,1)}, u32[]{:S(2)}) copy-start(bf16[1536,128]{1,0:T(8,128)(2,1)} %get-tuple-element.14.rows_hbm) | copy-start | bytes 1179652
  59.5 5.2 %collective-permute-start = (bf16[8,192,384]{2,1,0:T(8,128)(2,1)}, bf16[8,192,384]{2,1,0:T(8,128)(2,1)S(1)}, u32[]{:S(2)}, u32[]{:S(2)}) collective-permute-start(bf16[8,192,384]{2,1,0:T(8,128)(2,1)} %all-to-all-done.own_ref), channel_id=1, source_target_pairs={{0,1},{1,0},{2,3},{3,2},{4,5},{5,4},{6,7},{7,6},{8,9},{9,8},{10,11... | collective-permute-start | bytes 3538952 | tf_op jit(solution)/shard_map/ppermute | solution.py:279
  64.7 29.0 %copy-start.2 = (f32[192,128]{1,0:T(8,128)S(1)}, f32[192,128]{1,0:T(8,128)}, u32[]{:S(2)}) copy-start(f32[192,128]{1,0:T(8,128)} %get-tuple-element.15.valid_ref) | copy-start | bytes 294916
  95.4 20.9 %all-to-all-start.2 = ((bf16[64,24,128]{2,1,0:T(8,128)(2,1)}), bf16[64,24,128]{2,1,0:T(8,128)(2,1)S(1)}, u32[]{:S(2)}, u32[]{:S(2)}) async-start(bf16[64,24,128]{2,1,0:T(8,128)(2,1)} %bitcast.5), calls=%async_computation.2 | async-start | bytes 786432 | tf_op jit(solution)/shard_map/all_to_all | solution.py:265
  116.3 0.7 copy-start.3
Sparse Core Ops, SparseCore 0:
  59.6 46.6 all-gather.2

commit v7 on v5

--- a/solution.py
+++ b/solution.py
@@ -320,7 +320,7 @@
     )
     kept_block = lax.all_gather(og_kept, "mp", axis=0, axis_index_groups=pairs)
     og_chips = after(og_chips, kept_block)
-    kept_blocks = in_chunks(kept_block)
+    kept1 = hop(after(kept_block, og_chips))
     mine, pair = call(
         functools.partial(chips_kernel, n_mp),
         (og_chips, out_weight, pair_weight),
@@ -328,8 +328,7 @@
         "chips",
         24,
     )
-    pair = lax.ppermute(pair, "mp", swap)
-    kept1 = [hop(after(x, mine)) for x in kept_blocks]
+    pair = after(lax.ppermute(pair, "mp", swap), kept1)
     moved_send = call(
         moved_kernel,
         (mine, pair, send),
@@ -339,8 +338,19 @@
         scratch=wide,
     )
     rows_in = exchange(moved_send)
-    kept2 = [hop(after(x, moved_send)) for x in kept1]
+    kept1 = in_chunks(after(kept1, moved_send))
+    kept2 = [hop(x) for x in kept1]
     kept3 = [hop(x) for x in kept2]
+    acc, w_late = call(
+        functools.partial(partial_kernel, n_mp),
+        (og_kept, *kept1, *kept2, out_weight, pair_weight),
+        (sds((2, KEPT, cols), F32), sds((2, cols, 3 * feat), BF16)),
+        "partial",
+        56,
+        2 * KEPT * n_mp * feat * cols,
+    )
+    for x in (acc, *kept3):
+        rows_in = after(rows_in, x)
     back_send = call(
         functools.partial(remote_kernel, tok, img),
         (rows_in, used),
@@ -350,15 +360,7 @@
         scratch=wide,
     )
     back = exchange(back_send)
-    kept4 = [opposite(x) for x in kept3]
-    acc, w_late = call(
-        functools.partial(partial_kernel, n_mp),
-        (og_kept, *kept1, *kept2, out_weight, pair_weight),
-        (sds((2, KEPT, cols), F32), sds((2, cols, 3 * feat), BF16)),
-        "partial",
-        56,
-        2 * KEPT * n_mp * feat * cols,
-    )
+    kept4 = [opposite(after(x, back_send)) for x in kept3]
     mine, pair = call(
         last_kernel, (acc, *kept3, *kept4, w_late), (sds((KEPT, cols), F32),) * 2, "last"
     )

time: 139 us -> 146 us (1.050)
  waiting for transfers between devices: 30.5 us -> 36.1 us
    ppermute x8 -> x7, waiting for transfers between devices: 3.91 us -> 9.56 us  [hop(): return lax.ppermute(block, 'mp', ring)]
    ppermute x8 -> x7, starting transfers between devices: 21.8 us -> 18.7 us  [hop(): return lax.ppermute(block, 'mp', ring)]
    ppermute x0 -> x1, starting transfers between devices: none -> 2.86 us  [local(): pair = after(lax.ppermute(pair, 'mp', swap), kept1)]
    ppermute x2 -> x1, starting transfers between devices: 7.5 us -> 8.72 us  [local(): pair = lax.ppermute(pair, 'mp', swap)]
  transfers between devices with their start and end apart: 14 -> 13, of which waited for: 4 -> 5; matrix products, arithmetic and copies ran while one was open for 1% -> 1% of each run, Pallas kernels for 15% -> 15%
where the time goes in v7:
time: 146 us; the launch traced here: 145 us
  starting transfers between devices  75.5 us (52%)
  waiting for transfers between devices  36.1 us (25%)
  Pallas kernels  25.1 us (17%)
  blocking collectives  3.87 us (3%)
  local copies, waits for them, and re-layouts  3.8 us (3%)
    pallas_call x9, Pallas kernels, call(): pl.pallas_call(kernel, out_shape=outs, grid=(1,), in_specs=[whole(x) for...  25.1 us
    all_to_all x1, waiting for transfers between devices, local(): lax.all_to_all(og_moved, 'mp', split_axis=0, concat_axis=0, tiled=True, a...  25 us
    all_to_all x2, starting transfers between devices, exchange(): lax.all_to_all(shaped, 'dp', split_axis=0, concat_axis=0, tiled=True)  24.6 us
    ppermute x7, starting transfers between devices, hop(): return lax.ppermute(block, 'mp', ring)  18.7 us
    ppermute x1, starting transfers between devices, local(): pair_weight = lax.ppermute(out_weight, 'mp', swap)  16.1 us
    ppermute x7, waiting for transfers between devices, hop(): return lax.ppermute(block, 'mp', ring)  9.56 us
    ppermute x1, starting transfers between devices, local(): pair = lax.ppermute(pair, 'mp', swap)  8.72 us
    all_to_all x1, starting transfers between devices, local(): lax.all_to_all(og_moved, 'mp', split_axis=0, concat_axis=0, tiled=True, a...  4.54 us
  transfers between devices with their start and end apart: 13, of which 5 were waited for; matrix products, arithmetic and copies ran while one was open for 1% of the time, Pallas kernels for 15%

profile of v7, /device:TPU:1, one launch (start us, length us, event | category | flops | bytes accessed | tf_op | source)
XLA Modules:
  0.0 145.3 jit_solution(17227047600060922114)
XLA Ops:
  0.6 16.1 %collective-permute-start = (bf16[256,6144]{1,0:T(8,128)(2,1)}, bf16[256,6144]{1,0:T(8,128)(2,1)}, u32[]{:S(2)}, u32[]{:S(2)}) collective-permute-start(bf16[256,6144]{1,0:T(8,128)(2,1)} %refs_4_.1), channel_id=1, source_target_pairs={{0,1},{1,0},{2,3},{3,2},{4,5},{5,4},{6,7},{7,6},{8,9},{9,8},{10,11... | collective-permute-start | bytes 9437192 | tf_op jit(solution)/shard_map/ppermute | solution.py:297
  16.7 2.7 %plan.1 = (s32[8,512]{1,0:T(8,128)}, bf16[8,192,384]{2,1,0:T(8,128)(2,1)}) custom-call(s32[1,512]{1,0:T(1,128)} %bitcast.11, s32[1,512]{1,0:T(1,128)} %bitcast.12, s32[1,3]{1,0:T(1,128)} %bitcast.13, bf16[512,384]{1,0:T(8,128)(2,1)} %og_ref.3), custom_call_target="tpu_custom_call" | custom-call | bytes 1593356 | tf_op jit(solution)/shard_map/plan/pallas_call | solution.py:241
  19.4 4.5 %all-to-all-start = ((bf16[8,192,384]{2,1,0:T(8,128)(2,1)}), bf16[8,192,384]{2,1,0:T(8,128)(2,1)}, u32[]{:S(2)}, u32[]{:S(2)}) async-start(bf16[8,192,384]{2,1,0:T(8,128)(2,1)} %get-tuple-element.29), calls=%async_computation | async-start | bytes 2359296 | tf_op jit(solution)/shard_map/all_to_all | solution.py:304
  23.9 3.2 %pack.1 = (bf16[1536,128]{1,0:T(8,128)(2,1)}, bf16[400,384]{1,0:T(8,128)(2,1)}, bf16[400,768]{1,0:T(8,128)(2,1)}, f32[192,128]{1,0:T(8,128)}, f32[144,128]{1,0:T(8,128)}, /*index=5*/s32[512,128]{1,0:T(8,128)}) custom-call(s32[8,512]{1,0:T(8,128)} %get-tuple-element.30.pos_ref, bf16[512,384]{1,0:T(8,128)(2,1)} %og_ref.3, bf16[512,256]{1,0:T(8,128)(2,1)} %q_ref.1, ...), custom_call_target="tpu_custom_call" | custom-call | bytes 2945024 | tf_op jit(solution)/shard_map/pack/pallas_call | solution.py:241
  27.2 3.9 %all-gather = bf16[800,384]{1,0:T(8,128)(2,1)} all-gather(bf16[400,384]{1,0:T(8,128)(2,1)} %get-tuple-element.31.own_ref), channel_id=2, replica_groups={{0,1},{2,3},{4,5},{6,7},{8,9},{10,11},{12,13},{14,15},{16,17},{18,19},{..., dimensions={0}, use_global_device_ids=true | all-gather | bytes 921600 | tf_op jit(solution)/shard_map/all_gather | solution.py:321
  31.1 25.0 %all-to-all-done.og_ref = bf16[8,192,384]{2,1,0:T(8,128)(2,1)} async-done(((bf16[8,192,384]{2,1,0:T(8,128)(2,1)}), bf16[8,192,384]{2,1,0:T(8,128)(2,1)}, u32[]{:S(2)}, u32[]{:S(2)}) %all-to-all-start) | async-done | bytes 1179680 | tf_op jit(solution)/shard_map/all_to_all | solution.py:304
  56.0 0.0 copy-start.4
  56.0 2.0 %collective-permute-start.2 = (bf16[2,400,384]{2,1,0:T(8,128)(2,1)}, bf16[2,400,384]{2,1,0:T(8,128)(2,1)S(1)}, u32[]{:S(2)}, u32[]{:S(2)}) collective-permute-start(bf16[2,400,384]{2,1,0:T(8,128)(2,1)} %bitcast.10), channel_id=1, source_target_pairs={{0,2},{1,15},{2,4},{3,1},{4,6},{5,3},{6,8},{7,5},{8,10},{9,7},{10,... | collective-permute-start | bytes 1843208 | tf_op jit(solution)/shard_map/ppermute | solution.py:289
  58.1 0.0 collective-permute-done.w_pair_ref.refs_5_
  58.1 0.0 copy-done
  58.1 3.5 %chips.1 = (f32[192,256]{1,0:T(8,128)S(1)}, f32[192,256]{1,0:T(8,128)S(1)}) custom-call(bf16[8,192,384]{2,1,0:T(8,128)(2,1)} %all-to-all-done.og_ref, bf16[256,6144]{1,0:T(8,128)(2,1)S(1)} %copy-done, bf16[256,6144]{1,0:T(8,128)(2,1)} %collective-permute-done.w_pair_ref.refs_5_), custom_call_target="tpu_custom_call" | custom-call | bytes 7864320 | tf_op jit(solution)/shard_map/chips/pallas_call | solution.py:241
  61.6 2.9 %collective-permute-start.1 = (f32[192,256]{1,0:T(8,128)S(1)}, f32[192,256]{1,0:T(8,128)S(1)}, u32[]{:S(2)}, u32[]{:S(2)}) collective-permute-start(f32[192,256]{1,0:T(8,128)S(1)} %get-tuple-element.34), channel_id=1, source_target_pairs={{0,1},{1,0},{2,3},{3,2},{4,5},{5,4},{6,7},{7,6},{8,9},{9,8},{10,11... | collective-permute-start | bytes 589832 | tf_op jit(solution)/shard_map/ppermute | solution.py:331
  64.5 3.0 %collective-permute-done.2 = bf16[2,400,384]{2,1,0:T(8,128)(2,1)S(1)} collective-permute-done((bf16[2,400,384]{2,1,0:T(8,128)(2,1)}, bf16[2,400,384]{2,1,0:T(8,128)(2,1)S(1)}, u32[]{:S(2)}, u32[]{:S(2)}) %collective-permute-start.2) | collective-permute-done | bytes 614432 | tf_op jit(solution)/shard_map/ppermute | solution.py:289
  67.6 0.0 copy-start.11
  67.6 0.0 collective-permute-done.1.pair_ref
  67.6 0.0 copy-done.4
  67.6 0.9 moved.1
  68.5 0.0 copy-done.11
  68.5 12.8 %all-to-all-start.1 = ((bf16[64,24,128]{2,1,0:T(8,128)(2,1)}), bf16[64,24,128]{2,1,0:T(8,128)(2,1)S(1)}, u32[]{:S(2)}, u32[]{:S(2)}) async-start(bf16[64,24,128]{2,1,0:T(8,128)(2,1)} %bitcast.4), calls=%async_computation.1 | async-start | bytes 786432 | tf_op jit(solution)/shard_map/all_to_all | solution.py:283
  81.3 1.0 slice.6.refs_0_
  82.3 0.0 copy-start.7
  82.3 2.8 %collective-permute-start.3 = (bf16[2,208,384]{2,1,0:T(8,128)(2,1)S(1)}, bf16[2,208,384]{2,1,0:T(8,128)(2,1)S(1)}, u32[]{:S(2)}, u32[]{:S(2)}) collective-permute-start(bf16[2,208,384]{2,1,0:T(8,128)(2,1)S(1)} %slice.6.refs_0_), channel_id=1, source_target_pairs={{0,2},{1,15},{2,4},{3,1},{4,6},{5,3},{6,8},{7,5},{8,10},{9,7},{10,... | collective-permute-start | bytes 958472 | tf_op jit(solution)/shard_map/ppermute | solution.py:289
  85.1 1.0 slice.7.refs_1_
  86.1 0.0 copy-start.8
  86.2 1.9 %collective-permute-start.4 = (bf16[2,192,384]{2,1,0:T(8,128)(2,1)S(1)}, bf16[2,192,384]{2,1,0:T(8,128)(2,1)S(1)}, u32[]{:S(2)}, u32[]{:S(2)}) collective-permute-start(bf16[2,192,384]{2,1,0:T(8,128)(2,1)S(1)} %slice.7.refs_1_), channel_id=1, source_target_pairs={{0,2},{1,15},{2,4},{3,1},{4,6},{5,3},{6,8},{7,5},{8,10},{9,7},{10,... | collective-permute-start | bytes 884744 | tf_op jit(solution)/shard_map/ppermute | solution.py:289
  88.1 2.2 %collective-permute-done.3.refs_2_ = bf16[2,208,384]{2,1,0:T(8,128)(2,1)S(1)} collective-permute-done((bf16[2,208,384]{2,1,0:T(8,128)(2,1)S(1)}, bf16[2,208,384]{2,1,0:T(8,128)(2,1)S(1)}, u32[]{:S(2)}, u32[]{:S(2)}) %collective-permute-start.3) | collective-permute-done | bytes 319520 | tf_op jit(solution)/shard_map/ppermute | solution.py:289
  90.3 0.0 copy-start.12
  90.3 4.0 %collective-permute-start.5 = (bf16[2,208,384]{2,1,0:T(8,128)(2,1)S(1)}, bf16[2,208,384]{2,1,0:T(8,128)(2,1)S(1)}, u32[]{:S(2)}, u32[]{:S(2)}) collective-permute-start(bf16[2,208,384]{2,1,0:T(8,128)(2,1)S(1)} %collective-permute-done.3.refs_2_), channel_id=1, source_target_pairs={{0,2},{1,15},{2,4},{3,1},{4,6},{5,3},{6,8},{7,5},{8,10},{9,7},{10,... | collective-permute-start | bytes 958472 | tf_op jit(solution)/shard_map/ppermute | solution.py:289
  94.4 0.0 collective-permute-done.4.refs_3_
  94.4 0.0 copy-start.13
  94.4 3.1 %collective-permute-start.6 = (bf16[2,192,384]{2,1,0:T(8,128)(2,1)S(1)}, bf16[2,192,384]{2,1,0:T(8,128)(2,1)S(1)}, u32[]{:S(2)}, u32[]{:S(2)}) collective-permute-start(bf16[2,192,384]{2,1,0:T(8,128)(2,1)S(1)} %collective-permute-done.4.refs_3_), channel_id=1, source_target_pairs={{0,2},{1,15},{2,4},{3,1},{4,6},{5,3},{6,8},{7,5},{8,10},{9,7},{10,... | collective-permute-start | bytes 884744 | tf_op jit(solution)/shard_map/ppermute | solution.py:289
  97.6 0.0 copy-done.7
  97.6 0.0 copy-done.8
  97.6 0.0 copy-done.12
  97.6 0.0 copy-done.13
  97.6 0.0 copy-start.5
  97.6 6.0 %partial.1 = (f32[2,400,256]{2,1,0:T(8,128)}, bf16[2,256,1152]{2,1,0:T(8,128)(2,1)}) custom-call(bf16[400,384]{1,0:T(8,128)(2,1)} %get-tuple-element.31.own_ref, bf16[2,208,384]{2,1,0:T(8,128)(2,1)} %copy-done.7, bf16[2,192,384]{2,1,0:T(8,128)(2,1)} %copy-done.8, bf16[2,208,384]{2,1,0:T(8,128)(2,1)} %copy-done.12, bf16[2,192,384]{2,1,0:T(8,128)(2,1)} %copy-done.13, ...), custom_call_target="tpu_custom_call" | custom-call | flops 1258291200 | bytes 9826304 | tf_op jit(solution)/shard_map/partial/pallas_call | solution.py:241
  103.6 0.0 all-to-all-done.1
  103.6 0.0 collective-permute-done.5.refs_0_
  103.6 0.0 copy-start.9
  103.7 0.0 collective-permute-done.6.refs_1_
  103.7 0.0 copy-start.10
  103.7 0.0 copy-done.5
  103.7 1.7 %remote.1 = bf16[1536,128]{1,0:T(8,128)(2,1)} custom-call(bf16[1536,128]{1,0:T(8,128)(2,1)S(1)} %bitcast.8, f32[192,128]{1,0:T(8,128)S(1)} %copy-done.5), custom_call_target="tpu_custom_call" | custom-call | bytes 884736 | tf_op jit(solution)/shard_map/remote/pallas_call | solution.py:241
  105.4 11.8 %all-to-all-start.2 = ((bf16[64,24,128]{2,1,0:T(8,128)(2,1)}), bf16[64,24,128]{2,1,0:T(8,128)(2,1)S(1)}, u32[]{:S(2)}, u32[]{:S(2)}) async-start(bf16[64,24,128]{2,1,0:T(8,128)(2,1)} %bitcast.6), calls=%async_computation.2 | async-start | bytes 786432 | tf_op jit(solution)/shard_map/all_to_all | solution.py:283
  117.3 2.8 %collective-permute-start.7 = (bf16[1,208,384]{2,1,0:T(8,128)(2,1)S(1)}, bf16[1,208,384]{2,1,0:T(8,128)(2,1)S(1)}, u32[]{:S(2)}, u32[]{:S(2)}) collective-permute-start(bf16[1,208,384]{2,1,0:T(8,128)(2,1)S(1)} %constant_dynamic-slice_fusion.1), channel_id=1, source_target_pairs={{0,2},{1,15},{2,4},{3,1},{4,6},{5,3},{6,8},{7,5},{8,10},{9,7},{10,... | collective-permute-start | bytes 479240 | tf_op jit(solution)/shard_map/ppermute | solution.py:289
  120.1 1.9 %collective-permute-start.8 = (bf16[1,192,384]{2,1,0:T(8,128)(2,1)S(1)}, bf16[1,192,384]{2,1,0:T(8,128)(2,1)S(1)}, u32[]{:S(2)}, u32[]{:S(2)}) collective-permute-start(bf16[1,192,384]{2,1,0:T(8,128)(2,1)S(1)} %constant_dynamic-slice_fusion), channel_id=1, source_target_pairs={{0,2},{1,15},{2,4},{3,1},{4,6},{5,3},{6,8},{7,5},{8,10},{9,7},{10,... | collective-permute-start | bytes 442376 | tf_op jit(solution)/shard_map/ppermute | solution.py:289
  122.0 4.3 %collective-permute-done.8.refs_3_ = bf16[1,192,384]{2,1,0:T(8,128)(2,1)S(1)} collective-permute-done((bf16[1,192,384]{2,1,0:T(8,128)(2,1)S(1)}, bf16[1,192,384]{2,1,0:T(8,128)(2,1)S(1)}, u32[]{:S(2)}, u32[]{:S(2)}) %collective-permute-start.8) | collective-permute-done | bytes 147488 | tf_op jit(solution)/shard_map/ppermute | solution.py:289
  126.3 0.0 copy-start.15
  126.3 0.0 collective-permute-done.7.refs_2_
  126.3 0.0 copy-done.9
  126.3 0.0 copy-done.10
  126.3 0.6 copy-done.15
  127.0 0.1 copy-done.14
  127.0 3.6 %last.1 = (f32[400,256]{1,0:T(8,128)}, f32[400,256]{1,0:T(8,128)}) custom-call(f32[2,400,256]{2,1,0:T(8,128)} %get-tuple-element.39.acc_ref, bf16[2,208,384]{2,1,0:T(8,128)(2,1)} %copy-done.9, bf16[2,192,384]{2,1,0:T(8,128)(2,1)} %copy-done.10, bf16[1,208,384]{2,1,0:T(8,128)(2,1)} %copy-done.14, bf16[1,192,384]{2,1,0:T(8,128)(2,1)} %copy-done.15, ...), custom_call_target="tpu_custom_call" | custom-call | bytes 3739648 | tf_op jit(solution)/shard_map/last/pallas_call | solution.py:241
  130.6 8.7 %collective-permute-start.9 = (f32[400,256]{1,0:T(8,128)}, f32[400,256]{1,0:T(8,128)S(1)}, u32[]{:S(2)}, u32[]{:S(2)}) collective-permute-start(f32[400,256]{1,0:T(8,128)} %get-tuple-element.49), channel_id=1, source_target_pairs={{0,1},{1,0},{2,3},{3,2},{4,5},{5,4},{6,7},{7,6},{8,9},{9,8},{10,11... | collective-permute-start | bytes 1228808 | tf_op jit(solution)/shard_map/ppermute | solution.py:367
  139.4 1.6 %collective-permute-done.9.pair_ref = f32[400,256]{1,0:T(8,128)S(1)} collective-permute-done((f32[400,256]{1,0:T(8,128)}, f32[400,256]{1,0:T(8,128)S(1)}, u32[]{:S(2)}, u32[]{:S(2)}) %collective-permute-start.9) | collective-permute-done | bytes 409632 | tf_op jit(solution)/shard_map/ppermute | solution.py:367
  140.9 0.0 copy-done.1
  140.9 0.0 copy-done.2
  140.9 0.0 copy-done.6
  140.9 1.0 copy-done.3
  141.9 2.1 %kept.1 = (bf16[512,256]{1,0:T(8,128)(2,1)S(1)}, bf16[512,256]{1,0:T(8,128)(2,1)S(1)}, bf16[512,256]{1,0:T(8,128)(2,1)S(1)}) custom-call(f32[400,256]{1,0:T(8,128)S(1)} %copy-done.3, f32[400,256]{1,0:T(8,128)S(1)} %collective-permute-done.9.pair_ref, bf16[400,768]{1,0:T(8,128)(2,1)S(1)} %copy-done.2, f32[144,128]{1,0:T(8,128)S(1)} %copy-done.6, ...), custom_call_target="tpu_custom_call" | custom-call | bytes 2555904 | tf_op jit(solution)/shard_map/kept/pallas_call | solution.py:241
  144.1 0.0 all-to-all-done.2
  144.1 1.2 merge.1
  (8 shorter events, 0.1 us)
Async XLA Ops:
  0.6 57.5 %collective-permute-start = (bf16[256,6144]{1,0:T(8,128)(2,1)}, bf16[256,6144]{1,0:T(8,128)(2,1)}, u32[]{:S(2)}, u32[]{:S(2)}) collective-permute-start(bf16[256,6144]{1,0:T(8,128)(2,1)} %refs_4_.1), channel_id=1, source_target_pairs={{0,1},{1,0},{2,3},{3,2},{4,5},{5,4},{6,7},{7,6},{8,9},{9,8},{10,11... | collective-permute-start | bytes 9437192 | tf_op jit(solution)/shard_map/ppermute | solution.py:297
  19.4 38.7 %copy-start = (bf16[256,6144]{1,0:T(8,128)(2,1)S(1)}, bf16[256,6144]{1,0:T(8,128)(2,1)}, u32[]{:S(2)}) copy-start(bf16[256,6144]{1,0:T(8,128)(2,1)} %refs_4_.1) | copy-start | bytes 9437188
  19.4 36.6 %all-to-all-start = ((bf16[8,192,384]{2,1,0:T(8,128)(2,1)}), bf16[8,192,384]{2,1,0:T(8,128)(2,1)}, u32[]{:S(2)}, u32[]{:S(2)}) async-start(bf16[8,192,384]{2,1,0:T(8,128)(2,1)} %get-tuple-element.29), calls=%async_computation | async-start | bytes 2359296 | tf_op jit(solution)/shard_map/all_to_all | solution.py:304
  56.0 11.5 %copy-start.4 = (bf16[1536,128]{1,0:T(8,128)(2,1)S(1)}, bf16[1536,128]{1,0:T(8,128)(2,1)}, u32[]{:S(2)}) copy-start(bf16[1536,128]{1,0:T(8,128)(2,1)} %get-tuple-element.37.rows_ref) | copy-start | bytes 1179652
  56.0 11.5 %collective-permute-start.2 = (bf16[2,400,384]{2,1,0:T(8,128)(2,1)}, bf16[2,400,384]{2,1,0:T(8,128)(2,1)S(1)}, u32[]{:S(2)}, u32[]{:S(2)}) collective-permute-start(bf16[2,400,384]{2,1,0:T(8,128)(2,1)} %bitcast.10), channel_id=1, source_target_pairs={{0,2},{1,15},{2,4},{3,1},{4,6},{5,3},{6,8},{7,5},{8,10},{9,7},{10,... | collective-permute-start | bytes 1843208 | tf_op jit(solution)/shard_map/ppermute | solution.py:289
  61.6 5.9 %collective-permute-start.1 = (f32[192,256]{1,0:T(8,128)S(1)}, f32[192,256]{1,0:T(8,128)S(1)}, u32[]{:S(2)}, u32[]{:S(2)}) collective-permute-start(f32[192,256]{1,0:T(8,128)S(1)} %get-tuple-element.34), channel_id=1, source_target_pairs={{0,1},{1,0},{2,3},{3,2},{4,5},{5,4},{6,7},{7,6},{8,9},{9,8},{10,11... | collective-permute-start | bytes 589832 | tf_op jit(solution)/shard_map/ppermute | solution.py:331
  67.6 1.0 copy-start.11
  68.5 35.1 %all-to-all-start.1 = ((bf16[64,24,128]{2,1,0:T(8,128)(2,1)}), bf16[64,24,128]{2,1,0:T(8,128)(2,1)S(1)}, u32[]{:S(2)}, u32[]{:S(2)}) async-start(bf16[64,24,128]{2,1,0:T(8,128)(2,1)} %bitcast.4), calls=%async_computation.1 | async-start | bytes 786432 | tf_op jit(solution)/shard_map/all_to_all | solution.py:283
  82.3 15.3 %copy-start.7 = (bf16[2,208,384]{2,1,0:T(8,128)(2,1)}, bf16[2,208,384]{2,1,0:T(8,128)(2,1)S(1)}, u32[]{:S(2)}) copy-start(bf16[2,208,384]{2,1,0:T(8,128)(2,1)S(1)} %slice.6.refs_0_) | copy-start | bytes 958468
  82.3 8.0 %collective-permute-start.3 = (bf16[2,208,384]{2,1,0:T(8,128)(2,1)S(1)}, bf16[2,208,384]{2,1,0:T(8,128)(2,1)S(1)}, u32[]{:S(2)}, u32[]{:S(2)}) collective-permute-start(bf16[2,208,384]{2,1,0:T(8,128)(2,1)S(1)} %slice.6.refs_0_), channel_id=1, source_target_pairs={{0,2},{1,15},{2,4},{3,1},{4,6},{5,3},{6,8},{7,5},{8,10},{9,7},{10,... | collective-permute-start | bytes 958472 | tf_op jit(solution)/shard_map/ppermute | solution.py:289
  86.1 11.4 %copy-start.8 = (bf16[2,192,384]{2,1,0:T(8,128)(2,1)}, bf16[2,192,384]{2,1,0:T(8,128)(2,1)S(1)}, u32[]{:S(2)}) copy-start(bf16[2,192,384]{2,1,0:T(8,128)(2,1)S(1)} %slice.7.refs_1_) | copy-start | bytes 884740
  86.2 8.2 %collective-permute-start.4 = (bf16[2,192,384]{2,1,0:T(8,128)(2,1)S(1)}, bf16[2,192,384]{2,1,0:T(8,128)(2,1)S(1)}, u32[]{:S(2)}, u32[]{:S(2)}) collective-permute-start(bf16[2,192,384]{2,1,0:T(8,128)(2,1)S(1)} %slice.7.refs_1_), channel_id=1, source_target_pairs={{0,2},{1,15},{2,4},{3,1},{4,6},{5,3},{6,8},{7,5},{8,10},{9,7},{10,... | collective-permute-start | bytes 884744 | tf_op jit(solution)/shard_map/ppermute | solution.py:289
  90.3 7.2 %copy-start.12 = (bf16[2,208,384]{2,1,0:T(8,128)(2,1)}, bf16[2,208,384]{2,1,0:T(8,128)(2,1)S(1)}, u32[]{:S(2)}) copy-start(bf16[2,208,384]{2,1,0:T(8,128)(2,1)S(1)} %collective-permute-done.3.refs_2_) | copy-start | bytes 958468
  90.3 13.3 %collective-permute-start.5 = (bf16[2,208,384]{2,1,0:T(8,128)(2,1)S(1)}, bf16[2,208,384]{2,1,0:T(8,128)(2,1)S(1)}, u32[]{:S(2)}, u32[]{:S(2)}) collective-permute-start(bf16[2,208,384]{2,1,0:T(8,128)(2,1)S(1)} %collective-permute-done.3.refs_2_), channel_id=1, source_target_pairs={{0,2},{1,15},{2,4},{3,1},{4,6},{5,3},{6,8},{7,5},{8,10},{9,7},{10,... | collective-permute-start | bytes 958472 | tf_op jit(solution)/shard_map/ppermute | solution.py:289
  94.4 3.2 %copy-start.13 = (bf16[2,192,384]{2,1,0:T(8,128)(2,1)}, bf16[2,192,384]{2,1,0:T(8,128)(2,1)S(1)}, u32[]{:S(2)}) copy-start(bf16[2,192,384]{2,1,0:T(8,128)(2,1)S(1)} %collective-permute-done.4.refs_3_) | copy-start | bytes 884740
  94.4 9.3 %collective-permute-start.6 = (bf16[2,192,384]{2,1,0:T(8,128)(2,1)S(1)}, bf16[2,192,384]{2,1,0:T(8,128)(2,1)S(1)}, u32[]{:S(2)}, u32[]{:S(2)}) collective-permute-start(bf16[2,192,384]{2,1,0:T(8,128)(2,1)S(1)} %collective-permute-done.4.refs_3_), channel_id=1, source_target_pairs={{0,2},{1,15},{2,4},{3,1},{4,6},{5,3},{6,8},{7,5},{8,10},{9,7},{10,... | collective-permute-start | bytes 884744 | tf_op jit(solution)/shard_map/ppermute | solution.py:289
  97.6 6.1 %copy-start.5 = (f32[192,128]{1,0:T(8,128)S(1)}, f32[192,128]{1,0:T(8,128)}, u32[]{:S(2)}) copy-start(f32[192,128]{1,0:T(8,128)} %get-tuple-element.43.valid_ref) | copy-start | bytes 294916
  103.6 22.7 %copy-start.9 = (bf16[2,208,384]{2,1,0:T(8,128)(2,1)}, bf16[2,208,384]{2,1,0:T(8,128)(2,1)S(1)}, u32[]{:S(2)}) copy-start(bf16[2,208,384]{2,1,0:T(8,128)(2,1)S(1)} %collective-permute-done.5.refs_0_) | copy-start | bytes 958468
  103.7 22.6 %copy-start.10 = (bf16[2,192,384]{2,1,0:T(8,128)(2,1)}, bf16[2,192,384]{2,1,0:T(8,128)(2,1)S(1)}, u32[]{:S(2)}) copy-start(bf16[2,192,384]{2,1,0:T(8,128)(2,1)S(1)} %collective-permute-done.6.refs_1_) | copy-start | bytes 884740
  105.4 38.7 %all-to-all-start.2 = ((bf16[64,24,128]{2,1,0:T(8,128)(2,1)}), bf16[64,24,128]{2,1,0:T(8,128)(2,1)S(1)}, u32[]{:S(2)}, u32[]{:S(2)}) async-start(bf16[64,24,128]{2,1,0:T(8,128)(2,1)} %bitcast.6), calls=%async_computation.2 | async-start | bytes 786432 | tf_op jit(solution)/shard_map/all_to_all | solution.py:283
  117.3 9.0 %collective-permute-start.7 = (bf16[1,208,384]{2,1,0:T(8,128)(2,1)S(1)}, bf16[1,208,384]{2,1,0:T(8,128)(2,1)S(1)}, u32[]{:S(2)}, u32[]{:S(2)}) collective-permute-start(bf16[1,208,384]{2,1,0:T(8,128)(2,1)S(1)} %constant_dynamic-slice_fusion.1), channel_id=1, source_target_pairs={{0,2},{1,15},{2,4},{3,1},{4,6},{5,3},{6,8},{7,5},{8,10},{9,7},{10,... | collective-permute-start | bytes 479240 | tf_op jit(solution)/shard_map/ppermute | solution.py:289
  120.1 6.2 %collective-permute-start.8 = (bf16[1,192,384]{2,1,0:T(8,128)(2,1)S(1)}, bf16[1,192,384]{2,1,0:T(8,128)(2,1)S(1)}, u32[]{:S(2)}, u32[]{:S(2)}) collective-permute-start(bf16[1,192,384]{2,1,0:T(8,128)(2,1)S(1)} %constant_dynamic-slice_fusion), channel_id=1, source_target_pairs={{0,2},{1,15},{2,4},{3,1},{4,6},{5,3},{6,8},{7,5},{8,10},{9,7},{10,... | collective-permute-start | bytes 442376 | tf_op jit(solution)/shard_map/ppermute | solution.py:289
  126.3 0.7 copy-start.15
  126.3 0.7 copy-start.14
  127.0 13.9 %copy-start.1 = (s32[512,128]{1,0:T(8,128)S(1)}, s32[512,128]{1,0:T(8,128)}, u32[]{:S(2)}) copy-start(s32[512,128]{1,0:T(8,128)} %get-tuple-element.44.pos_ref) | copy-start | bytes 786436
  127.0 13.9 %copy-start.2 = (bf16[400,768]{1,0:T(8,128)(2,1)S(1)}, bf16[400,768]{1,0:T(8,128)(2,1)}, u32[]{:S(2)}) copy-start(bf16[400,768]{1,0:T(8,128)(2,1)} %get-tuple-element.50.rows_ref) | copy-start | bytes 1843204
  127.0 13.9 %copy-start.6 = (f32[144,128]{1,0:T(8,128)S(1)}, f32[144,128]{1,0:T(8,128)}, u32[]{:S(2)}) copy-start(f32[144,128]{1,0:T(8,128)} %get-tuple-element.51.valid_ref) | copy-start | bytes 221188
  130.6 10.3 %collective-permute-start.9 = (f32[400,256]{1,0:T(8,128)}, f32[400,256]{1,0:T(8,128)S(1)}, u32[]{:S(2)}, u32[]{:S(2)}) collective-permute-start(f32[400,256]{1,0:T(8,128)} %get-tuple-element.49), channel_id=1, source_target_pairs={{0,1},{1,0},{2,3},{3,2},{4,5},{5,4},{6,7},{7,6},{8,9},{9,8},{10,11... | collective-permute-start | bytes 1228808 | tf_op jit(solution)/shard_map/ppermute | solution.py:367
  140.9 1.0 copy-start.3

commit v8 on v6

--- a/solution.py
+++ b/solution.py
@@ -196,21 +196,12 @@
             grads_ref[name] = pick(hot, jnp.concatenate([parts[0][name], parts[1][name]], 1))
 
 
-def merge_kernel(back_ref, pos_hbm, kept_hbm, dq_ref, dk_ref, dv_ref, wide_ref, pos_ref, kept_ref, sems):
-    fetches = [
-        pltpu.make_async_copy(pos_hbm, pos_ref, sems.at[0]),
-        pltpu.make_async_copy(kept_hbm, kept_ref, sems.at[1]),
-    ]
-    for fetch in fetches:
-        fetch.start()
-    back = from_octets(back_ref, wide_ref, 6)
-    fetches[0].wait()
+def merge_kernel(back_ref, pos_ref, kept_ref, dq_ref, dk_ref, dv_ref, wide_ref):
     slots = back_ref.shape[0] // OCT
     hot = one_hot(iota((pos_ref.shape[0], slots), 1) == pos_ref[:, 0:1])
-    added = [pick(hot, jnp.concatenate(back[2 * i : 2 * i + 2], 1)) for i in range(3)]
-    fetches[1].wait()
+    back = from_octets(back_ref, wide_ref, 6)
     for i, out in enumerate((dq_ref, dk_ref, dv_ref)):
-        out[...] = kept_ref[i] + added[i]
+        out[...] = kept_ref[i] + pick(hot, jnp.concatenate(back[2 * i : 2 * i + 2], 1))
 
 
 def sds(shape, dtype):
@@ -335,14 +326,8 @@
         (back, pos_col, kept_grads),
         (sds((tok, cols), BF16),) * 3,
         "merge",
-        56,
-        scratch=wide
-        + [
-            pltpu.VMEM((tok, HD), jnp.int32),
-            pltpu.VMEM((3, tok, cols), BF16),
-            pltpu.SemaphoreType.DMA((2,)),
-        ],
-        in_hbm=(1, 2),
+        12,
+        scratch=wide,
     )
 
 

time: 129 us -> 128 us (level)
  Pallas kernels: 22 us -> 20.3 us
    pallas_call x6, Pallas kernels: 13.9 us -> 11.8 us  [call(): pl.pallas_call(kernel, out_shape=outs, grid=(1,), in_specs=[pl.BlockSpec(...]
where the time goes in v8:
time: 128 us; the launch traced here: 126 us
  waiting for transfers between devices  35.4 us (28%)
  blocking collectives  28 us (22%)
  starting transfers between devices  26.6 us (21%)
  Pallas kernels  20.3 us (16%)
  between operations  14.1 us (11%)
    all_to_all x1, waiting for transfers between devices, local(): lax.all_to_all(og_moved, 'mp', split_axis=0, concat_axis=0, tiled=True, a...  28.9 us
    all_to_all x1, blocking collectives, exchange(): lax.all_to_all(shaped, 'dp', split_axis=0, concat_axis=0, tiled=True)  28 us
    all_to_all x1, starting transfers between devices, local(): lax.all_to_all(og_moved, 'mp', split_axis=0, concat_axis=0, tiled=True, a...  17.5 us
    pallas_call x6, Pallas kernels, call(): pl.pallas_call(kernel, out_shape=outs, grid=(1,), in_specs=[pl.BlockSpec(...  11.8 us
    pallas_call x1, Pallas kernels, local(): pl.pallas_call(functools.partial(local_kernel, n_dp, tok, img), out_shape...  8.49 us
    all_to_all x1, starting transfers between devices, exchange(): lax.all_to_all(shaped, 'dp', split_axis=0, concat_axis=0, tiled=True)  6.53 us
    all_gather x1, waiting for transfers between devices, local(): kept_all = lax.all_gather(after(og_kept, og_chips), 'mp', axis=0)  4.38 us
  transfers between devices with their start and end apart: 4, of which 4 were waited for; matrix products, arithmetic and copies ran while one was open for 0% of the time, Pallas kernels for 13%

profile of v8, /device:TPU:1, one launch (start us, length us, event | category | flops | bytes accessed | tf_op | source)
XLA Modules:
  0.0 125.6 jit_solution(14078330406582624585)
XLA Ops:
  7.2 2.7 %plan.1 = (s32[8,512]{1,0:T(8,128)}, bf16[8,192,384]{2,1,0:T(8,128)(2,1)}) custom-call(s32[1,512]{1,0:T(1,128)} %bitcast.12, s32[1,512]{1,0:T(1,128)} %bitcast.13, s32[1,3]{1,0:T(1,128)} %bitcast.14, bf16[512,384]{1,0:T(8,128)(2,1)} %og_ref.3), custom_call_target="tpu_custom_call" | custom-call | bytes 1593356 | tf_op jit(solution)/shard_map/plan/pallas_call | solution.py:213
  9.9 0.0 copy-start
  9.9 17.5 %all-to-all-start = ((bf16[8,192,384]{2,1,0:T(8,128)(2,1)}), bf16[8,192,384]{2,1,0:T(8,128)(2,1)}, u32[]{:S(2)}, u32[]{:S(2)}) async-start(bf16[8,192,384]{2,1,0:T(8,128)(2,1)} %get-tuple-element.12), calls=%async_computation | async-start | bytes 2359296 | tf_op jit(solution)/shard_map/all_to_all | solution.py:267
  27.4 0.0 all-gather.3.cloned.1.call-start
  27.4 3.2 %pack.1 = (bf16[1536,128]{1,0:T(8,128)(2,1)}, bf16[400,384]{1,0:T(8,128)(2,1)}, bf16[400,768]{1,0:T(8,128)(2,1)}, f32[192,128]{1,0:T(8,128)}, f32[144,128]{1,0:T(8,128)}, /*index=5*/s32[512,128]{1,0:T(8,128)}) custom-call(s32[8,512]{1,0:T(8,128)} %get-tuple-element.13.pos_ref, bf16[512,384]{1,0:T(8,128)(2,1)} %og_ref.3, bf16[512,256]{1,0:T(8,128)(2,1)} %q_ref.1, ...), custom_call_target="tpu_custom_call" | custom-call | bytes 2945024 | tf_op jit(solution)/shard_map/pack/pallas_call | solution.py:213
  30.6 28.9 %all-to-all-done.own_ref = bf16[8,192,384]{2,1,0:T(8,128)(2,1)} async-done(((bf16[8,192,384]{2,1,0:T(8,128)(2,1)}), bf16[8,192,384]{2,1,0:T(8,128)(2,1)}, u32[]{:S(2)}, u32[]{:S(2)}) %all-to-all-start) | async-done | bytes 1179680 | tf_op jit(solution)/shard_map/all_to_all | solution.py:267
  59.5 0.0 all-gather.3.cloned.1.call-update
  59.5 0.0 copy-start.3
  59.5 2.5 %collective-permute-start = (bf16[8,192,384]{2,1,0:T(8,128)(2,1)}, bf16[8,192,384]{2,1,0:T(8,128)(2,1)S(1)}, u32[]{:S(2)}, u32[]{:S(2)}) collective-permute-start(bf16[8,192,384]{2,1,0:T(8,128)(2,1)} %all-to-all-done.own_ref), channel_id=1, source_target_pairs={{0,1},{1,0},{2,3},{3,2},{4,5},{5,4},{6,7},{7,6},{8,9},{9,8},{10,11... | collective-permute-start | bytes 3538952 | tf_op jit(solution)/shard_map/ppermute | solution.py:270
  62.1 0.0 copy-done
  62.1 2.0 %own.1.acc_ref = f32[192,256]{1,0:T(8,128)S(1)} custom-call(bf16[8,192,384]{2,1,0:T(8,128)(2,1)} %all-to-all-done.own_ref, bf16[256,6144]{1,0:T(8,128)(2,1)S(1)} %copy-done), custom_call_target="tpu_custom_call" | custom-call | flops 1000000000 | bytes 4521984 | tf_op jit(solution)/shard_map/own/pallas_call | solution.py:213
  64.1 0.7 collective-permute-done.pair_ref
  64.7 0.0 copy-done.3
  64.8 0.0 copy-start.4
  64.8 1.0 moved.1
  65.8 28.0 %all_to_all.15 = bf16[64,24,128]{2,1,0:T(8,128)(2,1)S(1)} all-to-all(bf16[64,24,128]{2,1,0:T(8,128)(2,1)S(1)} %bitcast.10), channel_id=1, replica_groups=mesh['dp'=64,'mp'=16] {'dp'}, dimensions={0} | all-to-all | bytes 786432 | tf_op jit(solution)/shard_map/all_to_all | solution.py:256
  93.8 0.0 copy-done.4
  93.8 1.7 %remote.1 = bf16[1536,128]{1,0:T(8,128)(2,1)} custom-call(bf16[1536,128]{1,0:T(8,128)(2,1)S(1)} %bitcast.8, f32[192,128]{1,0:T(8,128)S(1)} %copy-done.4), custom_call_target="tpu_custom_call" | custom-call | bytes 884736 | tf_op jit(solution)/shard_map/remote/pallas_call | solution.py:213
  95.5 6.5 %all-to-all-start.2 = ((bf16[64,24,128]{2,1,0:T(8,128)(2,1)}), bf16[64,24,128]{2,1,0:T(8,128)(2,1)S(1)}, u32[]{:S(2)}, u32[]{:S(2)}) async-start(bf16[64,24,128]{2,1,0:T(8,128)(2,1)} %bitcast.5), calls=%async_computation.2 | async-start | bytes 786432 | tf_op jit(solution)/shard_map/all_to_all | solution.py:256
  102.0 4.4 %all-gather.3.cloned.1.call-done = bf16[6400,384]{1,0:T(8,128)(2,1)} async-done(((bf16[400,384]{1,0:T(8,128)(2,1)}), bf16[6400,384]{1,0:T(8,128)(2,1)}) %all-gather.3.cloned.1.call-update) | async-done | bytes 4915216 | tf_op jit(solution)/shard_map/all_gather | solution.py:285
  106.4 0.0 copy-start.2
  106.4 8.5 %kept.1.kept_ref = bf16[3,512,256]{2,1,0:T(8,128)(2,1)} custom-call(bf16[16,400,384]{2,1,0:T(8,128)(2,1)} %bitcast.11, bf16[256,6144]{1,0:T(8,128)(2,1)} %w_ref.5, bf16[400,768]{1,0:T(8,128)(2,1)} %get-tuple-element.19.rows_ref, f32[144,128]{1,0:T(8,128)} %get-tuple-element.20.valid_ref, s32[512,128]{1,0:T(8,128)} %get-tuple-element.16.pos_ref), custom_call_target="tpu_custom_call" | custom-call | flops 1258291200 | bytes 9797632 | tf_op jit(solution)/shard_map/kept/pallas_call | solution.py:311
  114.9 1.5 %all-to-all-done.2 = bf16[64,24,128]{2,1,0:T(8,128)(2,1)S(1)} async-done(((bf16[64,24,128]{2,1,0:T(8,128)(2,1)}), bf16[64,24,128]{2,1,0:T(8,128)(2,1)S(1)}, u32[]{:S(2)}, u32[]{:S(2)}) %all-to-all-start.2) | async-done | bytes 393248 | tf_op jit(solution)/shard_map/all_to_all | solution.py:256
  116.3 0.0 copy-done.2
  116.3 0.0 copy-start.1
  116.4 1.1 copy-done.1
  117.5 1.2 merge.1
Async XLA Ops:
  9.9 52.2 %copy-start = (bf16[256,6144]{1,0:T(8,128)(2,1)S(1)}, bf16[256,6144]{1,0:T(8,128)(2,1)}, u32[]{:S(2)}) copy-start(bf16[256,6144]{1,0:T(8,128)(2,1)} %w_ref.5) | copy-start | bytes 9437188
  9.9 49.6 %all-to-all-start = ((bf16[8,192,384]{2,1,0:T(8,128)(2,1)}), bf16[8,192,384]{2,1,0:T(8,128)(2,1)}, u32[]{:S(2)}, u32[]{:S(2)}) async-start(bf16[8,192,384]{2,1,0:T(8,128)(2,1)} %get-tuple-element.12), calls=%async_computation | async-start | bytes 2359296 | tf_op jit(solution)/shard_map/all_to_all | solution.py:267
  27.4 79.0 %all-gather.3.cloned.1.call-start = ((), (), s32[]{:S(2)}) async-start(), calls=%async_computation.3 | async-start | bytes 5222400 | tf_op jit(solution)/shard_map/all_gather | solution.py:285
  59.5 5.2 %copy-start.3 = (bf16[1536,128]{1,0:T(8,128)(2,1)S(1)}, bf16[1536,128]{1,0:T(8,128)(2,1)}, u32[]{:S(2)}) copy-start(bf16[1536,128]{1,0:T(8,128)(2,1)} %get-tuple-element.14.rows_hbm) | copy-start | bytes 1179652
  59.5 5.2 %collective-permute-start = (bf16[8,192,384]{2,1,0:T(8,128)(2,1)}, bf16[8,192,384]{2,1,0:T(8,128)(2,1)S(1)}, u32[]{:S(2)}, u32[]{:S(2)}) collective-permute-start(bf16[8,192,384]{2,1,0:T(8,128)(2,1)} %all-to-all-done.own_ref), channel_id=1, source_target_pairs={{0,1},{1,0},{2,3},{3,2},{4,5},{5,4},{6,7},{7,6},{8,9},{9,8},{10,11... | collective-permute-start | bytes 3538952 | tf_op jit(solution)/shard_map/ppermute | solution.py:270
  64.8 29.0 %copy-start.4 = (f32[192,128]{1,0:T(8,128)S(1)}, f32[192,128]{1,0:T(8,128)}, u32[]{:S(2)}) copy-start(f32[192,128]{1,0:T(8,128)} %get-tuple-element.15.valid_ref) | copy-start | bytes 294916
  95.5 20.9 %all-to-all-start.2 = ((bf16[64,24,128]{2,1,0:T(8,128)(2,1)}), bf16[64,24,128]{2,1,0:T(8,128)(2,1)S(1)}, u32[]{:S(2)}, u32[]{:S(2)}) async-start(bf16[64,24,128]{2,1,0:T(8,128)(2,1)} %bitcast.5), calls=%async_computation.2 | async-start | bytes 786432 | tf_op jit(solution)/shard_map/all_to_all | solution.py:256
  106.4 10.0 %copy-start.2 = (s32[512,128]{1,0:T(8,128)S(1)}, s32[512,128]{1,0:T(8,128)}, u32[]{:S(2)}) copy-start(s32[512,128]{1,0:T(8,128)} %get-tuple-element.16.pos_ref) | copy-start | bytes 786436
  116.3 1.1 copy-start.1
Sparse Core Ops, SparseCore 0:
  59.7 46.6 all-gather.2

commit v9 on v8

--- a/solution.py
+++ b/solution.py
@@ -165,14 +165,12 @@
 
 
 def local_kernel(
-    n_dp, tok, img, og_ref, w_ref, rows_ref, valid_ref, pos_ref,
-    grads_ref, acc_ref,
+    tok, img, og_ref, w_ref, rows_ref, valid_ref, grads_ref, acc_ref
 ):
     project(og_ref, w_ref, acc_ref)
 
     @pl.when(pl.program_id(0) == pl.num_programs(0) - 1)
     def _():
-        slots = n_dp * CAP
         grad = acc_ref[...].astype(BF16)
         valid = valid_ref[:, 0:1]
         count = jnp.sum(valid, axis=0, keepdims=True)
@@ -190,10 +188,15 @@
                 v = rows_ref[span, (4 + head) * HD : (5 + head) * HD]
                 pieces.append(attend(q, k, v, grad[span, lanes], mask, weight))
             parts.append([jnp.concatenate(p, 0) for p in zip(*pieces)])
-        pos = pos_ref[:, 0:1] - slots
-        hot = one_hot(iota((tok, KEPT), 1) == pos)
         for name in range(3):
-            grads_ref[name] = pick(hot, jnp.concatenate([parts[0][name], parts[1][name]], 1))
+            grads_ref[name] = jnp.concatenate([parts[0][name], parts[1][name]], 1)
+
+
+def place_kernel(first, grads_ref, pos_ref, out_ref):
+    shape = (pos_ref.shape[0], grads_ref.shape[1])
+    hot = one_hot(iota(shape, 1) == pos_ref[:, 0:1] - first)
+    for name in range(3):
+        out_ref[name] = pick(hot, grads_ref[name])
 
 
 def merge_kernel(back_ref, pos_ref, kept_ref, dq_ref, dk_ref, dv_ref, wide_ref):
@@ -305,11 +308,11 @@
         scratch=wide,
     )
     back = exchange(back_send)
-    ins = (kept_all, out_weight, rows_kept, kept_used, pos_col)
-    outs = sds((3, tok, cols), BF16)
+    ins = (kept_all, out_weight, rows_kept, kept_used)
+    outs = sds((3, KEPT, cols), BF16)
     per_step = 4 if n_mp % 4 == 0 else 1
     kept_grads = pl.pallas_call(
-        functools.partial(local_kernel, n_dp, tok, img),
+        functools.partial(local_kernel, tok, img),
         out_shape=outs,
         grid=(n_mp // per_step,),
         in_specs=[
@@ -321,6 +324,13 @@
         scratch_shapes=[pltpu.VMEM((KEPT, cols), F32)],
         **options(ins, (outs,), "kept", 56, 2 * KEPT * n_mp * feat * cols),
     )(*ins)
+    kept_grads = call(
+        functools.partial(place_kernel, slots),
+        (kept_grads, pos_col),
+        sds((3, tok, cols), BF16),
+        "place",
+        12,
+    )
     return call(
         merge_kernel,
         (back, pos_col, kept_grads),

time: 128 us -> 127 us (level)
    pallas_call x6 -> x7, Pallas kernels: 11.8 us -> 12.4 us  [call(): pl.pallas_call(kernel, out_shape=outs, grid=(1,), in_specs=[pl.BlockSpec(...]
where the time goes in v9:
time: 127 us; the launch traced here: 124 us
  waiting for transfers between devices  34.7 us (27%)
  blocking collectives  28 us (22%)
  starting transfers between devices  26.6 us (21%)
  Pallas kernels  19.9 us (16%)
  between operations  14.1 us (11%)
    all_to_all x1, waiting for transfers between devices, local(): lax.all_to_all(og_moved, 'mp', split_axis=0, concat_axis=0, tiled=True, a...  28.9 us
    all_to_all x1, blocking collectives, exchange(): lax.all_to_all(shaped, 'dp', split_axis=0, concat_axis=0, tiled=True)  28 us
    all_to_all x1, starting transfers between devices, local(): lax.all_to_all(og_moved, 'mp', split_axis=0, concat_axis=0, tiled=True, a...  17.5 us
    pallas_call x7, Pallas kernels, call(): pl.pallas_call(kernel, out_shape=outs, grid=(1,), in_specs=[pl.BlockSpec(...  12.4 us
    pallas_call x1, Pallas kernels, local(): pl.pallas_call(functools.partial(local_kernel, tok, img), out_shape=outs,...  7.49 us
    all_to_all x1, starting transfers between devices, exchange(): lax.all_to_all(shaped, 'dp', split_axis=0, concat_axis=0, tiled=True)  6.53 us
    all_gather x1, waiting for transfers between devices, local(): kept_all = lax.all_gather(after(og_kept, og_chips), 'mp', axis=0)  4.38 us
  transfers between devices with their start and end apart: 4, of which 4 were waited for; matrix products, arithmetic and copies ran while one was open for 0% of the time, Pallas kernels for 13%

profile of v9, /device:TPU:1, one launch (start us, length us, event | category | flops | bytes accessed | tf_op | source)
XLA Modules:
  0.0 124.4 jit_solution(17592552557731977206)
XLA Ops:
  7.2 2.7 %plan.1 = (s32[8,512]{1,0:T(8,128)}, bf16[8,192,384]{2,1,0:T(8,128)(2,1)}) custom-call(s32[1,512]{1,0:T(1,128)} %bitcast.12, s32[1,512]{1,0:T(1,128)} %bitcast.13, s32[1,3]{1,0:T(1,128)} %bitcast.14, bf16[512,384]{1,0:T(8,128)(2,1)} %og_ref.3), custom_call_target="tpu_custom_call" | custom-call | bytes 1593356 | tf_op jit(solution)/shard_map/plan/pallas_call | solution.py:216
  9.9 0.0 copy-start
  9.9 17.5 %all-to-all-start = ((bf16[8,192,384]{2,1,0:T(8,128)(2,1)}), bf16[8,192,384]{2,1,0:T(8,128)(2,1)}, u32[]{:S(2)}, u32[]{:S(2)}) async-start(bf16[8,192,384]{2,1,0:T(8,128)(2,1)} %get-tuple-element.12), calls=%async_computation | async-start | bytes 2359296 | tf_op jit(solution)/shard_map/all_to_all | solution.py:270
  27.4 0.0 all-gather.3.cloned.1.call-start
  27.4 3.2 %pack.1 = (bf16[1536,128]{1,0:T(8,128)(2,1)}, bf16[400,384]{1,0:T(8,128)(2,1)}, bf16[400,768]{1,0:T(8,128)(2,1)}, f32[192,128]{1,0:T(8,128)}, f32[144,128]{1,0:T(8,128)}, /*index=5*/s32[512,128]{1,0:T(8,128)}) custom-call(s32[8,512]{1,0:T(8,128)} %get-tuple-element.13.pos_ref, bf16[512,384]{1,0:T(8,128)(2,1)} %og_ref.3, bf16[512,256]{1,0:T(8,128)(2,1)} %q_ref.1, ...), custom_call_target="tpu_custom_call" | custom-call | bytes 2945024 | tf_op jit(solution)/shard_map/pack/pallas_call | solution.py:216
  30.6 28.9 %all-to-all-done.own_ref = bf16[8,192,384]{2,1,0:T(8,128)(2,1)} async-done(((bf16[8,192,384]{2,1,0:T(8,128)(2,1)}), bf16[8,192,384]{2,1,0:T(8,128)(2,1)}, u32[]{:S(2)}, u32[]{:S(2)}) %all-to-all-start) | async-done | bytes 1179680 | tf_op jit(solution)/shard_map/all_to_all | solution.py:270
  59.5 0.0 all-gather.3.cloned.1.call-update
  59.5 0.0 copy-start.3
  59.5 2.5 %collective-permute-start = (bf16[8,192,384]{2,1,0:T(8,128)(2,1)}, bf16[8,192,384]{2,1,0:T(8,128)(2,1)S(1)}, u32[]{:S(2)}, u32[]{:S(2)}) collective-permute-start(bf16[8,192,384]{2,1,0:T(8,128)(2,1)} %all-to-all-done.own_ref), channel_id=1, source_target_pairs={{0,1},{1,0},{2,3},{3,2},{4,5},{5,4},{6,7},{7,6},{8,9},{9,8},{10,11... | collective-permute-start | bytes 3538952 | tf_op jit(solution)/shard_map/ppermute | solution.py:273
  62.1 0.0 copy-done
  62.1 2.0 %own.1.acc_ref = f32[192,256]{1,0:T(8,128)S(1)} custom-call(bf16[8,192,384]{2,1,0:T(8,128)(2,1)} %all-to-all-done.own_ref, bf16[256,6144]{1,0:T(8,128)(2,1)S(1)} %copy-done), custom_call_target="tpu_custom_call" | custom-call | flops 1000000000 | bytes 4521984 | tf_op jit(solution)/shard_map/own/pallas_call | solution.py:216
  64.1 0.7 collective-permute-done.pair_ref
  64.7 0.0 copy-done.3
  64.8 0.0 copy-start.4
  64.8 1.0 moved.1
  65.8 28.0 %all_to_all.15 = bf16[64,24,128]{2,1,0:T(8,128)(2,1)S(1)} all-to-all(bf16[64,24,128]{2,1,0:T(8,128)(2,1)S(1)} %bitcast.10), channel_id=1, replica_groups=mesh['dp'=64,'mp'=16] {'dp'}, dimensions={0} | all-to-all | bytes 786432 | tf_op jit(solution)/shard_map/all_to_all | solution.py:259
  93.8 0.0 copy-done.4
  93.8 1.7 %remote.1 = bf16[1536,128]{1,0:T(8,128)(2,1)} custom-call(bf16[1536,128]{1,0:T(8,128)(2,1)S(1)} %bitcast.8, f32[192,128]{1,0:T(8,128)S(1)} %copy-done.4), custom_call_target="tpu_custom_call" | custom-call | bytes 884736 | tf_op jit(solution)/shard_map/remote/pallas_call | solution.py:216
  95.5 6.5 %all-to-all-start.2 = ((bf16[64,24,128]{2,1,0:T(8,128)(2,1)}), bf16[64,24,128]{2,1,0:T(8,128)(2,1)S(1)}, u32[]{:S(2)}, u32[]{:S(2)}) async-start(bf16[64,24,128]{2,1,0:T(8,128)(2,1)} %bitcast.5), calls=%async_computation.2 | async-start | bytes 786432 | tf_op jit(solution)/shard_map/all_to_all | solution.py:259
  102.0 4.4 %all-gather.3.cloned.1.call-done = bf16[6400,384]{1,0:T(8,128)(2,1)} async-done(((bf16[400,384]{1,0:T(8,128)(2,1)}), bf16[6400,384]{1,0:T(8,128)(2,1)}) %all-gather.3.cloned.1.call-update) | async-done | bytes 4915216 | tf_op jit(solution)/shard_map/all_gather | solution.py:288
  106.4 0.0 copy-start.2
  106.4 7.5 %kept.1.grads_ref = bf16[3,400,256]{2,1,0:T(8,128)(2,1)} custom-call(bf16[16,400,384]{2,1,0:T(8,128)(2,1)} %bitcast.11, bf16[256,6144]{1,0:T(8,128)(2,1)} %w_ref.5, bf16[400,768]{1,0:T(8,128)(2,1)} %get-tuple-element.19.rows_ref, f32[144,128]{1,0:T(8,128)} %get-tuple-element.20.valid_ref), custom_call_target="tpu_custom_call" | custom-call | flops 1258291200 | bytes 9363456 | tf_op jit(solution)/shard_map/kept/pallas_call | solution.py:314
  113.9 0.0 copy-done.2
  113.9 0.0 copy-start.1
  113.9 1.1 copy-done.1
  114.9 0.6 place.1.kept_ref
  115.6 0.8 all-to-all-done.2
  116.3 1.2 merge.1
Async XLA Ops:
  9.9 52.2 %copy-start = (bf16[256,6144]{1,0:T(8,128)(2,1)S(1)}, bf16[256,6144]{1,0:T(8,128)(2,1)}, u32[]{:S(2)}) copy-start(bf16[256,6144]{1,0:T(8,128)(2,1)} %w_ref.5) | copy-start | bytes 9437188
  9.9 49.6 %all-to-all-start = ((bf16[8,192,384]{2,1,0:T(8,128)(2,1)}), bf16[8,192,384]{2,1,0:T(8,128)(2,1)}, u32[]{:S(2)}, u32[]{:S(2)}) async-start(bf16[8,192,384]{2,1,0:T(8,128)(2,1)} %get-tuple-element.12), calls=%async_computation | async-start | bytes 2359296 | tf_op jit(solution)/shard_map/all_to_all | solution.py:270
  27.4 79.0 %all-gather.3.cloned.1.call-start = ((), (), s32[]{:S(2)}) async-start(), calls=%async_computation.3 | async-start | bytes 5222400 | tf_op jit(solution)/shard_map/all_gather | solution.py:288
  59.5 5.2 %copy-start.3 = (bf16[1536,128]{1,0:T(8,128)(2,1)S(1)}, bf16[1536,128]{1,0:T(8,128)(2,1)}, u32[]{:S(2)}) copy-start(bf16[1536,128]{1,0:T(8,128)(2,1)} %get-tuple-element.14.rows_hbm) | copy-start | bytes 1179652
  59.5 5.2 %collective-permute-start = (bf16[8,192,384]{2,1,0:T(8,128)(2,1)}, bf16[8,192,384]{2,1,0:T(8,128)(2,1)S(1)}, u32[]{:S(2)}, u32[]{:S(2)}) collective-permute-start(bf16[8,192,384]{2,1,0:T(8,128)(2,1)} %all-to-all-done.own_ref), channel_id=1, source_target_pairs={{0,1},{1,0},{2,3},{3,2},{4,5},{5,4},{6,7},{7,6},{8,9},{9,8},{10,11... | collective-permute-start | bytes 3538952 | tf_op jit(solution)/shard_map/ppermute | solution.py:273
  64.8 29.0 %copy-start.4 = (f32[192,128]{1,0:T(8,128)S(1)}, f32[192,128]{1,0:T(8,128)}, u32[]{:S(2)}) copy-start(f32[192,128]{1,0:T(8,128)} %get-tuple-element.15.valid_ref) | copy-start | bytes 294916
  95.5 20.9 %all-to-all-start.2 = ((bf16[64,24,128]{2,1,0:T(8,128)(2,1)}), bf16[64,24,128]{2,1,0:T(8,128)(2,1)S(1)}, u32[]{:S(2)}, u32[]{:S(2)}) async-start(bf16[64,24,128]{2,1,0:T(8,128)(2,1)} %bitcast.5), calls=%async_computation.2 | async-start | bytes 786432 | tf_op jit(solution)/shard_map/all_to_all | solution.py:259
  106.4 7.5 %copy-start.2 = (s32[512,128]{1,0:T(8,128)S(1)}, s32[512,128]{1,0:T(8,128)}, u32[]{:S(2)}) copy-start(s32[512,128]{1,0:T(8,128)} %get-tuple-element.16.pos_ref) | copy-start | bytes 786436
  113.9 1.1 copy-start.1
Sparse Core Ops, SparseCore 0:
  59.7 46.6 all-gather.2

commit v10 on v9

--- a/solution.py
+++ b/solution.py
@@ -117,10 +117,12 @@
 def parity_dot(block_ref, w_ref, parity):
     chips, rows, feat = block_ref.shape
     acc = jnp.zeros((rows, w_ref.shape[0]), F32)
-    for chip in range(chips):
-        start = pl.multiple_of((2 * chip + parity) * feat, HD)
-        weight = w_ref[:, pl.ds(start, feat)]
-        acc = acc + lax.dot_general(block_ref[chip], weight, NT, preferred_element_type=F32)
+    for first in range(0, chips, 2):
+        pair = range(first, min(first + 2, chips))
+        starts = [pl.multiple_of((2 * chip + parity) * feat, HD) for chip in pair]
+        weight = jnp.concatenate([w_ref[:, pl.ds(start, feat)] for start in starts], 1)
+        features = jnp.concatenate([block_ref[chip] for chip in pair], 1)
+        acc = acc + lax.dot_general(features, weight, NT, preferred_element_type=F32)
     return acc
 
 

time: 127 us -> 127 us (level)
  no operation moved by 1% of the time
where the time goes in v10:
time: 127 us; the launch traced here: 124 us
  waiting for transfers between devices  34.7 us (27%)
  blocking collectives  28 us (22%)
  starting transfers between devices  26.6 us (21%)
  Pallas kernels  19.9 us (16%)
  between operations  14.1 us (11%)
    all_to_all x1, waiting for transfers between devices, local(): lax.all_to_all(og_moved, 'mp', split_axis=0, concat_axis=0, tiled=True, a...  28.9 us
    all_to_all x1, blocking collectives, exchange(): lax.all_to_all(shaped, 'dp', split_axis=0, concat_axis=0, tiled=True)  28 us
    all_to_all x1, starting transfers between devices, local(): lax.all_to_all(og_moved, 'mp', split_axis=0, concat_axis=0, tiled=True, a...  17.5 us
    pallas_call x7, Pallas kernels, call(): pl.pallas_call(kernel, out_shape=outs, grid=(1,), in_specs=[pl.BlockSpec(...  12.4 us
    pallas_call x1, Pallas kernels, local(): pl.pallas_call(functools.partial(local_kernel, tok, img), out_shape=outs,...  7.49 us
    all_to_all x1, starting transfers between devices, exchange(): lax.all_to_all(shaped, 'dp', split_axis=0, concat_axis=0, tiled=True)  6.53 us
    all_gather x1, waiting for transfers between devices, local(): kept_all = lax.all_gather(after(og_kept, og_chips), 'mp', axis=0)  4.37 us
  transfers between devices with their start and end apart: 4, of which 4 were waited for; matrix products, arithmetic and copies ran while one was open for 0% of the time, Pallas kernels for 13%

profile of v10, /device:TPU:1, one launch (start us, length us, event | category | flops | bytes accessed | tf_op | source)
XLA Modules:
  0.0 124.4 jit_solution(7063049265694394485)
XLA Ops:
  7.2 2.7 %plan.1 = (s32[8,512]{1,0:T(8,128)}, bf16[8,192,384]{2,1,0:T(8,128)(2,1)}) custom-call(s32[1,512]{1,0:T(1,128)} %bitcast.12, s32[1,512]{1,0:T(1,128)} %bitcast.13, s32[1,3]{1,0:T(1,128)} %bitcast.14, bf16[512,384]{1,0:T(8,128)(2,1)} %og_ref.3), custom_call_target="tpu_custom_call" | custom-call | bytes 1593356 | tf_op jit(solution)/shard_map/plan/pallas_call | solution.py:218
  9.9 0.0 copy-start
  9.9 17.5 %all-to-all-start = ((bf16[8,192,384]{2,1,0:T(8,128)(2,1)}), bf16[8,192,384]{2,1,0:T(8,128)(2,1)}, u32[]{:S(2)}, u32[]{:S(2)}) async-start(bf16[8,192,384]{2,1,0:T(8,128)(2,1)} %get-tuple-element.12), calls=%async_computation | async-start | bytes 2359296 | tf_op jit(solution)/shard_map/all_to_all | solution.py:272
  27.4 0.0 all-gather.3.cloned.1.call-start
  27.4 3.2 %pack.1 = (bf16[1536,128]{1,0:T(8,128)(2,1)}, bf16[400,384]{1,0:T(8,128)(2,1)}, bf16[400,768]{1,0:T(8,128)(2,1)}, f32[192,128]{1,0:T(8,128)}, f32[144,128]{1,0:T(8,128)}, /*index=5*/s32[512,128]{1,0:T(8,128)}) custom-call(s32[8,512]{1,0:T(8,128)} %get-tuple-element.13.pos_ref, bf16[512,384]{1,0:T(8,128)(2,1)} %og_ref.3, bf16[512,256]{1,0:T(8,128)(2,1)} %q_ref.1, ...), custom_call_target="tpu_custom_call" | custom-call | bytes 2945024 | tf_op jit(solution)/shard_map/pack/pallas_call | solution.py:218
  30.6 28.9 %all-to-all-done.own_ref = bf16[8,192,384]{2,1,0:T(8,128)(2,1)} async-done(((bf16[8,192,384]{2,1,0:T(8,128)(2,1)}), bf16[8,192,384]{2,1,0:T(8,128)(2,1)}, u32[]{:S(2)}, u32[]{:S(2)}) %all-to-all-start) | async-done | bytes 1179680 | tf_op jit(solution)/shard_map/all_to_all | solution.py:272
  59.5 0.0 all-gather.3.cloned.1.call-update
  59.5 0.0 copy-start.3
  59.5 2.5 %collective-permute-start = (bf16[8,192,384]{2,1,0:T(8,128)(2,1)}, bf16[8,192,384]{2,1,0:T(8,128)(2,1)S(1)}, u32[]{:S(2)}, u32[]{:S(2)}) collective-permute-start(bf16[8,192,384]{2,1,0:T(8,128)(2,1)} %all-to-all-done.own_ref), channel_id=1, source_target_pairs={{0,1},{1,0},{2,3},{3,2},{4,5},{5,4},{6,7},{7,6},{8,9},{9,8},{10,11... | collective-permute-start | bytes 3538952 | tf_op jit(solution)/shard_map/ppermute | solution.py:275
  62.1 0.0 copy-done
  62.1 2.0 %own.1.acc_ref = f32[192,256]{1,0:T(8,128)S(1)} custom-call(bf16[8,192,384]{2,1,0:T(8,128)(2,1)} %all-to-all-done.own_ref, bf16[256,6144]{1,0:T(8,128)(2,1)S(1)} %copy-done), custom_call_target="tpu_custom_call" | custom-call | flops 1000000000 | bytes 4521984 | tf_op jit(solution)/shard_map/own/pallas_call | solution.py:218
  64.1 0.7 collective-permute-done.pair_ref
  64.7 0.0 copy-done.3
  64.8 0.0 copy-start.4
  64.8 1.0 moved.1
  65.8 28.0 %all_to_all.15 = bf16[64,24,128]{2,1,0:T(8,128)(2,1)S(1)} all-to-all(bf16[64,24,128]{2,1,0:T(8,128)(2,1)S(1)} %bitcast.10), channel_id=1, replica_groups=mesh['dp'=64,'mp'=16] {'dp'}, dimensions={0} | all-to-all | bytes 786432 | tf_op jit(solution)/shard_map/all_to_all | solution.py:261
  93.8 0.0 copy-done.4
  93.8 1.7 %remote.1 = bf16[1536,128]{1,0:T(8,128)(2,1)} custom-call(bf16[1536,128]{1,0:T(8,128)(2,1)S(1)} %bitcast.8, f32[192,128]{1,0:T(8,128)S(1)} %copy-done.4), custom_call_target="tpu_custom_call" | custom-call | bytes 884736 | tf_op jit(solution)/shard_map/remote/pallas_call | solution.py:218
  95.5 6.5 %all-to-all-start.2 = ((bf16[64,24,128]{2,1,0:T(8,128)(2,1)}), bf16[64,24,128]{2,1,0:T(8,128)(2,1)S(1)}, u32[]{:S(2)}, u32[]{:S(2)}) async-start(bf16[64,24,128]{2,1,0:T(8,128)(2,1)} %bitcast.5), calls=%async_computation.2 | async-start | bytes 786432 | tf_op jit(solution)/shard_map/all_to_all | solution.py:261
  102.0 4.4 %all-gather.3.cloned.1.call-done = bf16[6400,384]{1,0:T(8,128)(2,1)} async-done(((bf16[400,384]{1,0:T(8,128)(2,1)}), bf16[6400,384]{1,0:T(8,128)(2,1)}) %all-gather.3.cloned.1.call-update) | async-done | bytes 4915216 | tf_op jit(solution)/shard_map/all_gather | solution.py:290
  106.4 0.0 copy-start.2
  106.4 7.5 %kept.1.grads_ref = bf16[3,400,256]{2,1,0:T(8,128)(2,1)} custom-call(bf16[16,400,384]{2,1,0:T(8,128)(2,1)} %bitcast.11, bf16[256,6144]{1,0:T(8,128)(2,1)} %w_ref.5, bf16[400,768]{1,0:T(8,128)(2,1)} %get-tuple-element.19.rows_ref, f32[144,128]{1,0:T(8,128)} %get-tuple-element.20.valid_ref), custom_call_target="tpu_custom_call" | custom-call | flops 1258291200 | bytes 9363456 | tf_op jit(solution)/shard_map/kept/pallas_call | solution.py:316
  113.9 0.0 copy-done.2
  113.9 0.0 copy-start.1
  113.9 1.1 copy-done.1
  114.9 0.6 place.1.kept_ref
  115.5 0.8 all-to-all-done.2
  116.3 1.2 merge.1
Async XLA Ops:
  9.9 52.2 %copy-start = (bf16[256,6144]{1,0:T(8,128)(2,1)S(1)}, bf16[256,6144]{1,0:T(8,128)(2,1)}, u32[]{:S(2)}) copy-start(bf16[256,6144]{1,0:T(8,128)(2,1)} %w_ref.5) | copy-start | bytes 9437188
  9.9 49.6 %all-to-all-start = ((bf16[8,192,384]{2,1,0:T(8,128)(2,1)}), bf16[8,192,384]{2,1,0:T(8,128)(2,1)}, u32[]{:S(2)}, u32[]{:S(2)}) async-start(bf16[8,192,384]{2,1,0:T(8,128)(2,1)} %get-tuple-element.12), calls=%async_computation | async-start | bytes 2359296 | tf_op jit(solution)/shard_map/all_to_all | solution.py:272
  27.4 79.0 %all-gather.3.cloned.1.call-start = ((), (), s32[]{:S(2)}) async-start(), calls=%async_computation.3 | async-start | bytes 5222400 | tf_op jit(solution)/shard_map/all_gather | solution.py:290
  59.5 5.2 %copy-start.3 = (bf16[1536,128]{1,0:T(8,128)(2,1)S(1)}, bf16[1536,128]{1,0:T(8,128)(2,1)}, u32[]{:S(2)}) copy-start(bf16[1536,128]{1,0:T(8,128)(2,1)} %get-tuple-element.14.rows_hbm) | copy-start | bytes 1179652
  59.5 5.2 %collective-permute-start = (bf16[8,192,384]{2,1,0:T(8,128)(2,1)}, bf16[8,192,384]{2,1,0:T(8,128)(2,1)S(1)}, u32[]{:S(2)}, u32[]{:S(2)}) collective-permute-start(bf16[8,192,384]{2,1,0:T(8,128)(2,1)} %all-to-all-done.own_ref), channel_id=1, source_target_pairs={{0,1},{1,0},{2,3},{3,2},{4,5},{5,4},{6,7},{7,6},{8,9},{9,8},{10,11... | collective-permute-start | bytes 3538952 | tf_op jit(solution)/shard_map/ppermute | solution.py:275
  64.8 29.0 %copy-start.4 = (f32[192,128]{1,0:T(8,128)S(1)}, f32[192,128]{1,0:T(8,128)}, u32[]{:S(2)}) copy-start(f32[192,128]{1,0:T(8,128)} %get-tuple-element.15.valid_ref) | copy-start | bytes 294916
  95.5 20.9 %all-to-all-start.2 = ((bf16[64,24,128]{2,1,0:T(8,128)(2,1)}), bf16[64,24,128]{2,1,0:T(8,128)(2,1)S(1)}, u32[]{:S(2)}, u32[]{:S(2)}) async-start(bf16[64,24,128]{2,1,0:T(8,128)(2,1)} %bitcast.5), calls=%async_computation.2 | async-start | bytes 786432 | tf_op jit(solution)/shard_map/all_to_all | solution.py:261
  106.4 7.5 %copy-start.2 = (s32[512,128]{1,0:T(8,128)S(1)}, s32[512,128]{1,0:T(8,128)}, u32[]{:S(2)}) copy-start(s32[512,128]{1,0:T(8,128)} %get-tuple-element.16.pos_ref) | copy-start | bytes 786436
  113.9 1.1 copy-start.1
Sparse Core Ops, SparseCore 0:
  59.7 46.6 all-gather.2
